TPU v7x, 32 devices: a whole 2x2x4 slice. The times are simulated.
32 devices in a mesh: dp: 4 (over z), pack: 8 (over y, x, core).
Axes of the slice: x: 2, y: 2, z: 4, core: 2. Of those that a mesh axis runs over, the one named last changes fastest.
Arguments:
- enc_keys: bfloat16 [8192, 4096], P(('dp', 'pack')), may hold values from -4 to 4
- enc_values: bfloat16 [8192, 4096], P(('dp', 'pack')), may hold values from -6 to 6
- dec_queries: bfloat16 [4096, 4096], P(('dp', 'pack')), may hold values from -4 to 4
- cotangent: bfloat16 [4096, 4096], P(('dp', 'pack')), may hold values from -6 to 6
- input_lengths: int32 [4, 16], P('dp'), may hold values from 16 to 240, as said below
- target_lengths: int32 [4, 16], P('dp'), may hold values from 8 to 120, as said below
- enc_pack: int32 [4, 16], P('dp'), may hold values from 0 to 7, as said below
- dec_pack: int32 [4, 16], P('dp'), may hold values from 0 to 7, as said below
- task_group: int32 [4, 16, 1], P('dp'), may hold values from 0 to 15
- dro_weights: int32 [16], replicated, may hold values from 1 to 8
Outputs:
- queries_gradient: bfloat16 [4096, 4096], P(('dp', 'pack'))
- keys_gradient: bfloat16 [8192, 4096], P(('dp', 'pack'))
- values_gradient: bfloat16 [8192, 4096], P(('dp', 'pack'))
- group_loss: float32 [16], replicated
Inputs may be any that keep to these rules, and one draw needn't show every extreme that they name: `input_lengths`: within one data group, the input lengths of the examples of one encoder pack add up to exactly 256; every length is a multiple of 16. `target_lengths`: within one data group, the target lengths of the examples of one decoder pack add up to exactly 128; every length is a multiple of 8. `enc_pack`: within one data group, every encoder pack holds exactly 2 examples. `dec_pack`: within one data group, every decoder pack holds exactly 2 examples.
All inputs are finite; a program needn't handle non-finite values.
Results may differ from a plain program's by a relative error of at most 0.012.
The roundings to bfloat16 on the way count: a program that leaves them out, or rounds other values in their place, can miss the bound.
Values may be sent and summed in bfloat16 or wider, within the bound.
No kernel may reach another device: no remote copies, remote signals or barrier semaphores. Data moves between devices by JAX's collectives and lax.ppermute only.
A program may use at most 128 MiB of HBM per device.

v0:
```python
import jax
import jax.numpy as jnp
from jax import lax
from jax.sharding import PartitionSpec as P

HEAD_DIM = 64
EX_DEV = 2
GROUPS = 16


def owner_value(member, values):
    return jnp.sum(jnp.where(member, values[:, None], 0), axis=0)


def pack_tables(lengths, pack_index, per_pack, slot_total, pack_total):
    ordinal = jnp.arange(lengths.shape[0], dtype=jnp.int32)
    same_pack = pack_index[:, None] == pack_index[None, :]
    earlier = ordinal[None, :] < ordinal[:, None]
    offsets = jnp.sum(jnp.where(same_pack & earlier, lengths[None, :], 0), axis=1)
    places = jnp.arange(slot_total, dtype=jnp.int32)
    inside = places[None, :] < lengths[:, None]
    starts = pack_index * per_pack + offsets
    tokens = jnp.arange(pack_total * per_pack, dtype=jnp.int32)
    token_pack = tokens // per_pack
    token_place = tokens % per_pack
    member = (
        (pack_index[:, None] == token_pack[None, :])
        & (offsets[:, None] <= token_place[None, :])
        & (token_place[None, :] < (offsets + lengths)[:, None])
    )
    return (starts, inside, member)


def padded_table(table, extra):
    return jnp.concatenate([table, jnp.zeros((extra, table.shape[1]), table.dtype)], axis=0)


def take_rows(table, starts, slot_total):
    return jnp.stack(
        [lax.dynamic_slice_in_dim(table, starts[item], slot_total, 0) for item in range(EX_DEV)],
        axis=0,
    )


def put_rows(buffer, block, starts, inside):
    slot_total = block.shape[1]
    for item in range(EX_DEV):
        current = lax.dynamic_slice_in_dim(buffer, starts[item], slot_total, 0)
        merged = jnp.where(inside[item][:, None], block[item], current)
        buffer = lax.dynamic_update_slice_in_dim(buffer, merged, starts[item], 0)
    return buffer


def split_heads(block):
    return block.reshape(block.shape[0], block.shape[1], block.shape[2] // HEAD_DIM, HEAD_DIM)


def merge_heads(block):
    return block.reshape(block.shape[0], block.shape[1], -1)


def probabilities(query_block, key_block, key_inside):
    scores = jnp.einsum(
        "eqhd,ekhd->ehqk",
        split_heads(query_block),
        split_heads(key_block),
        preferred_element_type=jnp.float32,
    )
    scores = jnp.where(key_inside[:, None, None, :], scores, -1e30)
    highest = jnp.max(scores, axis=-1, keepdims=True)
    powers = jnp.exp(scores - highest)
    return powers / jnp.sum(powers, axis=-1, keepdims=True)


def local(
    enc_keys,
    enc_values,
    dec_queries,
    cotangent,
    input_lengths,
    target_lengths,
    enc_pack,
    dec_pack,
    task_group,
    dro_weights,
):
    pack_total = lax.axis_size("pack")
    own_pack = lax.axis_index("pack")
    encoder_rows = enc_keys.shape[0]
    decoder_rows = dec_queries.shape[0]
    encoder_slot = 2 * encoder_rows // EX_DEV - 16
    decoder_slot = 2 * decoder_rows // EX_DEV - 8
    encoder_lengths = input_lengths[0]
    decoder_lengths = target_lengths[0]
    encoder_packs = enc_pack[0]
    decoder_packs = dec_pack[0]
    task_row = task_group[0, :, 0]
    group_index = jnp.arange(GROUPS, dtype=jnp.int32)
    group_match = task_row[:, None] == group_index[None, :]
    key_starts, key_inside, key_member = pack_tables(
        encoder_lengths, encoder_packs, encoder_rows, encoder_slot, pack_total
    )
    query_starts, query_inside, query_member = pack_tables(
        decoder_lengths, decoder_packs, decoder_rows, decoder_slot, pack_total
    )
    token_group = owner_value(query_member, task_row)
    group_counts = jnp.sum(jnp.where(group_match, decoder_lengths[:, None], 0), axis=0).astype(
        jnp.float32
    )
    counts = lax.psum(group_counts, "dp")
    key_heads, value_heads = (
        lax.all_to_all(enc_keys, "pack", split_axis=1, concat_axis=0, tiled=True),
        lax.all_to_all(enc_values, "pack", split_axis=1, concat_axis=0, tiled=True),
    )
    query_heads = lax.all_to_all(dec_queries, "pack", split_axis=1, concat_axis=0, tiled=True)
    head_width = key_heads.shape[1]
    query_group_rows = query_heads.shape[0]
    key_group_rows = key_heads.shape[0]
    key_table = padded_table(key_heads, encoder_slot)
    query_table = padded_table(query_heads, decoder_slot)
    query_start_blocks = query_starts.reshape(-1, EX_DEV)
    key_start_blocks = key_starts.reshape(-1, EX_DEV)
    key_inside_blocks = key_inside.reshape(-1, EX_DEV, encoder_slot)
    query_inside_blocks = query_inside.reshape(-1, EX_DEV, decoder_slot)

    def forward_block(entries):
        starts_query, starts_key, inside_key = entries
        return probabilities(
            take_rows(query_table, starts_query, decoder_slot),
            take_rows(key_table, starts_key, encoder_slot),
            inside_key,
        ).astype(jnp.bfloat16)

    attention_store = lax.map(
        forward_block, (query_start_blocks, key_start_blocks, key_inside_blocks)
    )
    value_table = padded_table(value_heads, encoder_slot)

    def output_step(buffer, entries):
        attention_low, starts_key, starts_query, inside_query = entries
        value_block = take_rows(value_table, starts_key, encoder_slot)
        attended = jnp.einsum(
            "ehqk,ekhd->eqhd",
            attention_low,
            split_heads(value_block),
            preferred_element_type=jnp.float32,
        )
        block = merge_heads(attended.astype(jnp.bfloat16))
        return (put_rows(buffer, block, starts_query, inside_query), block)

    attended_start = jnp.zeros((query_group_rows + decoder_slot, head_width), jnp.bfloat16)
    attended_buffer, attended_store = lax.scan(
        output_step,
        attended_start,
        (attention_store, key_start_blocks, query_start_blocks, query_inside_blocks),
    )
    attended_heads = attended_buffer[:query_group_rows]
    total_tokens = decoder_rows * pack_total * lax.axis_size("dp")
    attended_tokens = lax.all_to_all(
        attended_heads, "pack", split_axis=0, concat_axis=1, tiled=True
    )
    token_loss = jnp.sum(
        attended_tokens.astype(jnp.float32) * cotangent.astype(jnp.float32), axis=1
    )
    loss_group = lax.dynamic_slice_in_dim(token_group, own_pack * decoder_rows, decoder_rows)
    loss_part = jnp.sum(
        jnp.where(loss_group[None, :] == group_index[:, None], token_loss[None, :], 0.0), axis=1
    )
    loss_sum = lax.psum(loss_part, ("dp", "pack"))
    group_loss = loss_sum / counts
    weights = dro_weights.astype(jnp.float32)
    scales = weights / jnp.sum(weights) * (total_tokens / counts)
    example_scale = jnp.sum(jnp.where(group_match, scales[None, :], 0.0), axis=1)
    token_scale = owner_value(query_member, example_scale)
    own_scale = lax.dynamic_slice_in_dim(token_scale, own_pack * decoder_rows, decoder_rows)
    upstream = (cotangent.astype(jnp.float32) * own_scale[:, None]).astype(jnp.bfloat16)
    upstream_heads = lax.all_to_all(upstream, "pack", split_axis=1, concat_axis=0, tiled=True)
    upstream_table = padded_table(upstream_heads, decoder_slot)

    def backward_step(buffers, entries):
        query_buffer, key_buffer, value_buffer = buffers
        starts_query, starts_key, inside_key, inside_query, attention_low, attended = entries
        query_block = take_rows(query_table, starts_query, decoder_slot)
        key_block = take_rows(key_table, starts_key, encoder_slot)
        value_split = split_heads(take_rows(value_table, starts_key, encoder_slot))
        gradient = jnp.where(
            inside_query[:, :, None],
            take_rows(upstream_table, starts_query, decoder_slot),
            jnp.zeros((), jnp.bfloat16),
        )
        gradient_split = split_heads(gradient)
        attention = probabilities(query_block, key_block, inside_key)
        value_gradient = jnp.einsum(
            "ehqk,eqhd->ekhd", attention_low, gradient_split, preferred_element_type=jnp.float32
        ).astype(jnp.bfloat16)
        attention_gradient = jnp.einsum(
            "eqhd,ekhd->ehqk", gradient_split, value_split, preferred_element_type=jnp.float32
        )
        row_drift = jnp.einsum(
            "eqhd,eqhd->ehq",
            gradient_split,
            split_heads(attended),
            preferred_element_type=jnp.float32,
        )
        scores_gradient = (attention * (attention_gradient - row_drift[:, :, :, None])).astype(
            jnp.bfloat16
        )
        query_gradient = jnp.einsum(
            "ehqk,ekhd->eqhd",
            scores_gradient,
            split_heads(key_block),
            preferred_element_type=jnp.float32,
        ).astype(jnp.bfloat16)
        key_gradient = jnp.einsum(
            "ehqk,eqhd->ekhd",
            scores_gradient,
            split_heads(query_block),
            preferred_element_type=jnp.float32,
        ).astype(jnp.bfloat16)
        query_buffer = put_rows(
            query_buffer, merge_heads(query_gradient), starts_query, inside_query
        )
        key_buffer = put_rows(key_buffer, merge_heads(key_gradient), starts_key, inside_key)
        value_buffer = put_rows(value_buffer, merge_heads(value_gradient), starts_key, inside_key)
        return ((query_buffer, key_buffer, value_buffer), None)

    starting = (
        jnp.zeros((query_group_rows + decoder_slot, head_width), jnp.bfloat16),
        jnp.zeros((key_group_rows + encoder_slot, head_width), jnp.bfloat16),
        jnp.zeros((key_group_rows + encoder_slot, head_width), jnp.bfloat16),
    )
    finished, unused = lax.scan(
        backward_step,
        starting,
        (
            query_start_blocks,
            key_start_blocks,
            key_inside_blocks,
            query_inside_blocks,
            attention_store,
            attended_store,
        ),
    )
    query_result = finished[0][:query_group_rows]
    key_result = finished[1][:key_group_rows]
    value_result = finished[2][:key_group_rows]
    queries_gradient = lax.all_to_all(query_result, "pack", split_axis=0, concat_axis=1, tiled=True)
    keys_gradient, values_gradient = (
        lax.all_to_all(key_result, "pack", split_axis=0, concat_axis=1, tiled=True),
        lax.all_to_all(value_result, "pack", split_axis=0, concat_axis=1, tiled=True),
    )
    return (queries_gradient, keys_gradient, values_gradient, group_loss)


def solution(mesh):
    placed = (
        P(("dp", "pack"), None),
        P(("dp", "pack"), None),
        P(("dp", "pack"), None),
        P(("dp", "pack"), None),
        P("dp", None),
        P("dp", None),
        P("dp", None),
        P("dp", None),
        P("dp", None, None),
        P(),
    )
    return jax.shard_map(
        local,
        mesh=mesh,
        in_specs=placed,
        out_specs=(P(("dp", "pack"), None), P(("dp", "pack"), None), P(("dp", "pack"), None), P()),
        check_vma=False,
    )
```

profile of v0, /device:TPU:0, one launch (start us, length us, event | category | flops | bytes accessed | tf_op | source)
XLA Modules:
  0.0 832.8 jit_solution(14549999875438170626)
XLA Ops:
  3.1 5.2 all-to-all-start.1
  10.7 12.9 %all-to-all-done.1 = bf16[128,8,512]{0,2,1:T(8,128)(2,1)S(1)} async-done(((bf16[128,8,512]{0,2,1:T(8,128)(2,1)}), bf16[128,8,512]{0,2,1:T(8,128)(2,1)S(1)}, u32[]{:S(2)}, u32[]{:S(2)}) %all-to-all-start.1) | async-done | bytes 1048608 | tf_op jit(solution)/shard_map/all_to_all | solution.py:115
  30.4 4.1 copy.96
  38.5 15.4 %all-to-all-done = bf16[256,8,512]{0,2,1:T(8,128)(2,1)S(1)} async-done(((bf16[256,8,512]{0,2,1:T(8,128)(2,1)}), bf16[256,8,512]{0,2,1:T(8,128)(2,1)S(1)}, u32[]{:S(2)}, u32[]{:S(2)}) %all-to-all-start) | async-done | bytes 2097184 | tf_op jit(solution)/shard_map/all_to_all | solution.py:112
  58.9 3.9 copy.91
  62.8 3.9 copy.130
  70.0 106.8 %while.36 = (s32[]{:T(128)}, bf16[8,2,8,120,240]{4,3,2,1,0:T(8,128)(2,1)}, pred[8,2,240]{2,1,0:T(4,128)(4,1)S(1)}, s32[8,2]{0,1:T(2,128)S(1)}, bf16[1144,512]{0,...) while((s32[]{:T(128)}, ...), condition=%wide.region_5.6_spmd, body=%wide.region_2.5_spmd.sunk | while | flops 61198572 | bytes 3197165 | solution.py:134
  183.8 115.1 %while.37 = (s32[]{:T(128)}, bf16[1144,512]{0,1:T(8,128)(2,1)S(1)}, bf16[8,2,120,512]{2,3,1,0:T(8,128)(2,1)}, pred[8,2,120]{2,1,0:T(4,128)(4,1)S(1)}, s32[8,2]{0...) while((s32[]{:T(128)}, bf16[1144,512]{0,1:T(8,128)(2,1)S(1)}, ...), condition=%wide.region_7.8_spmd, body=%wide.region_6.7_spmd.sunk | while | flops 59473928 | bytes 4934157 | solution.py:152
  300.9 4.1 all-to-all-start.7
  305.0 11.7 %psum.14 = f32[16]{0:T(128)S(1)} all-reduce(f32[16]{0:T(128)S(1)} %convert_element_type.56), channel_id=1, replica_groups=mesh['dp'=4,'pack'=8] {'dp'}, use_global_device_ids=true, to_apply=%region_10.11 | all-reduce | flops 16 | bytes 128 | tf_op jit(solution)/shard_map/psum | solution.py:110
  330.5 15.2 %all-to-all-done.2 = bf16[128,8,512]{0,2,1:T(8,128)(2,1)S(1)} async-done(((bf16[128,8,512]{0,2,1:T(8,128)(2,1)}), bf16[128,8,512]{0,2,1:T(8,128)(2,1)S(1)}, u32[]{:S(2)}, u32[]{:S(2)}) %all-to-all-start.2) | async-done | bytes 1048608 | tf_op jit(solution)/shard_map/all_to_all | solution.py:177
  352.1 345.6 %while.38 = (s32[]{:T(128)}, bf16[1144,512]{0,1:T(8,128)(2,1)}, bf16[2288,512]{0,1:T(8,128)(2,1)}, bf16[2288,512]{0,1:T(8,128)(2,1)}, pred[8,2,120]{2,1,0:T(4,12...) while((s32[]{:T(128)}, bf16[1144,512]{0,1:T(8,128)(2,1)}, ...), condition=%wide.region_16.17_spmd, body=%wide.region_13.16_spmd.sunk | while | flops 301576576 | bytes 23691384 | solution.py:232
  457.3 3.8 dynamic_update_slice.50
  634.2 3.8 dynamic_update_slice.51
  643.2 3.8 dynamic_update_slice.52
  705.5 3.9 copy.113
  709.5 9.8 %all-to-all-done.4 = bf16[8,128,512]{2,1,0:T(8,128)(2,1)S(1)} async-done(((bf16[8,128,512]{2,1,0:T(8,128)(2,1)}), bf16[8,128,512]{2,1,0:T(8,128)(2,1)S(1)}, u32[]{:S(2)}, u32[]{:S(2)}) %all-to-all-start.4) | async-done | bytes 1048608 | tf_op jit(solution)/shard_map/all_to_all | solution.py:247
  719.3 4.5 all-to-all-start.5
  725.4 3.9 copy.115
  729.3 21.1 %all-to-all-done.5 = bf16[8,256,512]{2,1,0:T(8,128)(2,1)} async-done(((bf16[8,256,512]{2,1,0:T(8,128)(2,1)}), bf16[8,256,512]{2,1,0:T(8,128)(2,1)}, u32[]{:S(2)}, u32[]{:S(2)}) %all-to-all-start.5) | async-done | bytes 2097184 | tf_op jit(solution)/shard_map/all_to_all | solution.py:249
  754.3 60.0 %psum.15 = f32[16]{0:T(128)S(1)} all-reduce(f32[16]{0:T(128)S(1)} %select_reduce_fusion.4), channel_id=1, replica_groups=mesh['dp'=4,'pack'=8] {'dp','pack'}, use_global_device_ids=true, to_apply=%region_20.21 | all-reduce | flops 16 | bytes 128 | tf_op jit(solution)/shard_map/psum | solution.py:169
  818.4 3.9 copy.114
  822.3 4.1 copy.121
  828.8 4.1 copy.122
  (495 shorter events, 440.8 us)
Async XLA Ops:
  0.6 7.6 copy-start.3
  3.1 20.6 %all-to-all-start.1 = ((bf16[128,8,512]{0,2,1:T(8,128)(2,1)}), bf16[128,8,512]{0,2,1:T(8,128)(2,1)S(1)}, u32[]{:S(2)}, u32[]{:S(2)}) async-start(bf16[128,8,512]{0,2,1:T(8,128)(2,1)} %bitcast.60), calls=%async_computation.1 | async-start | bytes 2097152 | tf_op jit(solution)/shard_map/all_to_all | solution.py:115
  23.6 3.8 copy-start.4
  23.6 3.8 copy-start.6
  23.6 3.8 copy-start.7
  23.6 4.1 copy-start.5
  23.6 5.6 copy-start.8
  23.7 30.3 %all-to-all-start = ((bf16[256,8,512]{0,2,1:T(8,128)(2,1)}), bf16[256,8,512]{0,2,1:T(8,128)(2,1)S(1)}, u32[]{:S(2)}, u32[]{:S(2)}) async-start(bf16[256,8,512]{0,2,1:T(8,128)(2,1)} %bitcast.233), calls=%async_computation | async-start | bytes 4194304 | tf_op jit(solution)/shard_map/all_to_all | solution.py:112
  54.0 1.3 copy-start.2
  55.3 121.5 %all-to-all-start.3 = ((bf16[256,8,512]{0,2,1:T(8,128)(2,1)}), bf16[256,8,512]{0,2,1:T(8,128)(2,1)S(1)}, u32[]{:S(2)}, u32[]{:S(2)}) async-start(bf16[256,8,512]{0,2,1:T(8,128)(2,1)} %bitcast.67), calls=%async_computation.3 | async-start | bytes 4194304 | tf_op jit(solution)/shard_map/all_to_all | solution.py:113
  299.6 17.2 %copy-start.9 = (s32[16]{0:T(128)S(1)}, s32[16]{0:T(128)}, u32[]{:S(2)}) copy-start(s32[16]{0:T(128)} %param.25) | copy-start | bytes 196
  300.9 19.5 %all-to-all-start.7 = ((bf16[8,128,512]{1,2,0:T(8,128)(2,1)}), bf16[8,128,512]{1,2,0:T(8,128)(2,1)S(1)}, u32[]{:S(2)}, u32[]{:S(2)}) async-start(bf16[8,128,512]{1,2,0:T(8,128)(2,1)} %copy.118), calls=%async_computation.7 | async-start | bytes 2097152 | tf_op jit(solution)/shard_map/all_to_all | solution.py:159
  326.8 18.9 %all-to-all-start.2 = ((bf16[128,8,512]{0,2,1:T(8,128)(2,1)}), bf16[128,8,512]{0,2,1:T(8,128)(2,1)S(1)}, u32[]{:S(2)}, u32[]{:S(2)}) async-start(bf16[128,8,512]{0,2,1:T(8,128)(2,1)} %bitcast.64), calls=%async_computation.2 | async-start | bytes 2097152 | tf_op jit(solution)/shard_map/all_to_all | solution.py:177
  699.0 4.9 copy-start
  700.4 18.9 %all-to-all-start.4 = ((bf16[8,128,512]{2,1,0:T(8,128)(2,1)}), bf16[8,128,512]{2,1,0:T(8,128)(2,1)S(1)}, u32[]{:S(2)}, u32[]{:S(2)}) async-start(bf16[8,128,512]{2,1,0:T(8,128)(2,1)} %bitcast.244), calls=%async_computation.4 | async-start | bytes 2097152 | tf_op jit(solution)/shard_map/all_to_all | solution.py:247
  719.3 4.5 copy-start.1
  719.3 31.1 %all-to-all-start.5 = ((bf16[8,256,512]{2,1,0:T(8,128)(2,1)}), bf16[8,256,512]{2,1,0:T(8,128)(2,1)}, u32[]{:S(2)}, u32[]{:S(2)}) async-start(bf16[8,256,512]{2,1,0:T(8,128)(2,1)} %bitcast.234), calls=%async_computation.5 | async-start | bytes 4194304 | tf_op jit(solution)/shard_map/all_to_all | solution.py:249
  750.4 76.0 %all-to-all-start.6 = ((bf16[8,256,512]{2,1,0:T(8,128)(2,1)}), bf16[8,256,512]{2,1,0:T(8,128)(2,1)S(1)}, u32[]{:S(2)}, u32[]{:S(2)}) async-start(bf16[8,256,512]{2,1,0:T(8,128)(2,1)} %bitcast.76), calls=%async_computation.6 | async-start | bytes 4194304 | tf_op jit(solution)/shard_map/all_to_all | solution.py:250
where the time goes:
time: 842 us; the launch traced here: 833 us
  local copies, waits for them, and re-layouts  334 us (40%)
  loops' own time  188 us (22%)
  matrix products  79.6 us (9%)
  waiting for transfers between devices  76.5 us (9%)
  blocking collectives  71.8 us (9%)
  other arithmetic  50.5 us (6%)
  starting transfers between devices  32 us (4%)
    dynamic_update_slice x64, local copies, waits for them, and re-layouts, put_rows(): buffer = lax.dynamic_update_slice_in_dim(buffer, merged, starts[item], 0)  157 us
    another operation x1, loops' own time, local(): lax.scan(backward_step, starting, (query_start_blocks, key_start_blocks,...  63 us
    another operation x1, loops' own time, local(): lax.scan(output_step, attended_start, (attention_store, key_start_blocks,...  62.7 us
    another operation x1, loops' own time, local(): lax.map(forward_block, (query_start_blocks, key_start_blocks, key_inside_...  62.3 us
    psum x1, blocking collectives, local(): loss_sum = lax.psum(loss_part, ('dp', 'pack'))  60 us
    dynamic_slice x40, local copies, waits for them, and re-layouts, take_rows(): lax.dynamic_slice_in_dim(table, starts[item], slot_total, 0)  57.4 us
    select_n x48, other arithmetic, put_rows(): merged = jnp.where(inside[item][:, None], block[item], current)  42.2 us
    unnamed x31, local copies, waits for them, and re-layouts  30.1 us
  transfers between devices with their start and end apart: 8, of which 6 were waited for; matrix products, arithmetic and copies ran while one was open for 11% of the time, Pallas kernels for 0%

commit v1 on v0

v1 whole, which is shorter than its diff:
```python
import functools

import jax
import jax.numpy as jnp
from jax import lax
from jax.experimental import pallas as pl
from jax.experimental.pallas import tpu as pltpu
from jax.sharding import PartitionSpec as P

HEAD_DIM = 64
PAIR = 2 * HEAD_DIM
EX_DEV = 2
GROUPS = 16
CHUNKS = 4
UNROLL = 2
ALONE = pltpu.CompilerParams(vmem_limit_bytes=60 * 1024 * 1024)
ROOM = pltpu.CompilerParams(vmem_limit_bytes=16 * 1024 * 1024)
FIELDS = 8
SMALL = pl.CostEstimate(flops=0, bytes_accessed=2 * 1024 * 1024, transcendentals=0)
ANY = pl.BlockSpec(memory_space=pl.ANY)
HBM = pl.BlockSpec(memory_space=pltpu.HBM)
SMEM = pl.BlockSpec(memory_space=pltpu.SMEM)
VMEM = pl.BlockSpec(memory_space=pltpu.VMEM)


def table_kernel(
    me_ref,
    input_ref,
    target_ref,
    enc_ref,
    dec_ref,
    task_ref,
    k_ref,
    v_ref,
    *refs,
):
    kv_ref, table_ref, count_ref, held, sem = refs[-5:]
    me = me_ref[0]
    core = lax.rem(me, 2)
    half = held.shape[-1]
    columns = pl.ds(pl.multiple_of((1 - core) * half, half), half)
    into = [
        pltpu.make_async_copy(source.at[:, columns], held.at[tensor], sem.at[tensor])
        for tensor, source in enumerate((k_ref, v_ref))
    ]
    out = [
        pltpu.make_async_copy(held.at[tensor], kv_ref.at[tensor], sem.at[2 + tensor])
        for tensor in range(2)
    ]
    for copy in into:
        copy.start()
    total = enc_ref.shape[1]
    for side in range(2):
        pack = me + side * (1 - 2 * core)

        def find(item, carry, pack=pack):
            first, second = carry
            hit = enc_ref[0, item] == pack
            return (
                jnp.where(hit & (first < 0), item, first),
                jnp.where(hit & (first >= 0), item, second),
            )

        first, second = lax.fori_loop(0, total, find, (jnp.int32(-1), jnp.int32(-1)))
        second = jnp.maximum(second, 0)
        first = jnp.maximum(first, 0)
        for place, item in enumerate((first, second)):
            row = 2 * side + place
            dec = dec_ref[0, item]

            def before(other, offset, dec=dec):
                return offset + jnp.where(dec_ref[0, other] == dec, target_ref[0, other], 0)

            table_ref[row, 0] = dec ^ me
            table_ref[row, 1] = lax.fori_loop(0, item, before, jnp.int32(0))
            table_ref[row, 2] = target_ref[0, item]
            table_ref[row, 3] = jnp.int32(0) if place == 0 else input_ref[0, first]
            table_ref[row, 4] = input_ref[0, item]
            table_ref[row, 5] = task_ref[0, item]
            table_ref[row, 6] = 0
            table_ref[row, 7] = 0
    lane = lax.broadcasted_iota(jnp.int32, (1, 128), 1)
    counts = jnp.zeros((1, 128), jnp.float32)
    for item in range(total):
        amount = target_ref[0, item].astype(jnp.float32)
        counts = counts + jnp.where(lane == task_ref[0, item], amount, 0.0)
    count_ref[...] = counts
    for tensor in range(2):
        into[tensor].wait()
        out[tensor].start()
    for tensor in range(2):
        out[tensor].wait()


def tabulate(me, lengths, targets, enc_pack, dec_pack, task, keys, values, waits):
    rows, features = keys.shape
    half = features // 2
    return pl.pallas_call(
        table_kernel,
        out_shape=[
            jax.ShapeDtypeStruct((2, rows, half), keys.dtype),
            jax.ShapeDtypeStruct((4, FIELDS), jnp.int32),
            jax.ShapeDtypeStruct((1, 128), jnp.float32),
        ],
        in_specs=[SMEM] * 6 + [HBM] * 2 + [ANY] * len(waits),
        out_specs=[ANY, SMEM, VMEM],
        scratch_shapes=[pltpu.VMEM((2, rows, half), keys.dtype), pltpu.SemaphoreType.DMA((4,))],
        compiler_params=ROOM,
        cost_estimate=SMALL,
        name="tabulate",
    )(me, lengths, targets, enc_pack, dec_pack, task, keys, values, *waits)


def split_kernel(me_ref, q_ref, c_ref, own_ref, other_ref, held, sem):
    half = held.shape[-1]
    core = lax.rem(me_ref[0], 2)
    into, out = [], []
    for side, (base, target) in enumerate(((core, own_ref), (1 - core, other_ref))):
        columns = pl.ds(pl.multiple_of(base * half, PAIR), half)
        for tensor, source in enumerate((q_ref, c_ref)):
            place = 2 * side + tensor
            into.append(
                pltpu.make_async_copy(source.at[:, columns], held.at[place], sem.at[place])
            )
            out.append(
                pltpu.make_async_copy(held.at[place], target.at[tensor], sem.at[4 + place])
            )
    for copy in into:
        copy.start()
    for place in range(4):
        into[place].wait()
        out[place].start()
    for copy in out:
        copy.wait()


def split(me, queries, cotangent):
    rows, features = queries.shape
    half = features // 2
    return pl.pallas_call(
        split_kernel,
        out_shape=[jax.ShapeDtypeStruct((2, rows, half), queries.dtype)] * 2,
        in_specs=[SMEM] + [HBM] * 2,
        out_specs=[ANY] * 2,
        scratch_shapes=[
            pltpu.VMEM((4, rows, half), queries.dtype),
            pltpu.SemaphoreType.DMA((8,)),
        ],
        compiler_params=ROOM,
        cost_estimate=SMALL,
        name="split_columns",
    )(me, queries, cotangent)


def layout(packs):
    if packs == 8:
        return [(0, 2), (2, 2), (4, 2), (6, 1), (7, 1)]
    return [(first, 2) for first in range(0, packs, 2)]


def attention_kernel(
    me_ref, table_ref, scale_ref, *refs, packs, first, waits, half, at
):
    places = layout(packs)
    sources = len(places)
    pieces = refs[:packs]
    k_ref, v_ref, sibling_ref = refs[packs : packs + 3]
    outs = refs[packs + 3 + (0 if first else 3) + waits :]
    k_out, v_out, sibling_out = outs[:3]
    query_outs = outs[3 : 3 + sources]
    loss_out = outs[3 + sources]
    kv, qc, dq, dkv, loss, bias, scaling, in_sem, qc_sem, out_sem, dkv_sem = outs[sources + 4 :]
    width = qc.shape[-1]
    rows = qc.shape[2]
    keys = kv.shape[2]
    core = lax.rem(me_ref[0], 2)
    own_columns = pl.ds(pl.multiple_of(core * half + at, PAIR), width)
    half_columns = pl.ds(at, width)
    kv_copies = [
        [
            pltpu.make_async_copy(k_ref.at[:, own_columns], kv.at[0, 0], in_sem.at[0, 0]),
            pltpu.make_async_copy(v_ref.at[:, own_columns], kv.at[0, 1], in_sem.at[0, 1]),
        ],
        [
            pltpu.make_async_copy(
                sibling_ref.at[tensor, :, half_columns], kv.at[1, tensor], in_sem.at[1, tensor]
            )
            for tensor in range(2)
        ],
    ]
    dkv_copies = [
        [
            pltpu.make_async_copy(dkv.at[0, 0], k_out.at[:, own_columns], dkv_sem.at[0, 0]),
            pltpu.make_async_copy(dkv.at[0, 1], v_out.at[:, own_columns], dkv_sem.at[0, 1]),
        ],
        [
            pltpu.make_async_copy(
                dkv.at[1, tensor], sibling_out.at[tensor, :, half_columns], dkv_sem.at[1, tensor]
            )
            for tensor in range(2)
        ],
    ]
    for side in range(2):
        for copy in kv_copies[side]:
            copy.start()
        for place in range(2):
            item = 2 * side + place
            owner = table_ref[item, 0]
            for distance, piece in enumerate(pieces):

                @pl.when(owner == distance)
                def _(piece=piece, item=item):
                    pltpu.make_async_copy(
                        piece.at[:, :, half_columns], qc.at[item], qc_sem.at[item]
                    ).start()

    dq[...] = jnp.zeros_like(dq)
    loss[...] = jnp.zeros_like(loss)
    lane = lax.broadcasted_iota(jnp.int32, (1, PAIR), 1)
    low = lane < HEAD_DIM
    row = lax.broadcasted_iota(jnp.int32, (rows, PAIR), 0)
    row_lane = lax.broadcasted_iota(jnp.int32, (1, rows), 1)
    key = lax.broadcasted_iota(jnp.int32, (keys, rows), 0)

    def dot(left, right):
        return jnp.dot(left, right, preferred_element_type=jnp.float32)

    vector = jnp.zeros((1, 128), jnp.float32)
    for side in range(2):
        for copy in kv_copies[side]:
            copy.wait()
        for place in range(2):
            item = 2 * side + place
            pltpu.make_async_copy(
                pieces[0].at[:, :, half_columns], qc.at[item], qc_sem.at[item]
            ).wait()
        owner, scale_rows = [], []
        for place in range(2):
            item = 2 * side + place
            start, length = table_ref[item, 1], table_ref[item, 2]
            key_start, key_length = table_ref[item, 3], table_ref[item, 4]
            scale = scale_ref[0, table_ref[item, 5]]
            span = slice(place * rows, (place + 1) * rows)
            bias[:, span] = jnp.where(
                (key >= key_start) & (key < key_start + key_length), 0.0, -1e30
            )
            scaling[span] = jnp.where((row >= start) & (row < start + length), scale, 0.0)
            scale_rows.append(
                jnp.where((row_lane >= start) & (row_lane < start + length), scale, 0.0)
            )
            owner.append(table_ref[item, 0])
        scale_row = jnp.concatenate(scale_rows, axis=1)

        def pair_step(pair, carry, side=side, owner=owner, scale_row=scale_row):
            columns = pl.ds(pl.multiple_of(pair * PAIR, PAIR), PAIR)
            key_pair = kv[side, 0, :, columns]
            value_pair = kv[side, 1, :, columns]
            query = jnp.concatenate([qc[2 * side + place, 0, :, columns] for place in range(2)], axis=0)
            cot = jnp.concatenate([qc[2 * side + place, 1, :, columns] for place in range(2)], axis=0)
            zero = jnp.zeros_like(key_pair)

            def heads(array):
                return jnp.concatenate(
                    [jnp.where(low, array, zero), jnp.where(low, zero, array)], axis=0
                )

            up = (cot.astype(jnp.float32) * scaling[...]).astype(jnp.bfloat16)
            query_turned, key_turned, value_turned = query.T, key_pair.T, value_pair.T
            cot_turned = cot.T.astype(jnp.float32)
            up_turned = (cot_turned * scale_row).astype(jnp.bfloat16)
            both_scores = dot(heads(key_pair), query_turned)
            both_slopes = dot(heads(value_pair), up_turned)
            query_parts, weights_parts, grad_parts = [], [], []
            for head in range(2):
                spread = slice(head * keys, (head + 1) * keys)
                part = slice(head * HEAD_DIM, (head + 1) * HEAD_DIM)
                scores = both_scores[spread] + bias[...]
                highest = jnp.max(scores, axis=0, keepdims=True)
                powers = jnp.exp(scores - highest)
                weights = powers * (1.0 / jnp.sum(powers, axis=0, keepdims=True))
                weights_low = weights.astype(jnp.bfloat16)
                attended = dot(value_turned[part], weights_low)
                attended = attended.astype(jnp.bfloat16).astype(jnp.float32)
                token = cot_turned[part] * attended
                loss[side] += jnp.sum(token.reshape(HEAD_DIM // 8, 8, 2 * rows), axis=0)
                drift = jnp.sum(
                    up_turned[part].astype(jnp.float32) * attended, axis=0, keepdims=True
                )
                grad = (weights * (both_slopes[spread] - drift)).astype(jnp.bfloat16)
                query_parts.append(dot(key_turned[part], grad))
                grad_parts.append(grad)
                weights_parts.append(weights_low)
            query_grad = jnp.concatenate(query_parts, axis=0).astype(jnp.bfloat16).T
            for place in range(2):
                at = owner[place]
                span = slice(place * rows, (place + 1) * rows)
                dq[at, :, columns] = dq[at, :, columns] + query_grad[span]
            key_grad = dot(jnp.concatenate(grad_parts, axis=1), heads(query))
            value_grad = dot(jnp.concatenate(weights_parts, axis=1), heads(up))
            dkv[side, 0, :, columns] = key_grad.astype(jnp.bfloat16)
            dkv[side, 1, :, columns] = value_grad.astype(jnp.bfloat16)
            return carry

        lax.fori_loop(0, width // PAIR, pair_step, 0, unroll=UNROLL)
        for copy in dkv_copies[side]:
            copy.start()
        for place in range(2):
            item = 2 * side + place
            start, length = table_ref[item, 1], table_ref[item, 2]
            part = jnp.sum(loss[side][:, place * rows : (place + 1) * rows], axis=0, keepdims=True)
            part = jnp.where((row_lane >= start) & (row_lane < start + length), part, 0.0)
            amount = jnp.sum(part, axis=1, keepdims=True)
            vector = vector + jnp.where(lane == table_ref[item, 5], amount, 0.0)

    query_copies = [
        pltpu.make_async_copy(
            dq.at[pl.ds(base, 2)] if count == 2 else dq.at[base], target, out_sem.at[i]
        )
        for i, (target, (base, count)) in enumerate(zip(query_outs, places))
    ]
    for copy in query_copies:
        copy.start()
    loss_out[...] = vector
    for side in range(2):
        for copy in dkv_copies[side]:
            copy.wait()
    for copy in query_copies:
        copy.wait()


def attention_chunk(
    me, table, scales, pieces, keys, values, sibling, full, waits, packs, at, width
):
    sources = len(layout(packs))
    rows = pieces[0].shape[1]
    key_rows, features = keys.shape
    half = features // 2
    low = jnp.bfloat16
    first = full is None
    flops = rows * key_rows * width
    before = 3 + packs + 3
    return pl.pallas_call(
        functools.partial(
            attention_kernel,
            packs=packs,
            first=first,
            waits=len(waits),
            half=half,
            at=at,
        ),
        out_shape=[
            jax.ShapeDtypeStruct(keys.shape, low),
            jax.ShapeDtypeStruct(keys.shape, low),
            jax.ShapeDtypeStruct((2, key_rows, half), low),
        ]
        + [
            jax.ShapeDtypeStruct((count, rows, width)[2 - count :], low)
            for _, count in layout(packs)
        ]
        + [jax.ShapeDtypeStruct((1, 128), jnp.float32)],
        in_specs=[SMEM] * 3 + [ANY] * packs + [HBM] * 2 + [ANY] + [HBM] * (0 if first else 3) + [ANY] * len(waits),
        out_specs=[HBM] * 3 + [ANY] * sources + [VMEM],
        scratch_shapes=[
            pltpu.VMEM((2, 2, key_rows, width), low),
            pltpu.VMEM((4, 2, rows, width), low),
            pltpu.VMEM((packs, rows, width), low),
            pltpu.VMEM((2, 2, key_rows, width), low),
            pltpu.VMEM((2, 8, 2 * rows), jnp.float32),
            pltpu.VMEM((key_rows, 2 * rows), jnp.float32),
            pltpu.VMEM((2 * rows, PAIR), jnp.float32),
            pltpu.SemaphoreType.DMA((2, 2)),
            pltpu.SemaphoreType.DMA((4,)),
            pltpu.SemaphoreType.DMA((sources,)),
            pltpu.SemaphoreType.DMA((2, 2)),
        ],
        input_output_aliases={} if first else {before + i: i for i in range(3)},
        compiler_params=ROOM,
        cost_estimate=pl.CostEstimate(
            flops=flops, bytes_accessed=8 * 1024 * 1024, transcendentals=0
        ),
        name="attention_chunk",
    )(me, table, scales, *pieces, keys, values, sibling, *(() if first else full), *waits)


def finish_kernel(me_ref, *refs, spots, half, with_keys):
    count = 2 * len(spots)
    outs = refs[-1 - (3 if with_keys else 1) : -1]
    sem = refs[-1]
    core = lax.rem(me_ref[0], 2)
    moves = []
    for i, (at, width) in enumerate(spots):
        for side, base in enumerate((core, 1 - core)):
            columns = pl.ds(pl.multiple_of(base * half + at, PAIR), width)
            moves.append((refs[2 * i + side], outs[0], columns))
    if with_keys:
        other = pl.ds(pl.multiple_of((1 - core) * half, PAIR), half)
        moves += [(refs[count].at[tensor], outs[1 + tensor], other) for tensor in range(2)]
    copies = [
        pltpu.make_async_copy(source, out.at[:, columns], sem.at[i])
        for i, (source, out, columns) in enumerate(moves)
    ]
    for copy in copies:
        copy.start()
    for copy in copies:
        copy.wait()


def finish(me, parts, spots, like, back=None, given=()):
    with_keys = back is not None
    read = len(parts) + (1 if with_keys else 0)
    shapes = [jax.ShapeDtypeStruct(like.shape, like.dtype)]
    if with_keys:
        shapes += [jax.ShapeDtypeStruct(array.shape, array.dtype) for array in given]
    skipped = len(shapes) - len(given)
    return pl.pallas_call(
        functools.partial(
            finish_kernel, spots=spots, half=like.shape[1] // 2, with_keys=with_keys
        ),
        out_shape=shapes,
        in_specs=[SMEM] + [VMEM] * read + [HBM] * len(given),
        out_specs=[HBM] * len(shapes),
        scratch_shapes=[pltpu.SemaphoreType.DMA((len(parts) + 2,))],
        input_output_aliases={1 + read + i: skipped + i for i in range(len(given))},
        compiler_params=ROOM,
        cost_estimate=SMALL,
        name="finish",
    )(me, *parts, *((back,) if with_keys else ()), *given)


def swap(array, axis_name, size, bits):
    return lax.ppermute(array, axis_name, [(i, i ^ bits) for i in range(size)])


def after(vector, arrays):
    for array in arrays:
        vector = vector + 0.0 * array[0, 0, 0].astype(jnp.float32)
    return vector


def group_sum(array, axis_name, size):
    step = 1
    while step < size:
        if 4 * step <= size:
            first, second, third = (swap(array, axis_name, size, step * i) for i in (1, 2, 3))
            array = (array + first) + (second + third)
            step *= 4
        else:
            array = array + swap(array, axis_name, size, step)
            step *= 2
    return array


def local(
    enc_keys,
    enc_values,
    dec_queries,
    cotangent,
    input_lengths,
    target_lengths,
    enc_pack,
    dec_pack,
    task_group,
    dro_weights,
    *,
    packs,
    groups,
):
    me = lax.axis_index("pack").astype(jnp.int32).reshape(1)
    rows, features = dec_queries.shape
    half = features // 2
    total_tokens = rows * packs * groups
    relayed = packs == 8

    def swapped(array, bits):
        return swap(array, "pack", packs, bits)

    own, other = split(me, dec_queries, cotangent)
    pieces = [own]
    for bits in range(1, 6 if relayed else packs):
        pieces.append(swapped(other if bits & 1 else own, bits))
    if relayed:
        pieces += [swapped(pieces[2], 4), swapped(pieces[5], 2)]
    kv_other, table, group_counts = tabulate(
        me,
        input_lengths,
        target_lengths,
        enc_pack,
        dec_pack,
        task_group[:, :, 0],
        enc_keys,
        enc_values,
        [own],
    )
    kv_sibling = swapped(kv_other, 1)
    counts = group_sum(group_counts, "dp", groups)
    weights = dro_weights.astype(jnp.float32)
    weights = jnp.pad(weights, (0, 128 - GROUPS)).reshape(1, 128)
    scales = weights / jnp.sum(weights) * (total_tokens / counts)

    full, losses, query_parts, spots = None, [], [], []
    halfway, whole = [], []
    width = half // CHUNKS
    for chunk in range(CHUNKS):
        at = chunk * width
        order = sum(halfway[:-1][-1:], []) + whole[:-2][-1:]
        *result, loss = attention_chunk(
            me, table, scales, pieces, enc_keys, enc_values, kv_sibling, full,
            order, packs, at, width,
        )
        full, parts = result[:3], result[3:]
        losses.append(loss)
        if relayed:
            far = swapped(parts.pop(), 4)
            near = swapped(parts.pop(), 2)
            parts[2] = parts[2] + jnp.stack([near, jnp.zeros_like(near)])
            parts[1] = parts[1] + jnp.stack([jnp.zeros_like(far), far])
            halfway.append(parts[1:])
        summed = parts[0]
        for chip in range(1, len(parts)):
            summed = summed + swapped(parts[chip], 2 * chip)
        whole.append(summed)
        query_parts += [summed[0], swapped(summed[1], 1)]
        spots.append((at, width))
    back = swapped(full[2], 1)
    queries_gradient, keys_gradient, values_gradient = finish(
        me, query_parts[:-2], spots[:-1], dec_queries, back, full[:2]
    )
    (queries_gradient,) = finish(
        me, query_parts[-2:], spots[-1:], dec_queries, None, (queries_gradient,)
    )
    loss = functools.reduce(jnp.add, losses)
    loss = group_sum(after(loss, whole[-3:-2]), "pack", packs)
    loss = group_sum(after(loss, parts[1:]), "dp", groups)
    group_loss = (loss / counts)[0, :GROUPS]
    return (queries_gradient, keys_gradient, values_gradient, group_loss)


def solution(mesh):
    placed = (
        P(("dp", "pack"), None),
        P(("dp", "pack"), None),
        P(("dp", "pack"), None),
        P(("dp", "pack"), None),
        P("dp", None),
        P("dp", None),
        P("dp", None),
        P("dp", None),
        P("dp", None, None),
        P(),
    )
    return jax.shard_map(
        functools.partial(local, packs=mesh.shape["pack"], groups=mesh.shape["dp"]),
        mesh=mesh,
        in_specs=placed,
        out_specs=(P(("dp", "pack"), None), P(("dp", "pack"), None), P(("dp", "pack"), None), P()),
        check_vma=False,
    )
```

time: 842 us -> 161 us (0.19); the launches traced: 833 us -> 161 us
  local copies, waits for them, and re-layouts: 334 us -> 6.33 us
  loops' own time: 188 us -> 0 us
  matrix products: 79.6 us -> 0 us
  blocking collectives: 71.8 us -> 0 us
  other arithmetic: 50.5 us -> 1.67 us
  Pallas kernels: 0 us -> 37.2 us
    another operation x3 -> x0, loops' own time: 188 us -> none  [the longest x1 63 us: local(): lax.scan(backward_step, starting, (query_start_blocks, key_start_blocks,...]
    dynamic_update_slice x72 -> x0, local copies, waits for them, and re-layouts: 163 us -> none  [the longest x64 157 us: put_rows(): buffer = lax.dynamic_update_slice_in_dim(buffer, merged, starts[item], 0)]
    all_to_all x8 -> x0, waiting for transfers between devices: 76.5 us -> none  [the longest x1 21.1 us: local(): lax.all_to_all(key_result, 'pack', split_axis=0, concat_axis=1, tiled=True)]
    ppermute x0 -> x39, waiting for transfers between devices: none -> 73.3 us  [swap(): return lax.ppermute(array, axis_name, [(i, i ^ bits) for i in range(size)])]
    psum x2 -> x0, blocking collectives: 71.8 us -> none  [the longest x1 60 us: local(): loss_sum = lax.psum(loss_part, ('dp', 'pack'))]
    dynamic_slice x98 -> x0, local copies, waits for them, and re-layouts: 67.8 us -> none  [the longest x40 57.4 us: take_rows(): lax.dynamic_slice_in_dim(table, starts[item], slot_total, 0)]
    dot_general x40 -> x0, matrix products: 48.8 us -> none  [the longest x8 17.3 us: backward_step(): jnp.einsum('eqhd,ekhd->ehqk', gradient_split, value_split, preferred_elem...]
    select_n x49 -> x0, other arithmetic: 42.2 us -> none  [the longest x48 42.2 us: put_rows(): merged = jnp.where(inside[item][:, None], block[item], current)]
  transfers between devices with their start and end apart: 8 -> 39, of which waited for: 6 -> 16; matrix products, arithmetic and copies ran while one was open for 11% -> 2% of each run, Pallas kernels for 0% -> 17%
where the time goes in v1:
time: 161 us
  waiting for transfers between devices  73.3 us (46%)
  starting transfers between devices  39.7 us (25%)
  Pallas kernels  37.2 us (23%)
  local copies, waits for them, and re-layouts  6.33 us (4%)
  between operations  3.05 us (2%)
  other arithmetic  1.67 us (1%)
    ppermute x39, waiting for transfers between devices, swap(): return lax.ppermute(array, axis_name, [(i, i ^ bits) for i in range(size)])  73.3 us
    ppermute x39, starting transfers between devices, swap(): return lax.ppermute(array, axis_name, [(i, i ^ bits) for i in range(size)])  39.7 us
    pallas_call x4, Pallas kernels, attention_chunk(): pl.pallas_call(functools.partial(attention_kernel, packs=packs, first=fir...  32.3 us
    unnamed x20, local copies, waits for them, and re-layouts  4.2 us
  transfers between devices with their start and end apart: 39, of which 16 were waited for; matrix products, arithmetic and copies ran while one was open for 2% of the time, Pallas kernels for 17%

profile of v1, /device:TPU:0, one launch (start us, length us, event | category | flops | bytes accessed | tf_op | source)
XLA Modules:
  0.0 161.1 jit_solution(849412612388058685)
XLA Ops:
  4.2 2.6 %collective-permute-start.7 = (bf16[2,128,2048]{2,1,0:T(8,128)(2,1)S(1)}, bf16[2,128,2048]{2,1,0:T(8,128)(2,1)S(1)}, u32[]{:S(2)}, u32[]{:S(2)}) collective-permute-start(bf16[2,128,2048]{2,1,0:T(8,128)(2,1)S(1)} %get-tuple-element.51), channel_id=1, source_target_pairs={{0,5},{1,4},{2,7},{3,6},{4,1},{5,0},{6,3},{7,2},{8,13},{9,12},{10,... | collective-permute-start | bytes 3145736 | tf_op jit(solution)/shard_map/ppermute | solution.py:431
  9.9 2.1 %tabulate.1 = (bf16[2,256,2048]{2,1,0:T(8,128)(2,1)S(1)}, s32[4,8]{1,0:T(4,128)S(1)}, f32[1,128]{1,0:T(1,128)S(1)}) custom-call(s32[1]{0:T(128)} %bitcast.me_ref, s32[1,16]{1,0:T(1,128)S(1)} %copy-done.4, s32[1,16]{1,0:T(1,128)S(1)} %copy-done.5, s32[1,16]{1,0:T(1,128)S(1)} %copy-done.6, s32[1,16]{1,0:T(1,128)S(1)} %copy-done.7, s32[1,16]{1,0:T(1,128)S(1)} %bitcast.33, ...), custom_call_target="tpu_custom_call" | custom-call | bytes 2097152 | tf_op jit(solution)/shard_map/tabulate/pallas_call | solution.py:98
  12.1 2.7 %collective-permute-start.1 = (f32[1,128]{1,0:T(1,128)S(1)}, f32[1,128]{1,0:T(1,128)S(1)}, u32[]{:S(2)}, u32[]{:S(2)}) collective-permute-start(f32[1,128]{1,0:T(1,128)S(1)} %get-tuple-element.50), channel_id=1, source_target_pairs={{0,16},{8,24},{16,0},{24,8},{1,17},{9,25},{17,1},{25,9},{2,18},{10... | collective-permute-start | bytes 1544 | tf_op jit(solution)/shard_map/ppermute | solution.py:431
  14.8 1.8 %collective-permute-done.1 = f32[1,128]{1,0:T(1,128)S(1)} collective-permute-done((f32[1,128]{1,0:T(1,128)S(1)}, f32[1,128]{1,0:T(1,128)S(1)}, u32[]{:S(2)}, u32[]{:S(2)}) %collective-permute-start.1) | collective-permute-done | bytes 544 | tf_op jit(solution)/shard_map/ppermute | solution.py:431
  16.6 3.7 %collective-permute-start.2 = (f32[1,128]{1,0:T(1,128)S(1)}, f32[1,128]{1,0:T(1,128)S(1)}, u32[]{:S(2)}, u32[]{:S(2)}) collective-permute-start(f32[1,128]{1,0:T(1,128)S(1)} %get-tuple-element.50), channel_id=1, source_target_pairs={{0,24},{8,16},{16,8},{24,0},{1,25},{9,17},{17,9},{25,1},{2,26},{10... | collective-permute-start | bytes 1544 | tf_op jit(solution)/shard_map/ppermute | solution.py:431
  21.9 3.5 %collective-permute-done = f32[1,128]{1,0:T(1,128)S(1)} collective-permute-done((f32[1,128]{1,0:T(1,128)S(1)}, f32[1,128]{1,0:T(1,128)S(1)}, u32[]{:S(2)}, u32[]{:S(2)}) %collective-permute-start) | collective-permute-done | bytes 544 | tf_op jit(solution)/shard_map/ppermute | solution.py:431
  26.0 6.9 %collective-permute-done.4.refs_2_ = bf16[2,128,2048]{2,1,0:T(8,128)(2,1)S(1)} collective-permute-done((bf16[2,128,2048]{2,1,0:T(8,128)(2,1)S(1)}, bf16[2,128,2048]{2,1,0:T(8,128)(2,1)S(1)}, u32[]{:S(2)}, u32[]{:S(2)}) %collective-permute-start.4) | collective-permute-done | bytes 1048608 | tf_op jit(solution)/shard_map/ppermute | solution.py:431
  32.8 2.0 %collective-permute-start.9 = (bf16[2,128,2048]{2,1,0:T(8,128)(2,1)S(1)}, bf16[2,128,2048]{2,1,0:T(8,128)(2,1)S(1)}, u32[]{:S(2)}, u32[]{:S(2)}) collective-permute-start(bf16[2,128,2048]{2,1,0:T(8,128)(2,1)S(1)} %collective-permute-done.7.refs_5_), channel_id=1, source_target_pairs={{0,2},{1,3},{2,0},{3,1},{4,6},{5,7},{6,4},{7,5},{8,10},{9,11},{10,... | collective-permute-start | bytes 3145736 | tf_op jit(solution)/shard_map/ppermute | solution.py:431
  36.1 18.2 %collective-permute-done.5.refs_3_ = bf16[2,128,2048]{2,1,0:T(8,128)(2,1)S(1)} collective-permute-done((bf16[2,128,2048]{2,1,0:T(8,128)(2,1)S(1)}, bf16[2,128,2048]{2,1,0:T(8,128)(2,1)S(1)}, u32[]{:S(2)}, u32[]{:S(2)}) %collective-permute-start.5) | collective-permute-done | bytes 1048608 | tf_op jit(solution)/shard_map/ppermute | solution.py:431
  54.3 21.1 %collective-permute-done.8.refs_6_ = bf16[2,128,2048]{2,1,0:T(8,128)(2,1)S(1)} collective-permute-done((bf16[2,128,2048]{2,1,0:T(8,128)(2,1)S(1)}, bf16[2,128,2048]{2,1,0:T(8,128)(2,1)S(1)}, u32[]{:S(2)}, u32[]{:S(2)}) %collective-permute-start.8) | collective-permute-done | bytes 1048608 | tf_op jit(solution)/shard_map/ppermute | solution.py:431
  76.9 8.0 %attention_chunk.4 = (bf16[256,4096]{1,0:T(8,128)(2,1)}, bf16[256,4096]{1,0:T(8,128)(2,1)}, bf16[2,256,2048]{2,1,0:T(8,128)(2,1)S(1)}, bf16[2,128,512]{2,1,0:T(8...) custom-call(s32[1]{0:T(128)} %bitcast.me_ref, ...), custom_call_target="tpu_custom_call" | custom-call | flops 16777216 | bytes 8388608 | tf_op jit(solution)/shard_map/attention_chunk/pallas_call | solution.py:342
  87.0 8.0 %attention_chunk.5 = (bf16[256,4096]{1,0:T(8,128)(2,1)}, bf16[256,4096]{1,0:T(8,128)(2,1)}, bf16[2,256,2048]{2,1,0:T(8,128)(2,1)S(1)}, bf16[2,128,512]{2,1,0:T(8...) custom-call(s32[1]{0:T(128)} %bitcast.me_ref, ...), custom_call_target="tpu_custom_call", output_to_operand_aliasing={{0}: (14, {}), {1}: (15, {}), {2}: (16, {})} | custom-call | flops 16777216 | bytes 8388608 | tf_op jit(solution)/shard_map/attention_chunk/pallas_call | solution.py:342
  97.6 1.8 %collective-permute-start.15 = (bf16[2,128,512]{2,1,0:T(8,128)(2,1)S(1)}, bf16[2,128,512]{2,1,0:T(8,128)(2,1)S(1)}, u32[]{:S(2)}, u32[]{:S(2)}) collective-permute-start(bf16[2,128,512]{2,1,0:T(8,128)(2,1)S(1)} %pad_add_fusion.7.refs_14_), channel_id=1, source_target_pairs={{0,2},{1,3},{2,0},{3,1},{4,6},{5,7},{6,4},{7,5},{8,10},{9,11},{10,... | collective-permute-start | bytes 786440 | tf_op jit(solution)/shard_map/ppermute | solution.py:431
  99.4 3.7 %collective-permute-done.14 = bf16[128,512]{1,0:T(8,128)(2,1)S(1)} collective-permute-done((bf16[128,512]{1,0:T(8,128)(2,1)S(1)}, bf16[128,512]{1,0:T(8,128)(2,1)S(1)}, u32[]{:S(2)}, u32[]{:S(2)}) %collective-permute-start.14) | collective-permute-done | bytes 131104 | tf_op jit(solution)/shard_map/ppermute | solution.py:431
  103.6 8.2 %attention_chunk.6 = (bf16[256,4096]{1,0:T(8,128)(2,1)}, bf16[256,4096]{1,0:T(8,128)(2,1)}, bf16[2,256,2048]{2,1,0:T(8,128)(2,1)S(1)}, bf16[2,128,512]{2,1,0:T(8...) custom-call(s32[1]{0:T(128)} %bitcast.me_ref, ...), custom_call_target="tpu_custom_call", output_to_operand_aliasing={{0}: (14, {}), {1}: (15, {}), {2}: (16, {})} | custom-call | flops 16777216 | bytes 8388608 | tf_op jit(solution)/shard_map/attention_chunk/pallas_call | solution.py:342
  112.0 2.0 %collective-permute-start.23 = (bf16[2,128,512]{2,1,0:T(8,128)(2,1)S(1)}, bf16[2,128,512]{2,1,0:T(8,128)(2,1)S(1)}, u32[]{:S(2)}, u32[]{:S(2)}) collective-permute-start(bf16[2,128,512]{2,1,0:T(8,128)(2,1)S(1)} %pad_add_fusion.5.refs_14_), channel_id=1, source_target_pairs={{0,2},{1,3},{2,0},{3,1},{4,6},{5,7},{6,4},{7,5},{8,10},{9,11},{10,... | collective-permute-start | bytes 786440 | tf_op jit(solution)/shard_map/ppermute | solution.py:431
  114.0 2.8 %collective-permute-done.28 = bf16[128,512]{1,0:T(8,128)(2,1)S(1)} collective-permute-done((bf16[128,512]{1,0:T(8,128)(2,1)S(1)}, bf16[128,512]{1,0:T(8,128)(2,1)S(1)}, u32[]{:S(2)}, u32[]{:S(2)}) %collective-permute-start.28) | collective-permute-done | bytes 131104 | tf_op jit(solution)/shard_map/ppermute | solution.py:431
  118.5 3.8 %collective-permute-done.26 = bf16[128,512]{1,0:T(8,128)(2,1)S(1)} collective-permute-done((bf16[128,512]{1,0:T(8,128)(2,1)S(1)}, bf16[128,512]{1,0:T(8,128)(2,1)S(1)}, u32[]{:S(2)}, u32[]{:S(2)}) %collective-permute-start.26) | collective-permute-done | bytes 131104 | tf_op jit(solution)/shard_map/ppermute | solution.py:431
  122.2 1.7 %collective-permute-start.29 = (bf16[2,128,512]{2,1,0:T(8,128)(2,1)S(1)}, bf16[2,128,512]{2,1,0:T(8,128)(2,1)S(1)}, u32[]{:S(2)}, u32[]{:S(2)}) collective-permute-start(bf16[2,128,512]{2,1,0:T(8,128)(2,1)S(1)} %pad_add_fusion), channel_id=1, source_target_pairs={{0,4},{1,5},{2,6},{3,7},{4,0},{5,1},{6,2},{7,3},{8,12},{9,13},{10,... | collective-permute-start | bytes 786440 | tf_op jit(solution)/shard_map/ppermute | solution.py:431
  126.0 8.1 %attention_chunk.7 = (bf16[256,4096]{1,0:T(8,128)(2,1)}, bf16[256,4096]{1,0:T(8,128)(2,1)}, bf16[2,256,2048]{2,1,0:T(8,128)(2,1)S(1)}, bf16[2,128,512]{2,1,0:T(8...) custom-call(s32[1]{0:T(128)} %bitcast.me_ref, ...), custom_call_target="tpu_custom_call", output_to_operand_aliasing={{0}: (14, {}), {1}: (15, {}), {2}: (16, {})} | custom-call | flops 16777216 | bytes 8388608 | tf_op jit(solution)/shard_map/attention_chunk/pallas_call | solution.py:342
  139.4 3.2 %collective-permute-done.19 = bf16[128,512]{1,0:T(8,128)(2,1)S(1)} collective-permute-done((bf16[128,512]{1,0:T(8,128)(2,1)S(1)}, bf16[128,512]{1,0:T(8,128)(2,1)S(1)}, u32[]{:S(2)}, u32[]{:S(2)}) %collective-permute-start.19) | collective-permute-done | bytes 131104 | tf_op jit(solution)/shard_map/ppermute | solution.py:431
  148.7 2.6 %collective-permute-start.37 = (f32[1,128]{1,0:T(1,128)S(1)}, f32[1,128]{1,0:T(1,128)S(1)}, u32[]{:S(2)}, u32[]{:S(2)}) collective-permute-start(f32[1,128]{1,0:T(1,128)S(1)} %add_add_fusion.4), channel_id=1, source_target_pairs={{0,16},{8,24},{16,0},{24,8},{1,17},{9,25},{17,1},{25,9},{2,18},{10... | collective-permute-start | bytes 1544 | tf_op jit(solution)/shard_map/ppermute | solution.py:431
  154.7 1.9 %collective-permute-done.38 = f32[1,128]{1,0:T(1,128)S(1)} collective-permute-done((f32[1,128]{1,0:T(1,128)S(1)}, f32[1,128]{1,0:T(1,128)S(1)}, u32[]{:S(2)}, u32[]{:S(2)}) %collective-permute-start.38) | collective-permute-done | bytes 544 | tf_op jit(solution)/shard_map/ppermute | solution.py:431
  158.6 1.6 %finish.2 = (bf16[128,4096]{1,0:T(8,128)(2,1)}, bf16[256,4096]{1,0:T(8,128)(2,1)}, bf16[256,4096]{1,0:T(8,128)(2,1)}) custom-call(s32[1]{0:T(128)} %bitcast.me_ref, bf16[128,512]{1,0:T(8,128)(2,1)S(1)} %get-tuple-element.99.refs_0_, bf16[128,512]{1,0:T(8,128)(2,1)S(1)} %collective-permute-done.22.refs_1_, ...), custom_call_target="tpu_custom_call", output_to_operand_aliasing={{1}: (8, {}), {2}: (9, {})} | custom-call | bytes 2097152 | tf_op jit(solution)/shard_map/finish/pallas_call | solution.py:415
  (109 shorter events, 36.0 us)
Async XLA Ops:
  3.7 21.8 %collective-permute-start.3 = (bf16[2,128,2048]{2,1,0:T(8,128)(2,1)S(1)}, bf16[2,128,2048]{2,1,0:T(8,128)(2,1)S(1)}, u32[]{:S(2)}, u32[]{:S(2)}) collective-permute-start(bf16[2,128,2048]{2,1,0:T(8,128)(2,1)S(1)} %get-tuple-element.51), channel_id=1, source_target_pairs={{0,1},{1,0},{2,3},{3,2},{4,5},{5,4},{6,7},{7,6},{8,9},{9,8},{10,11... | collective-permute-start | bytes 3145736 | tf_op jit(solution)/shard_map/ppermute | solution.py:431
  4.2 28.7 %collective-permute-start.7 = (bf16[2,128,2048]{2,1,0:T(8,128)(2,1)S(1)}, bf16[2,128,2048]{2,1,0:T(8,128)(2,1)S(1)}, u32[]{:S(2)}, u32[]{:S(2)}) collective-permute-start(bf16[2,128,2048]{2,1,0:T(8,128)(2,1)S(1)} %get-tuple-element.51), channel_id=1, source_target_pairs={{0,5},{1,4},{2,7},{3,6},{4,1},{5,0},{6,3},{7,2},{8,13},{9,12},{10,... | collective-permute-start | bytes 3145736 | tf_op jit(solution)/shard_map/ppermute | solution.py:431
  6.8 26.0 %collective-permute-start.4 = (bf16[2,128,2048]{2,1,0:T(8,128)(2,1)S(1)}, bf16[2,128,2048]{2,1,0:T(8,128)(2,1)S(1)}, u32[]{:S(2)}, u32[]{:S(2)}) collective-permute-start(bf16[2,128,2048]{2,1,0:T(8,128)(2,1)S(1)} %get-tuple-element.48.refs_0_), channel_id=1, source_target_pairs={{0,2},{1,3},{2,0},{3,1},{4,6},{5,7},{6,4},{7,5},{8,10},{9,11},{10,... | collective-permute-start | bytes 3145736 | tf_op jit(solution)/shard_map/ppermute | solution.py:431
  12.0 64.9 %collective-permute-start.10 = (bf16[2,256,2048]{2,1,0:T(8,128)(2,1)S(1)}, bf16[2,256,2048]{2,1,0:T(8,128)(2,1)S(1)}, u32[]{:S(2)}, u32[]{:S(2)}) collective-permute-start(bf16[2,256,2048]{2,1,0:T(8,128)(2,1)S(1)} %get-tuple-element.52), channel_id=1, source_target_pairs={{0,1},{1,0},{2,3},{3,2},{4,5},{5,4},{6,7},{7,6},{8,9},{9,8},{10,11... | collective-permute-start | bytes 6291464 | tf_op jit(solution)/shard_map/ppermute | solution.py:431
  16.6 5.3 %collective-permute-start.2 = (f32[1,128]{1,0:T(1,128)S(1)}, f32[1,128]{1,0:T(1,128)S(1)}, u32[]{:S(2)}, u32[]{:S(2)}) collective-permute-start(f32[1,128]{1,0:T(1,128)S(1)} %get-tuple-element.50), channel_id=1, source_target_pairs={{0,24},{8,16},{16,8},{24,0},{1,25},{9,17},{17,9},{25,1},{2,26},{10... | collective-permute-start | bytes 1544 | tf_op jit(solution)/shard_map/ppermute | solution.py:431
  25.5 28.9 %collective-permute-start.5 = (bf16[2,128,2048]{2,1,0:T(8,128)(2,1)S(1)}, bf16[2,128,2048]{2,1,0:T(8,128)(2,1)S(1)}, u32[]{:S(2)}, u32[]{:S(2)}) collective-permute-start(bf16[2,128,2048]{2,1,0:T(8,128)(2,1)S(1)} %get-tuple-element.51), channel_id=1, source_target_pairs={{0,3},{1,2},{2,1},{3,0},{4,7},{5,6},{6,5},{7,4},{8,11},{9,10},{10,... | collective-permute-start | bytes 3145736 | tf_op jit(solution)/shard_map/ppermute | solution.py:431
  25.5 28.9 %collective-permute-start.6 = (bf16[2,128,2048]{2,1,0:T(8,128)(2,1)S(1)}, bf16[2,128,2048]{2,1,0:T(8,128)(2,1)S(1)}, u32[]{:S(2)}, u32[]{:S(2)}) collective-permute-start(bf16[2,128,2048]{2,1,0:T(8,128)(2,1)S(1)} %get-tuple-element.48.refs_0_), channel_id=1, source_target_pairs={{0,4},{1,5},{2,6},{3,7},{4,0},{5,1},{6,2},{7,3},{8,12},{9,13},{10,... | collective-permute-start | bytes 3145736 | tf_op jit(solution)/shard_map/ppermute | solution.py:431
  32.8 42.6 %collective-permute-start.8 = (bf16[2,128,2048]{2,1,0:T(8,128)(2,1)S(1)}, bf16[2,128,2048]{2,1,0:T(8,128)(2,1)S(1)}, u32[]{:S(2)}, u32[]{:S(2)}) collective-permute-start(bf16[2,128,2048]{2,1,0:T(8,128)(2,1)S(1)} %collective-permute-done.4.refs_2_), channel_id=1, source_target_pairs={{0,4},{1,5},{2,6},{3,7},{4,0},{5,1},{6,2},{7,3},{8,12},{9,13},{10,... | collective-permute-start | bytes 3145736 | tf_op jit(solution)/shard_map/ppermute | solution.py:431
  32.8 44.0 %collective-permute-start.9 = (bf16[2,128,2048]{2,1,0:T(8,128)(2,1)S(1)}, bf16[2,128,2048]{2,1,0:T(8,128)(2,1)S(1)}, u32[]{:S(2)}, u32[]{:S(2)}) collective-permute-start(bf16[2,128,2048]{2,1,0:T(8,128)(2,1)S(1)} %collective-permute-done.7.refs_5_), channel_id=1, source_target_pairs={{0,2},{1,3},{2,0},{3,1},{4,6},{5,7},{6,4},{7,5},{8,10},{9,11},{10,... | collective-permute-start | bytes 3145736 | tf_op jit(solution)/shard_map/ppermute | solution.py:431
  84.9 12.2 %collective-permute-start.12 = (bf16[128,512]{1,0:T(8,128)(2,1)S(1)}, bf16[128,512]{1,0:T(8,128)(2,1)S(1)}, u32[]{:S(2)}, u32[]{:S(2)}) collective-permute-start(bf16[128,512]{1,0:T(8,128)(2,1)S(1)} %get-tuple-element.62), channel_id=1, source_target_pairs={{0,2},{1,3},{2,0},{3,1},{4,6},{5,7},{6,4},{7,5},{8,10},{9,11},{10,... | collective-permute-start | bytes 393224 | tf_op jit(solution)/shard_map/ppermute | solution.py:431
  86.5 11.1 %collective-permute-start.11 = (bf16[128,512]{1,0:T(8,128)(2,1)S(1)}, bf16[128,512]{1,0:T(8,128)(2,1)S(1)}, u32[]{:S(2)}, u32[]{:S(2)}) collective-permute-start(bf16[128,512]{1,0:T(8,128)(2,1)S(1)} %get-tuple-element.60), channel_id=1, source_target_pairs={{0,4},{1,5},{2,6},{3,7},{4,0},{5,1},{6,2},{7,3},{8,12},{9,13},{10,... | collective-permute-start | bytes 393224 | tf_op jit(solution)/shard_map/ppermute | solution.py:431
  95.0 16.9 %collective-permute-start.13 = (bf16[128,512]{1,0:T(8,128)(2,1)S(1)}, bf16[128,512]{1,0:T(8,128)(2,1)S(1)}, u32[]{:S(2)}, u32[]{:S(2)}) collective-permute-start(bf16[128,512]{1,0:T(8,128)(2,1)S(1)} %get-tuple-element.67), channel_id=1, source_target_pairs={{0,4},{1,5},{2,6},{3,7},{4,0},{5,1},{6,2},{7,3},{8,12},{9,13},{10,... | collective-permute-start | bytes 393224 | tf_op jit(solution)/shard_map/ppermute | solution.py:431
  96.6 6.4 %collective-permute-start.14 = (bf16[128,512]{1,0:T(8,128)(2,1)S(1)}, bf16[128,512]{1,0:T(8,128)(2,1)S(1)}, u32[]{:S(2)}, u32[]{:S(2)}) collective-permute-start(bf16[128,512]{1,0:T(8,128)(2,1)S(1)} %get-tuple-element.69), channel_id=1, source_target_pairs={{0,2},{1,3},{2,0},{3,1},{4,6},{5,7},{6,4},{7,5},{8,10},{9,11},{10,... | collective-permute-start | bytes 393224 | tf_op jit(solution)/shard_map/ppermute | solution.py:431
  97.2 26.8 %collective-permute-start.16 = (bf16[2,128,512]{2,1,0:T(8,128)(2,1)S(1)}, bf16[2,128,512]{2,1,0:T(8,128)(2,1)S(1)}, u32[]{:S(2)}, u32[]{:S(2)}) collective-permute-start(bf16[2,128,512]{2,1,0:T(8,128)(2,1)S(1)} %pad_add_fusion.6.refs_15_), channel_id=1, source_target_pairs={{0,4},{1,5},{2,6},{3,7},{4,0},{5,1},{6,2},{7,3},{8,12},{9,13},{10,... | collective-permute-start | bytes 786440 | tf_op jit(solution)/shard_map/ppermute | solution.py:431
  97.6 27.0 %collective-permute-start.15 = (bf16[2,128,512]{2,1,0:T(8,128)(2,1)S(1)}, bf16[2,128,512]{2,1,0:T(8,128)(2,1)S(1)}, u32[]{:S(2)}, u32[]{:S(2)}) collective-permute-start(bf16[2,128,512]{2,1,0:T(8,128)(2,1)S(1)} %pad_add_fusion.7.refs_14_), channel_id=1, source_target_pairs={{0,2},{1,3},{2,0},{3,1},{4,6},{5,7},{6,4},{7,5},{8,10},{9,11},{10,... | collective-permute-start | bytes 786440 | tf_op jit(solution)/shard_map/ppermute | solution.py:431
  103.1 21.6 %collective-permute-start.24 = (bf16[2,128,512]{2,1,0:T(8,128)(2,1)S(1)}, bf16[2,128,512]{2,1,0:T(8,128)(2,1)S(1)}, u32[]{:S(2)}, u32[]{:S(2)}) collective-permute-start(bf16[2,128,512]{2,1,0:T(8,128)(2,1)S(1)} %pad_add_fusion.4.refs_15_), channel_id=1, source_target_pairs={{0,4},{1,5},{2,6},{3,7},{4,0},{5,1},{6,2},{7,3},{8,12},{9,13},{10,... | collective-permute-start | bytes 786440 | tf_op jit(solution)/shard_map/ppermute | solution.py:431
  112.0 12.7 %collective-permute-start.23 = (bf16[2,128,512]{2,1,0:T(8,128)(2,1)S(1)}, bf16[2,128,512]{2,1,0:T(8,128)(2,1)S(1)}, u32[]{:S(2)}, u32[]{:S(2)}) collective-permute-start(bf16[2,128,512]{2,1,0:T(8,128)(2,1)S(1)} %pad_add_fusion.5.refs_14_), channel_id=1, source_target_pairs={{0,2},{1,3},{2,0},{3,1},{4,6},{5,7},{6,4},{7,5},{8,10},{9,11},{10,... | collective-permute-start | bytes 786440 | tf_op jit(solution)/shard_map/ppermute | solution.py:431
  116.8 5.4 %collective-permute-start.26 = (bf16[128,512]{1,0:T(8,128)(2,1)S(1)}, bf16[128,512]{1,0:T(8,128)(2,1)S(1)}, u32[]{:S(2)}, u32[]{:S(2)}) collective-permute-start(bf16[128,512]{1,0:T(8,128)(2,1)S(1)} %get-tuple-element.79), channel_id=1, source_target_pairs={{0,4},{1,5},{2,6},{3,7},{4,0},{5,1},{6,2},{7,3},{8,12},{9,13},{10,... | collective-permute-start | bytes 393224 | tf_op jit(solution)/shard_map/ppermute | solution.py:431
  122.2 26.4 %collective-permute-start.29 = (bf16[2,128,512]{2,1,0:T(8,128)(2,1)S(1)}, bf16[2,128,512]{2,1,0:T(8,128)(2,1)S(1)}, u32[]{:S(2)}, u32[]{:S(2)}) collective-permute-start(bf16[2,128,512]{2,1,0:T(8,128)(2,1)S(1)} %pad_add_fusion), channel_id=1, source_target_pairs={{0,4},{1,5},{2,6},{3,7},{4,0},{5,1},{6,2},{7,3},{8,12},{9,13},{10,... | collective-permute-start | bytes 786440 | tf_op jit(solution)/shard_map/ppermute | solution.py:431
  124.0 27.2 %collective-permute-start.27 = (bf16[2,128,512]{2,1,0:T(8,128)(2,1)S(1)}, bf16[2,128,512]{2,1,0:T(8,128)(2,1)S(1)}, u32[]{:S(2)}, u32[]{:S(2)}) collective-permute-start(bf16[2,128,512]{2,1,0:T(8,128)(2,1)S(1)} %pad_add_fusion.1), channel_id=1, source_target_pairs={{0,2},{1,3},{2,0},{3,1},{4,6},{5,7},{6,4},{7,5},{8,10},{9,11},{10,... | collective-permute-start | bytes 786440 | tf_op jit(solution)/shard_map/ppermute | solution.py:431
  139.4 19.1 %collective-permute-start.31 = (bf16[2,256,2048]{2,1,0:T(8,128)(2,1)S(1)}, bf16[2,256,2048]{2,1,0:T(8,128)(2,1)S(1)}, u32[]{:S(2)}, u32[]{:S(2)}) collective-permute-start(bf16[2,256,2048]{2,1,0:T(8,128)(2,1)S(1)} %get-tuple-element.82), channel_id=1, source_target_pairs={{0,1},{1,0},{2,3},{3,2},{4,5},{5,4},{6,7},{7,6},{8,9},{9,8},{10,11... | collective-permute-start | bytes 6291464 | tf_op jit(solution)/shard_map/ppermute | solution.py:431
  144.1 13.0 %collective-permute-start.20 = (bf16[2,128,512]{2,1,0:T(8,128)(2,1)S(1)}, bf16[2,128,512]{2,1,0:T(8,128)(2,1)S(1)}, u32[]{:S(2)}, u32[]{:S(2)}) collective-permute-start(bf16[2,128,512]{2,1,0:T(8,128)(2,1)S(1)} %pad_add_fusion.2), channel_id=1, source_target_pairs={{0,4},{1,5},{2,6},{3,7},{4,0},{5,1},{6,2},{7,3},{8,12},{9,13},{10,... | collective-permute-start | bytes 786440 | tf_op jit(solution)/shard_map/ppermute | solution.py:431
  147.1 10.1 %collective-permute-start.18 = (bf16[2,128,512]{2,1,0:T(8,128)(2,1)S(1)}, bf16[2,128,512]{2,1,0:T(8,128)(2,1)S(1)}, u32[]{:S(2)}, u32[]{:S(2)}) collective-permute-start(bf16[2,128,512]{2,1,0:T(8,128)(2,1)S(1)} %pad_add_fusion.3), channel_id=1, source_target_pairs={{0,2},{1,3},{2,0},{3,1},{4,6},{5,7},{6,4},{7,5},{8,10},{9,11},{10,... | collective-permute-start | bytes 786440 | tf_op jit(solution)/shard_map/ppermute | solution.py:431
  151.3 5.3 %collective-permute-start.38 = (f32[1,128]{1,0:T(1,128)S(1)}, f32[1,128]{1,0:T(1,128)S(1)}, u32[]{:S(2)}, u32[]{:S(2)}) collective-permute-start(f32[1,128]{1,0:T(1,128)S(1)} %add_add_fusion.4), channel_id=1, source_target_pairs={{0,24},{8,16},{16,8},{24,0},{1,25},{9,17},{17,9},{25,1},{2,26},{10... | collective-permute-start | bytes 1544 | tf_op jit(solution)/shard_map/ppermute | solution.py:431
  (25 other events, 116.4 us)

commit v2 on v1

--- a/solution.py
+++ b/solution.py
@@ -1,4 +1,6 @@
 import functools
+import itertools
+import math
 
 import jax
 import jax.numpy as jnp
@@ -11,8 +13,8 @@
 PAIR = 2 * HEAD_DIM
 EX_DEV = 2
 GROUPS = 16
-CHUNKS = 4
-UNROLL = 2
+CHUNKS = (1, 1)
+LOCKSTEP = 4
 ALONE = pltpu.CompilerParams(vmem_limit_bytes=60 * 1024 * 1024)
 ROOM = pltpu.CompilerParams(vmem_limit_bytes=16 * 1024 * 1024)
 FIELDS = 8
@@ -92,7 +94,7 @@
         out[tensor].wait()
 
 
-def tabulate(me, lengths, targets, enc_pack, dec_pack, task, keys, values, waits):
+def tabulate(me, lengths, targets, enc_pack, dec_pack, task, keys, values):
     rows, features = keys.shape
     half = features // 2
     return pl.pallas_call(
@@ -102,13 +104,13 @@
             jax.ShapeDtypeStruct((4, FIELDS), jnp.int32),
             jax.ShapeDtypeStruct((1, 128), jnp.float32),
         ],
-        in_specs=[SMEM] * 6 + [HBM] * 2 + [ANY] * len(waits),
+        in_specs=[SMEM] * 6 + [HBM] * 2,
         out_specs=[ANY, SMEM, VMEM],
         scratch_shapes=[pltpu.VMEM((2, rows, half), keys.dtype), pltpu.SemaphoreType.DMA((4,))],
         compiler_params=ROOM,
         cost_estimate=SMALL,
         name="tabulate",
-    )(me, lengths, targets, enc_pack, dec_pack, task, keys, values, *waits)
+    )(me, lengths, targets, enc_pack, dec_pack, task, keys, values)
 
 
 def split_kernel(me_ref, q_ref, c_ref, own_ref, other_ref, held, sem):
@@ -159,17 +161,17 @@
 
 
 def attention_kernel(
-    me_ref, table_ref, scale_ref, *refs, packs, first, waits, half, at
+    me_ref, table_ref, scale_ref, *refs, packs, first, bases, half, at
 ):
     places = layout(packs)
     sources = len(places)
     pieces = refs[:packs]
     k_ref, v_ref, sibling_ref = refs[packs : packs + 3]
-    outs = refs[packs + 3 + (0 if first else 3) + waits :]
+    outs = refs[packs + 3 + (0 if first else 3) :]
     k_out, v_out, sibling_out = outs[:3]
     query_outs = outs[3 : 3 + sources]
     loss_out = outs[3 + sources]
-    kv, qc, dq, dkv, loss, bias, scaling, in_sem, qc_sem, out_sem, dkv_sem = outs[sources + 4 :]
+    kv, qc, dq, dkv, loss, scaling, in_sem, qc_sem, out_sem, dkv_sem = outs[sources + 4 :]
     width = qc.shape[-1]
     rows = qc.shape[2]
     keys = kv.shape[2]
@@ -209,9 +211,11 @@
             for distance, piece in enumerate(pieces):
 
                 @pl.when(owner == distance)
-                def _(piece=piece, item=item):
+                def _(piece=piece, item=item, distance=distance):
                     pltpu.make_async_copy(
-                        piece.at[:, :, half_columns], qc.at[item], qc_sem.at[item]
+                        piece.at[:, :, pl.ds(at - bases[distance], width)],
+                        qc.at[item],
+                        qc_sem.at[item],
                     ).start()
 
     dq[...] = jnp.zeros_like(dq)
@@ -220,7 +224,8 @@
     low = lane < HEAD_DIM
     row = lax.broadcasted_iota(jnp.int32, (rows, PAIR), 0)
     row_lane = lax.broadcasted_iota(jnp.int32, (1, rows), 1)
-    key = lax.broadcasted_iota(jnp.int32, (keys, rows), 0)
+    key = lax.broadcasted_iota(jnp.int32, (keys, 1), 0)
+    key_lane = lax.broadcasted_iota(jnp.int32, (1, keys), 1)
 
     def dot(left, right):
         return jnp.dot(left, right, preferred_element_type=jnp.float32)
@@ -235,79 +240,150 @@
                 pieces[0].at[:, :, half_columns], qc.at[item], qc_sem.at[item]
             ).wait()
         owner, scale_rows = [], []
+        border = table_ref[2 * side, 4]
         for place in range(2):
             item = 2 * side + place
             start, length = table_ref[item, 1], table_ref[item, 2]
-            key_start, key_length = table_ref[item, 3], table_ref[item, 4]
             scale = scale_ref[0, table_ref[item, 5]]
-            span = slice(place * rows, (place + 1) * rows)
-            bias[:, span] = jnp.where(
-                (key >= key_start) & (key < key_start + key_length), 0.0, -1e30
-            )
-            scaling[span] = jnp.where((row >= start) & (row < start + length), scale, 0.0)
+            scaling[place] = jnp.where((row >= start) & (row < start + length), scale, 0.0)
             scale_rows.append(
                 jnp.where((row_lane >= start) & (row_lane < start + length), scale, 0.0)
             )
             owner.append(table_ref[item, 0])
-        scale_row = jnp.concatenate(scale_rows, axis=1)
-
-        def pair_step(pair, carry, side=side, owner=owner, scale_row=scale_row):
+
+        def pair_chain(pair, side=side, owner=owner, scale_rows=scale_rows, border=border):
             columns = pl.ds(pl.multiple_of(pair * PAIR, PAIR), PAIR)
+            early, early_lane = key < border, key_lane < border
             key_pair = kv[side, 0, :, columns]
             value_pair = kv[side, 1, :, columns]
-            query = jnp.concatenate([qc[2 * side + place, 0, :, columns] for place in range(2)], axis=0)
-            cot = jnp.concatenate([qc[2 * side + place, 1, :, columns] for place in range(2)], axis=0)
             zero = jnp.zeros_like(key_pair)
-
-            def heads(array):
+            blank = jnp.zeros((HEAD_DIM, rows), key_pair.dtype)
+
+            def by_example(array):
                 return jnp.concatenate(
-                    [jnp.where(low, array, zero), jnp.where(low, zero, array)], axis=0
+                    [jnp.where(early, array, zero), jnp.where(early, zero, array)], axis=1
                 )
 
-            up = (cot.astype(jnp.float32) * scaling[...]).astype(jnp.bfloat16)
-            query_turned, key_turned, value_turned = query.T, key_pair.T, value_pair.T
-            cot_turned = cot.T.astype(jnp.float32)
-            up_turned = (cot_turned * scale_row).astype(jnp.bfloat16)
-            both_scores = dot(heads(key_pair), query_turned)
-            both_slopes = dot(heads(value_pair), up_turned)
-            query_parts, weights_parts, grad_parts = [], [], []
+            def by_head(array):
+                nothing = jnp.zeros_like(array)
+                return jnp.concatenate(
+                    [jnp.where(low, array, nothing), jnp.where(low, nothing, array)], axis=0
+                )
+
+            def spread(turned):
+                blocks = []
+                for array in turned:
+                    blocks.append(jnp.concatenate([array[:HEAD_DIM], blank], axis=1))
+                    blocks.append(jnp.concatenate([blank, array[HEAD_DIM:]], axis=1))
+                return jnp.concatenate(blocks, axis=0)
+
+            def example_parts(turned, part):
+                array = turned[part]
+                nothing = jnp.zeros_like(array)
+                return jnp.concatenate(
+                    [jnp.where(early_lane, array, nothing), jnp.where(early_lane, nothing, array)],
+                    axis=0,
+                )
+
+            queries = [qc[2 * side + place, 0, :, columns] for place in range(2)]
+            cots = [qc[2 * side + place, 1, :, columns] for place in range(2)]
+            yield
+            ups = [
+                (cots[place].astype(jnp.float32) * scaling[place]).astype(jnp.bfloat16)
+                for place in range(2)
+            ]
+            key_turned, value_turned = key_pair.T, value_pair.T
+            cots_turned = [cot.T.astype(jnp.float32) for cot in cots]
+            ups_turned = [
+                (cots_turned[place] * scale_rows[place]).astype(jnp.bfloat16) for place in range(2)
+            ]
+            queries_turned = [query.T for query in queries]
+            yield
+            scores = dot(by_example(key_pair), spread(queries_turned))
+            slopes = dot(by_example(value_pair), spread(ups_turned))
+            yield
+            lowest = jnp.float32(-3e38)
+            highest = [
+                jnp.max(jnp.where(early, scores, lowest), axis=0, keepdims=True),
+                jnp.max(jnp.where(early, lowest, scores), axis=0, keepdims=True),
+            ]
+            yield
+            powers = jnp.exp(scores - jnp.where(early, highest[0], highest[1]))
+            inverse = [
+                1.0 / jnp.sum(jnp.where(early, powers, 0.0), axis=0, keepdims=True),
+                1.0 / jnp.sum(jnp.where(early, 0.0, powers), axis=0, keepdims=True),
+            ]
+            yield
+            weights = powers * jnp.where(early, inverse[0], inverse[1])
+            weights_low = weights.astype(jnp.bfloat16)
+            yield
+            drifts = [[], []]
+            losses = []
             for head in range(2):
-                spread = slice(head * keys, (head + 1) * keys)
                 part = slice(head * HEAD_DIM, (head + 1) * HEAD_DIM)
-                scores = both_scores[spread] + bias[...]
-                highest = jnp.max(scores, axis=0, keepdims=True)
-                powers = jnp.exp(scores - highest)
-                weights = powers * (1.0 / jnp.sum(powers, axis=0, keepdims=True))
-                weights_low = weights.astype(jnp.bfloat16)
-                attended = dot(value_turned[part], weights_low)
+                lanes = slice(head * rows, (head + 1) * rows)
+                attended = dot(example_parts(value_turned, part), weights_low[:, lanes])
                 attended = attended.astype(jnp.bfloat16).astype(jnp.float32)
-                token = cot_turned[part] * attended
-                loss[side] += jnp.sum(token.reshape(HEAD_DIM // 8, 8, 2 * rows), axis=0)
-                drift = jnp.sum(
-                    up_turned[part].astype(jnp.float32) * attended, axis=0, keepdims=True
-                )
-                grad = (weights * (both_slopes[spread] - drift)).astype(jnp.bfloat16)
-                query_parts.append(dot(key_turned[part], grad))
-                grad_parts.append(grad)
-                weights_parts.append(weights_low)
-            query_grad = jnp.concatenate(query_parts, axis=0).astype(jnp.bfloat16).T
+                for place in range(2):
+                    item = 2 * side + place
+                    here = attended[place * HEAD_DIM : (place + 1) * HEAD_DIM]
+                    token = cots_turned[place][part] * here
+                    losses.append(
+                        (item, jnp.sum(token.reshape(HEAD_DIM // 8, 8, rows), axis=0))
+                    )
+                    drifts[place].append(
+                        jnp.sum(
+                            ups_turned[place][part].astype(jnp.float32) * here,
+                            axis=0,
+                            keepdims=True,
+                        )
+                    )
+            yield
+            drift = [jnp.concatenate(parts, axis=1) for parts in drifts]
+            grad = weights * (slopes - jnp.where(early, drift[0], drift[1]))
+            grad = grad.astype(jnp.bfloat16)
+            yield
+            query_parts = [[], []]
+            for head in range(2):
+                part = slice(head * HEAD_DIM, (head + 1) * HEAD_DIM)
+                lanes = slice(head * rows, (head + 1) * rows)
+                found = dot(example_parts(key_turned, part), grad[:, lanes])
+                for place in range(2):
+                    query_parts[place].append(found[place * HEAD_DIM : (place + 1) * HEAD_DIM])
+            key_grad = dot(grad, jnp.concatenate([by_head(query) for query in queries], axis=1))
+            value_grad = dot(weights_low, jnp.concatenate([by_head(up) for up in ups], axis=1))
+            yield
+            query_grads = [
+                jnp.concatenate(query_parts[place], axis=0).astype(jnp.bfloat16).T
+                for place in range(2)
+            ]
+            pair_grads = [
+                jnp.where(early, found[:, :PAIR], found[:, PAIR:]).astype(jnp.bfloat16)
+                for found in (key_grad, value_grad)
+            ]
+            yield
             for place in range(2):
                 at = owner[place]
-                span = slice(place * rows, (place + 1) * rows)
-                dq[at, :, columns] = dq[at, :, columns] + query_grad[span]
-            key_grad = dot(jnp.concatenate(grad_parts, axis=1), heads(query))
-            value_grad = dot(jnp.concatenate(weights_parts, axis=1), heads(up))
-            dkv[side, 0, :, columns] = key_grad.astype(jnp.bfloat16)
-            dkv[side, 1, :, columns] = value_grad.astype(jnp.bfloat16)
+                dq[at, :, columns] = dq[at, :, columns] + query_grads[place]
+            for tensor in range(2):
+                dkv[side, tensor, :, columns] = pair_grads[tensor]
+            for item, part in losses:
+                loss[item] += part
+
+        def group_step(group, carry, pair_chain=pair_chain):
+            chains = [pair_chain(group * lockstep + i) for i in range(lockstep)]
+            for _ in itertools.zip_longest(*chains):
+                pass
             return carry
 
-        lax.fori_loop(0, width // PAIR, pair_step, 0, unroll=UNROLL)
+        lockstep = math.gcd(LOCKSTEP, width // PAIR)
+        lax.fori_loop(0, width // PAIR // lockstep, group_step, 0)
         for copy in dkv_copies[side]:
             copy.start()
         for place in range(2):
             item = 2 * side + place
             start, length = table_ref[item, 1], table_ref[item, 2]
-            part = jnp.sum(loss[side][:, place * rows : (place + 1) * rows], axis=0, keepdims=True)
+            part = jnp.sum(loss[item], axis=0, keepdims=True)
             part = jnp.where((row_lane >= start) & (row_lane < start + length), part, 0.0)
             amount = jnp.sum(part, axis=1, keepdims=True)
             vector = vector + jnp.where(lane == table_ref[item, 5], amount, 0.0)
@@ -329,7 +405,7 @@
 
 
 def attention_chunk(
-    me, table, scales, pieces, keys, values, sibling, full, waits, packs, at, width
+    me, table, scales, pieces, keys, values, sibling, full, packs, bases, at, width
 ):
     sources = len(layout(packs))
     rows = pieces[0].shape[1]
@@ -344,7 +420,7 @@
             attention_kernel,
             packs=packs,
             first=first,
-            waits=len(waits),
+            bases=bases,
             half=half,
             at=at,
         ),
@@ -358,28 +434,29 @@
             for _, count in layout(packs)
         ]
         + [jax.ShapeDtypeStruct((1, 128), jnp.float32)],
-        in_specs=[SMEM] * 3 + [ANY] * packs + [HBM] * 2 + [ANY] + [HBM] * (0 if first else 3) + [ANY] * len(waits),
+        in_specs=[SMEM] * 3 + [ANY] * packs + [HBM] * 2 + [ANY] + [HBM] * (0 if first else 3),
         out_specs=[HBM] * 3 + [ANY] * sources + [VMEM],
         scratch_shapes=[
             pltpu.VMEM((2, 2, key_rows, width), low),
             pltpu.VMEM((4, 2, rows, width), low),
             pltpu.VMEM((packs, rows, width), low),
             pltpu.VMEM((2, 2, key_rows, width), low),
-            pltpu.VMEM((2, 8, 2 * rows), jnp.float32),
-            pltpu.VMEM((key_rows, 2 * rows), jnp.float32),
-            pltpu.VMEM((2 * rows, PAIR), jnp.float32),
+            pltpu.VMEM((4, 8, rows), jnp.float32),
+            pltpu.VMEM((2, rows, PAIR), jnp.float32),
             pltpu.SemaphoreType.DMA((2, 2)),
             pltpu.SemaphoreType.DMA((4,)),
             pltpu.SemaphoreType.DMA((sources,)),
             pltpu.SemaphoreType.DMA((2, 2)),
         ],
         input_output_aliases={} if first else {before + i: i for i in range(3)},
-        compiler_params=ROOM,
+        compiler_params=pltpu.CompilerParams(
+            vmem_limit_bytes=14 * 1024 * 1024 + 2 * packs * rows * width
+        ),
         cost_estimate=pl.CostEstimate(
             flops=flops, bytes_accessed=8 * 1024 * 1024, transcendentals=0
         ),
         name="attention_chunk",
-    )(me, table, scales, *pieces, keys, values, sibling, *(() if first else full), *waits)
+    )(me, table, scales, *pieces, keys, values, sibling, *(() if first else full))
 
 
 def finish_kernel(me_ref, *refs, spots, half, with_keys):
@@ -431,23 +508,15 @@
     return lax.ppermute(array, axis_name, [(i, i ^ bits) for i in range(size)])
 
 
-def after(vector, arrays):
-    for array in arrays:
-        vector = vector + 0.0 * array[0, 0, 0].astype(jnp.float32)
-    return vector
-
-
-def group_sum(array, axis_name, size):
-    step = 1
-    while step < size:
-        if 4 * step <= size:
-            first, second, third = (swap(array, axis_name, size, step * i) for i in (1, 2, 3))
-            array = (array + first) + (second + third)
-            step *= 4
-        else:
-            array = array + swap(array, axis_name, size, step)
-            step *= 2
+def doubled_sum(array, axis_name, size, first=1, last=None):
+    step = first
+    while step < (last or size):
+        array = array + swap(array, axis_name, size, step)
+        step *= 2
     return array
+
+
+together = lax.optimization_barrier
 
 
 def local(
@@ -474,63 +543,117 @@
     def swapped(array, bits):
         return swap(array, "pack", packs, bits)
 
+    def tabulated(me):
+        return tabulate(
+            me,
+            input_lengths,
+            target_lengths,
+            enc_pack,
+            dec_pack,
+            task_group[:, :, 0],
+            enc_keys,
+            enc_values,
+        )
+
+    def scales_of(group_counts):
+        counts = doubled_sum(group_counts, "dp", groups)
+        weights = dro_weights.astype(jnp.float32)
+        weights = jnp.pad(weights, (0, 128 - GROUPS)).reshape(1, 128)
+        return counts, weights / jnp.sum(weights) * (total_tokens / counts)
+
+    widths = [half * share // sum(CHUNKS) for share in CHUNKS]
+    starts = [sum(widths[:i]) for i in range(len(widths))]
+    spots = list(zip(starts, widths))
     own, other = split(me, dec_queries, cotangent)
-    pieces = [own]
-    for bits in range(1, 6 if relayed else packs):
-        pieces.append(swapped(other if bits & 1 else own, bits))
-    if relayed:
-        pieces += [swapped(pieces[2], 4), swapped(pieces[5], 2)]
-    kv_other, table, group_counts = tabulate(
-        me,
-        input_lengths,
-        target_lengths,
-        enc_pack,
-        dec_pack,
-        task_group[:, :, 0],
-        enc_keys,
-        enc_values,
-        [own],
-    )
-    kv_sibling = swapped(kv_other, 1)
-    counts = group_sum(group_counts, "dp", groups)
-    weights = dro_weights.astype(jnp.float32)
-    weights = jnp.pad(weights, (0, 128 - GROUPS)).reshape(1, 128)
-    scales = weights / jnp.sum(weights) * (total_tokens / counts)
-
-    full, losses, query_parts, spots = None, [], [], []
-    halfway, whole = [], []
-    width = half // CHUNKS
-    for chunk in range(CHUNKS):
-        at = chunk * width
-        order = sum(halfway[:-1][-1:], []) + whole[:-2][-1:]
-        *result, loss = attention_chunk(
-            me, table, scales, pieces, enc_keys, enc_values, kv_sibling, full,
-            order, packs, at, width,
+    if not relayed:
+        pieces = [own] + [swapped(other if i & 1 else own, i) for i in range(1, packs)]
+        kv_other, table, group_counts = tabulated(me)
+        kv_sibling = swapped(kv_other, 1)
+        counts, scales = scales_of(group_counts)
+        full, losses, query_parts = None, [], []
+        for at, width in spots:
+            *result, loss = attention_chunk(
+                me, table, scales, pieces, enc_keys, enc_values, kv_sibling, full,
+                packs, [0] * packs, at, width,
+            )
+            full, parts = result[:3], result[3:]
+            losses.append(loss)
+            summed = parts[0]
+            for chip in range(1, len(parts)):
+                summed = summed + swapped(parts[chip], 2 * chip)
+            query_parts += [summed[0], swapped(summed[1], 1)]
+        back = swapped(full[2], 1)
+        loss = doubled_sum(functools.reduce(jnp.add, losses), "pack", packs)
+        loss = doubled_sum(loss, "dp", groups)
+    else:
+        first = widths[0]
+        x_own, y_own = swapped(own, 2), swapped(own, 4)
+        x_other, y_other = swapped(other, 3), swapped(other, 5)
+        sibling = swapped(other, 1)
+        me_later, x_own = together((me, x_own))
+        kv_other, table, group_counts = tabulated(me_later)
+        near = [x_own[:, :, :first], x_own[:, :, first:]]
+        x_own, y_own, x_other, y_other, sibling, kv_other, group_counts, table, near = together(
+            (x_own, y_own, x_other, y_other, sibling, kv_other, group_counts, table, near)
         )
-        full, parts = result[:3], result[3:]
-        losses.append(loss)
-        if relayed:
-            far = swapped(parts.pop(), 4)
-            near = swapped(parts.pop(), 2)
-            parts[2] = parts[2] + jnp.stack([near, jnp.zeros_like(near)])
-            parts[1] = parts[1] + jnp.stack([jnp.zeros_like(far), far])
-            halfway.append(parts[1:])
-        summed = parts[0]
-        for chip in range(1, len(parts)):
-            summed = summed + swapped(parts[chip], 2 * chip)
-        whole.append(summed)
-        query_parts += [summed[0], swapped(summed[1], 1)]
-        spots.append((at, width))
-    back = swapped(full[2], 1)
+        far = [y_other[:, :, :first], y_other[:, :, first:]]
+        diagonal = [swapped(near[0], 4), swapped(far[0], 2)]
+        kv_sibling = swapped(kv_other, 1)
+        counts, scales = scales_of(group_counts)
+        diagonal, near, far, kv_sibling, scales = together(
+            (diagonal, near, far, kv_sibling, scales)
+        )
+        later = [swapped(near[1], 4), swapped(far[1], 2)]
+
+        def attend(full, chunk, diagonal, base):
+            at, width = spots[chunk]
+            pieces = [own, sibling, x_own, x_other, y_own, y_other, *diagonal]
+            *result, loss = attention_chunk(
+                me, table, scales, pieces, enc_keys, enc_values, kv_sibling, full,
+                packs, [0] * 6 + [base] * 2, at, width,
+            )
+            return result[:3], result[3:], loss
+
+        def forwarded(parts):
+            return [swapped(parts[3], 2), swapped(parts[4], 4)]
+
+        def merged(parts, relay):
+            via_x, via_y = relay
+            to_y = parts[2] + jnp.stack([via_x, jnp.zeros_like(via_x)])
+            to_x = parts[1] + jnp.stack([jnp.zeros_like(via_y), via_y])
+            return [swapped(to_x, 2), swapped(to_y, 4)]
+
+        def total(parts, arrived):
+            return parts[0] + arrived[0] + arrived[1]
+
+        full, parts_a, loss_a = attend(None, 0, diagonal, 0)
+        later, full, parts_a = together((later, full, parts_a))
+
+        relay_a = forwarded(parts_a)
+        full, parts_b, loss_b = attend(full, 1, later, first)
+        relay_a, full, parts_b = together((relay_a, full, parts_b))
+
+        arrived_a = merged(parts_a, relay_a)
+        relay_b = forwarded(parts_b)
+        loss = doubled_sum(doubled_sum(loss_a + loss_b, "dp", groups), "pack", packs, 1, 2)
+        arrived_a, relay_b, loss = together((arrived_a, relay_b, loss))
+
+        arrived_b = merged(parts_b, relay_b)
+        total_a = total(parts_a, arrived_a)
+        query_parts = [total_a[0], swapped(total_a[1], 1)]
+        back = swapped(full[2], 1)
+        arrived_b, query_parts, back = together((arrived_b, query_parts, back))
+
+        total_b = total(parts_b, arrived_b)
+        query_parts += [total_b[0], swapped(total_b[1], 1)]
+        loss = doubled_sum(loss, "pack", packs, 2)
+
     queries_gradient, keys_gradient, values_gradient = finish(
         me, query_parts[:-2], spots[:-1], dec_queries, back, full[:2]
     )
     (queries_gradient,) = finish(
         me, query_parts[-2:], spots[-1:], dec_queries, None, (queries_gradient,)
     )
-    loss = functools.reduce(jnp.add, losses)
-    loss = group_sum(after(loss, whole[-3:-2]), "pack", packs)
-    loss = group_sum(after(loss, parts[1:]), "dp", groups)
     group_loss = (loss / counts)[0, :GROUPS]
     return (queries_gradient, keys_gradient, values_gradient, group_loss)
 

time: 161 us -> 138 us (0.86)
  Pallas kernels: 37.2 us -> 24.2 us
  starting transfers between devices: 39.7 us -> 27.1 us
  waiting for transfers between devices: 73.3 us -> 78.8 us
  between operations: 3.05 us -> 1.07 us
    pallas_call x4 -> x2, Pallas kernels: 32.3 us -> 19.4 us  [attention_chunk(): pl.pallas_call(functools.partial(attention_kernel, packs=packs, first=fir...]
    ppermute x39 -> x28, starting transfers between devices: 39.7 us -> 27.1 us  [swap(): return lax.ppermute(array, axis_name, [(i, i ^ bits) for i in range(size)])]
    ppermute x39 -> x28, waiting for transfers between devices: 73.3 us -> 78.8 us  [swap(): return lax.ppermute(array, axis_name, [(i, i ^ bits) for i in range(size)])]
  transfers between devices with their start and end apart: 39 -> 28, of which waited for: 16 -> 16; matrix products, arithmetic and copies ran while one was open for 2% -> 2% of each run, Pallas kernels for 17% -> 17%
where the time goes in v2:
time: 138 us
  waiting for transfers between devices  78.8 us (57%)
  starting transfers between devices  27.1 us (20%)
  Pallas kernels  24.2 us (18%)
  local copies, waits for them, and re-layouts  4.94 us (4%)
  other arithmetic  1.66 us (1%)
    ppermute x28, waiting for transfers between devices, swap(): return lax.ppermute(array, axis_name, [(i, i ^ bits) for i in range(size)])  78.8 us
    ppermute x28, starting transfers between devices, swap(): return lax.ppermute(array, axis_name, [(i, i ^ bits) for i in range(size)])  27.1 us
    pallas_call x2, Pallas kernels, attention_chunk(): pl.pallas_call(functools.partial(attention_kernel, packs=packs, first=fir...  19.4 us
    unnamed x20, local copies, waits for them, and re-layouts  4.21 us
  transfers between devices with their start and end apart: 28, of which 16 were waited for; matrix products, arithmetic and copies ran while one was open for 2% of the time, Pallas kernels for 17%

profile of v2, /device:TPU:0, one launch (start us, length us, event | category | flops | bytes accessed | tf_op | source)
XLA Modules:
  0.0 137.7 jit_solution(3441351711121083560)
XLA Ops:
  3.7 3.0 %collective-permute-start = (bf16[2,128,2048]{2,1,0:T(8,128)(2,1)S(1)}, bf16[2,128,2048]{2,1,0:T(8,128)(2,1)S(1)}, u32[]{:S(2)}, u32[]{:S(2)}) collective-permute-start(bf16[2,128,2048]{2,1,0:T(8,128)(2,1)S(1)} %get-tuple-element.78.refs_0_), channel_id=1, source_target_pairs={{0,2},{1,3},{2,0},{3,1},{4,6},{5,7},{6,4},{7,5},{8,10},{9,11},{10,... | collective-permute-start | bytes 3145736 | tf_op jit(solution)/shard_map/ppermute | solution.py:508
  6.7 1.6 %collective-permute-start.3 = (bf16[2,128,2048]{2,1,0:T(8,128)(2,1)S(1)}, bf16[2,128,2048]{2,1,0:T(8,128)(2,1)S(1)}, u32[]{:S(2)}, u32[]{:S(2)}) collective-permute-start(bf16[2,128,2048]{2,1,0:T(8,128)(2,1)S(1)} %get-tuple-element.80), channel_id=1, source_target_pairs={{0,5},{1,4},{2,7},{3,6},{4,1},{5,0},{6,3},{7,2},{8,13},{9,12},{10,... | collective-permute-start | bytes 3145736 | tf_op jit(solution)/shard_map/ppermute | solution.py:508
  8.8 21.8 %collective-permute-done.refs_2_ = bf16[2,128,2048]{2,1,0:T(8,128)(2,1)S(1)} collective-permute-done((bf16[2,128,2048]{2,1,0:T(8,128)(2,1)S(1)}, bf16[2,128,2048]{2,1,0:T(8,128)(2,1)S(1)}, u32[]{:S(2)}, u32[]{:S(2)}) %collective-permute-start) | collective-permute-done | bytes 1048608 | tf_op jit(solution)/shard_map/ppermute | solution.py:508
  30.7 1.6 %copy-done.1 = bf16[256,4096]{1,0:T(8,128)(2,1)S(1)} copy-done((bf16[256,4096]{1,0:T(8,128)(2,1)S(1)}, bf16[256,4096]{1,0:T(8,128)(2,1)}, u32[]{:S(2)}) %copy-start.1) | copy-done | bytes 2097176
  32.3 2.0 %tabulate.1 = (bf16[2,256,2048]{2,1,0:T(8,128)(2,1)S(1)}, s32[4,8]{1,0:T(4,128)S(1)}, f32[1,128]{1,0:T(1,128)S(1)}) custom-call(s32[1]{0:T(128)} %bitcast.me_ref, s32[1,16]{1,0:T(1,128)S(1)} %copy-done.4, s32[1,16]{1,0:T(1,128)S(1)} %copy-done.5, s32[1,16]{1,0:T(1,128)S(1)} %copy-done.6, s32[1,16]{1,0:T(1,128)S(1)} %copy-done.7, s32[1,16]{1,0:T(1,128)S(1)} %bitcast.18, ...), custom_call_target="tpu_custom_call" | custom-call | bytes 2097152 | tf_op jit(solution)/shard_map/tabulate/pallas_call | solution.py:100
  34.4 17.1 %collective-permute-done.2.refs_3_ = bf16[2,128,2048]{2,1,0:T(8,128)(2,1)S(1)} collective-permute-done((bf16[2,128,2048]{2,1,0:T(8,128)(2,1)S(1)}, bf16[2,128,2048]{2,1,0:T(8,128)(2,1)S(1)}, u32[]{:S(2)}, u32[]{:S(2)}) %collective-permute-start.2) | collective-permute-done | bytes 1048608 | tf_op jit(solution)/shard_map/ppermute | solution.py:508
  51.5 3.0 %collective-permute-done.1.refs_4_ = bf16[2,128,2048]{2,1,0:T(8,128)(2,1)S(1)} collective-permute-done((bf16[2,128,2048]{2,1,0:T(8,128)(2,1)S(1)}, bf16[2,128,2048]{2,1,0:T(8,128)(2,1)S(1)}, u32[]{:S(2)}, u32[]{:S(2)}) %collective-permute-start.1) | collective-permute-done | bytes 1048608 | tf_op jit(solution)/shard_map/ppermute | solution.py:508
  56.8 1.6 %collective-permute-start.8 = (f32[1,128]{1,0:T(1,128)S(1)}, f32[1,128]{1,0:T(1,128)S(1)}, u32[]{:S(2)}, u32[]{:S(2)}) collective-permute-start(f32[1,128]{1,0:T(1,128)S(1)} %get-tuple-element.89), channel_id=1, source_target_pairs={{0,8},{8,0},{16,24},{24,16},{1,9},{9,1},{17,25},{25,17},{2,10},{10... | collective-permute-start | bytes 1544 | tf_op jit(solution)/shard_map/ppermute | solution.py:508
  58.4 2.0 %collective-permute-done.8 = f32[1,128]{1,0:T(1,128)S(1)} collective-permute-done((f32[1,128]{1,0:T(1,128)S(1)}, f32[1,128]{1,0:T(1,128)S(1)}, u32[]{:S(2)}, u32[]{:S(2)}) %collective-permute-start.8) | collective-permute-done | bytes 544 | tf_op jit(solution)/shard_map/ppermute | solution.py:508
  60.3 2.6 %collective-permute-start.9 = (f32[1,128]{1,0:T(1,128)S(1)}, f32[1,128]{1,0:T(1,128)S(1)}, u32[]{:S(2)}, u32[]{:S(2)}) collective-permute-start(f32[1,128]{1,0:T(1,128)S(1)} %add.58), channel_id=1, source_target_pairs={{0,16},{8,24},{16,0},{24,8},{1,17},{9,25},{17,1},{25,9},{2,18},{10... | collective-permute-start | bytes 1544 | tf_op jit(solution)/shard_map/ppermute | solution.py:508
  65.4 3.5 %collective-permute-done.5.refs_6_ = bf16[2,128,1024]{2,1,0:T(8,128)(2,1)S(1)} collective-permute-done((bf16[2,128,1024]{2,1,0:T(8,128)(2,1)S(1)}, bf16[2,128,1024]{2,1,0:T(8,128)(2,1)S(1)}, u32[]{:S(2)}, u32[]{:S(2)}) %collective-permute-start.5) | collective-permute-done | bytes 524320 | tf_op jit(solution)/shard_map/ppermute | solution.py:508
  71.2 9.6 %attention_chunk.2 = (bf16[256,4096]{1,0:T(8,128)(2,1)}, bf16[256,4096]{1,0:T(8,128)(2,1)}, bf16[2,256,2048]{2,1,0:T(8,128)(2,1)S(1)}, bf16[2,128,1024]{2,1,0:T(...) custom-call(s32[1]{0:T(128)} %bitcast.me_ref, ...), custom_call_target="tpu_custom_call" | custom-call | flops 33554432 | bytes 8388608 | tf_op jit(solution)/shard_map/attention_chunk/pallas_call | solution.py:418
  80.9 2.7 %collective-permute-done.10.refs_6_ = bf16[2,128,1024]{2,1,0:T(8,128)(2,1)S(1)} collective-permute-done((bf16[2,128,1024]{2,1,0:T(8,128)(2,1)S(1)}, bf16[2,128,1024]{2,1,0:T(8,128)(2,1)S(1)}, u32[]{:S(2)}, u32[]{:S(2)}) %collective-permute-start.10) | collective-permute-done | bytes 524320 | tf_op jit(solution)/shard_map/ppermute | solution.py:508
  84.3 1.6 %collective-permute-start.13 = (bf16[128,1024]{1,0:T(8,128)(2,1)S(1)}, bf16[128,1024]{1,0:T(8,128)(2,1)S(1)}, u32[]{:S(2)}, u32[]{:S(2)}) collective-permute-start(bf16[128,1024]{1,0:T(8,128)(2,1)S(1)} %get-tuple-element.110), channel_id=1, source_target_pairs={{0,4},{1,5},{2,6},{3,7},{4,0},{5,1},{6,2},{7,3},{8,12},{9,13},{10,... | collective-permute-start | bytes 786440 | tf_op jit(solution)/shard_map/ppermute | solution.py:508
  85.8 9.8 %attention_chunk.3 = (bf16[256,4096]{1,0:T(8,128)(2,1)}, bf16[256,4096]{1,0:T(8,128)(2,1)}, bf16[2,256,2048]{2,1,0:T(8,128)(2,1)S(1)}, bf16[2,128,1024]{2,1,0:T(...) custom-call(s32[1]{0:T(128)} %bitcast.me_ref, ...), custom_call_target="tpu_custom_call", output_to_operand_aliasing={{0}: (14, {}), {1}: (15, {}), {2}: (16, {})} | custom-call | flops 33554432 | bytes 8388608 | tf_op jit(solution)/shard_map/attention_chunk/pallas_call | solution.py:418
  95.8 1.6 %collective-permute-start.14 = (bf16[2,128,1024]{2,1,0:T(8,128)(2,1)S(1)}, bf16[2,128,1024]{2,1,0:T(8,128)(2,1)S(1)}, u32[]{:S(2)}, u32[]{:S(2)}) collective-permute-start(bf16[2,128,1024]{2,1,0:T(8,128)(2,1)S(1)} %pad_add_fusion.3), channel_id=1, source_target_pairs={{0,2},{1,3},{2,0},{3,1},{4,6},{5,7},{6,4},{7,5},{8,10},{9,11},{10,... | collective-permute-start | bytes 1572872 | tf_op jit(solution)/shard_map/ppermute | solution.py:508
  98.0 1.6 %collective-permute-start.18 = (f32[1,128]{1,0:T(1,128)S(1)}, f32[1,128]{1,0:T(1,128)S(1)}, u32[]{:S(2)}, u32[]{:S(2)}) collective-permute-start(f32[1,128]{1,0:T(1,128)S(1)} %add.62), channel_id=1, source_target_pairs={{0,8},{8,0},{16,24},{24,16},{1,9},{9,1},{17,25},{25,17},{2,10},{10... | collective-permute-start | bytes 1544 | tf_op jit(solution)/shard_map/ppermute | solution.py:508
  99.6 2.0 %collective-permute-done.18 = f32[1,128]{1,0:T(1,128)S(1)} collective-permute-done((f32[1,128]{1,0:T(1,128)S(1)}, f32[1,128]{1,0:T(1,128)S(1)}, u32[]{:S(2)}, u32[]{:S(2)}) %collective-permute-start.18) | collective-permute-done | bytes 544 | tf_op jit(solution)/shard_map/ppermute | solution.py:508
  101.5 2.6 %collective-permute-start.19 = (f32[1,128]{1,0:T(1,128)S(1)}, f32[1,128]{1,0:T(1,128)S(1)}, u32[]{:S(2)}, u32[]{:S(2)}) collective-permute-start(f32[1,128]{1,0:T(1,128)S(1)} %add.63), channel_id=1, source_target_pairs={{0,16},{8,24},{16,0},{24,8},{1,17},{9,25},{17,1},{25,9},{2,18},{10... | collective-permute-start | bytes 1544 | tf_op jit(solution)/shard_map/ppermute | solution.py:508
  104.1 1.8 %collective-permute-done.19 = f32[1,128]{1,0:T(1,128)S(1)} collective-permute-done((f32[1,128]{1,0:T(1,128)S(1)}, f32[1,128]{1,0:T(1,128)S(1)}, u32[]{:S(2)}, u32[]{:S(2)}) %collective-permute-start.19) | collective-permute-done | bytes 544 | tf_op jit(solution)/shard_map/ppermute | solution.py:508
  108.6 7.2 %collective-permute-done.16 = bf16[128,1024]{1,0:T(8,128)(2,1)S(1)} collective-permute-done((bf16[128,1024]{1,0:T(8,128)(2,1)S(1)}, bf16[128,1024]{1,0:T(8,128)(2,1)S(1)}, u32[]{:S(2)}, u32[]{:S(2)}) %collective-permute-start.16) | collective-permute-done | bytes 262176 | tf_op jit(solution)/shard_map/ppermute | solution.py:508
  118.6 1.6 %collective-permute-start.26 = (f32[1,128]{1,0:T(1,128)S(1)}, f32[1,128]{1,0:T(1,128)S(1)}, u32[]{:S(2)}, u32[]{:S(2)}) collective-permute-start(f32[1,128]{1,0:T(1,128)S(1)} %add.65), channel_id=1, source_target_pairs={{0,2},{1,3},{2,0},{3,1},{4,6},{5,7},{6,4},{7,5},{8,10},{9,11},{10,... | collective-permute-start | bytes 1544 | tf_op jit(solution)/shard_map/ppermute | solution.py:508
  120.2 10.9 %collective-permute-done.26 = f32[1,128]{1,0:T(1,128)S(1)} collective-permute-done((f32[1,128]{1,0:T(1,128)S(1)}, f32[1,128]{1,0:T(1,128)S(1)}, u32[]{:S(2)}, u32[]{:S(2)}) %collective-permute-start.26) | collective-permute-done | bytes 544 | tf_op jit(solution)/shard_map/ppermute | solution.py:508
  132.7 2.0 %collective-permute-done.27 = f32[1,128]{1,0:T(1,128)S(1)} collective-permute-done((f32[1,128]{1,0:T(1,128)S(1)}, f32[1,128]{1,0:T(1,128)S(1)}, u32[]{:S(2)}, u32[]{:S(2)}) %collective-permute-start.27) | collective-permute-done | bytes 544 | tf_op jit(solution)/shard_map/ppermute | solution.py:508
  (79 shorter events, 21.9 us)
Async XLA Ops:
  3.7 27.0 %collective-permute-start = (bf16[2,128,2048]{2,1,0:T(8,128)(2,1)S(1)}, bf16[2,128,2048]{2,1,0:T(8,128)(2,1)S(1)}, u32[]{:S(2)}, u32[]{:S(2)}) collective-permute-start(bf16[2,128,2048]{2,1,0:T(8,128)(2,1)S(1)} %get-tuple-element.78.refs_0_), channel_id=1, source_target_pairs={{0,2},{1,3},{2,0},{3,1},{4,6},{5,7},{6,4},{7,5},{8,10},{9,11},{10,... | collective-permute-start | bytes 3145736 | tf_op jit(solution)/shard_map/ppermute | solution.py:508
  6.7 27.7 %collective-permute-start.4 = (bf16[2,128,2048]{2,1,0:T(8,128)(2,1)S(1)}, bf16[2,128,2048]{2,1,0:T(8,128)(2,1)S(1)}, u32[]{:S(2)}, u32[]{:S(2)}) collective-permute-start(bf16[2,128,2048]{2,1,0:T(8,128)(2,1)S(1)} %get-tuple-element.80), channel_id=1, source_target_pairs={{0,1},{1,0},{2,3},{3,2},{4,5},{5,4},{6,7},{7,6},{8,9},{9,8},{10,11... | collective-permute-start | bytes 3145736 | tf_op jit(solution)/shard_map/ppermute | solution.py:508
  6.7 27.8 %collective-permute-start.3 = (bf16[2,128,2048]{2,1,0:T(8,128)(2,1)S(1)}, bf16[2,128,2048]{2,1,0:T(8,128)(2,1)S(1)}, u32[]{:S(2)}, u32[]{:S(2)}) collective-permute-start(bf16[2,128,2048]{2,1,0:T(8,128)(2,1)S(1)} %get-tuple-element.80), channel_id=1, source_target_pairs={{0,5},{1,4},{2,7},{3,6},{4,1},{5,0},{6,3},{7,2},{8,13},{9,12},{10,... | collective-permute-start | bytes 3145736 | tf_op jit(solution)/shard_map/ppermute | solution.py:508
  8.3 43.3 %collective-permute-start.2 = (bf16[2,128,2048]{2,1,0:T(8,128)(2,1)S(1)}, bf16[2,128,2048]{2,1,0:T(8,128)(2,1)S(1)}, u32[]{:S(2)}, u32[]{:S(2)}) collective-permute-start(bf16[2,128,2048]{2,1,0:T(8,128)(2,1)S(1)} %get-tuple-element.80), channel_id=1, source_target_pairs={{0,3},{1,2},{2,1},{3,0},{4,7},{5,6},{6,5},{7,4},{8,11},{9,10},{10,... | collective-permute-start | bytes 3145736 | tf_op jit(solution)/shard_map/ppermute | solution.py:508
  8.4 46.2 %collective-permute-start.1 = (bf16[2,128,2048]{2,1,0:T(8,128)(2,1)S(1)}, bf16[2,128,2048]{2,1,0:T(8,128)(2,1)S(1)}, u32[]{:S(2)}, u32[]{:S(2)}) collective-permute-start(bf16[2,128,2048]{2,1,0:T(8,128)(2,1)S(1)} %get-tuple-element.78.refs_0_), channel_id=1, source_target_pairs={{0,4},{1,5},{2,6},{3,7},{4,0},{5,1},{6,2},{7,3},{8,12},{9,13},{10,... | collective-permute-start | bytes 3145736 | tf_op jit(solution)/shard_map/ppermute | solution.py:508
  54.6 15.7 %collective-permute-start.7 = (bf16[2,256,2048]{2,1,0:T(8,128)(2,1)S(1)}, bf16[2,256,2048]{2,1,0:T(8,128)(2,1)S(1)}, u32[]{:S(2)}, u32[]{:S(2)}) collective-permute-start(bf16[2,256,2048]{2,1,0:T(8,128)(2,1)S(1)} %get-tuple-element.88), channel_id=1, source_target_pairs={{0,1},{1,0},{2,3},{3,2},{4,5},{5,4},{6,7},{7,6},{8,9},{9,8},{10,11... | collective-permute-start | bytes 6291464 | tf_op jit(solution)/shard_map/ppermute | solution.py:508
  54.6 14.3 %collective-permute-start.5 = (bf16[2,128,1024]{2,1,0:T(8,128)(2,1)S(1)}, bf16[2,128,1024]{2,1,0:T(8,128)(2,1)S(1)}, u32[]{:S(2)}, u32[]{:S(2)}) collective-permute-start(bf16[2,128,1024]{2,1,0:T(8,128)(2,1)S(1)} %get-tuple-element.85), channel_id=1, source_target_pairs={{0,4},{1,5},{2,6},{3,7},{4,0},{5,1},{6,2},{7,3},{8,12},{9,13},{10,... | collective-permute-start | bytes 1572872 | tf_op jit(solution)/shard_map/ppermute | solution.py:508
  56.2 14.1 %collective-permute-start.6 = (bf16[2,128,1024]{2,1,0:T(8,128)(2,1)S(1)}, bf16[2,128,1024]{2,1,0:T(8,128)(2,1)S(1)}, u32[]{:S(2)}, u32[]{:S(2)}) collective-permute-start(bf16[2,128,1024]{2,1,0:T(8,128)(2,1)S(1)} %get-tuple-element.155), channel_id=1, source_target_pairs={{0,2},{1,3},{2,0},{3,1},{4,6},{5,7},{6,4},{7,5},{8,10},{9,11},{10,... | collective-permute-start | bytes 1572872 | tf_op jit(solution)/shard_map/ppermute | solution.py:508
  60.3 4.4 %collective-permute-start.9 = (f32[1,128]{1,0:T(1,128)S(1)}, f32[1,128]{1,0:T(1,128)S(1)}, u32[]{:S(2)}, u32[]{:S(2)}) collective-permute-start(f32[1,128]{1,0:T(1,128)S(1)} %add.58), channel_id=1, source_target_pairs={{0,16},{8,24},{16,0},{24,8},{1,17},{9,25},{17,1},{25,9},{2,18},{10... | collective-permute-start | bytes 1544 | tf_op jit(solution)/shard_map/ppermute | solution.py:508
  70.3 13.2 %collective-permute-start.10 = (bf16[2,128,1024]{2,1,0:T(8,128)(2,1)S(1)}, bf16[2,128,1024]{2,1,0:T(8,128)(2,1)S(1)}, u32[]{:S(2)}, u32[]{:S(2)}) collective-permute-start(bf16[2,128,1024]{2,1,0:T(8,128)(2,1)S(1)} %get-tuple-element.90), channel_id=1, source_target_pairs={{0,4},{1,5},{2,6},{3,7},{4,0},{5,1},{6,2},{7,3},{8,12},{9,13},{10,... | collective-permute-start | bytes 1572872 | tf_op jit(solution)/shard_map/ppermute | solution.py:508
  70.8 13.0 %collective-permute-start.11 = (bf16[2,128,1024]{2,1,0:T(8,128)(2,1)S(1)}, bf16[2,128,1024]{2,1,0:T(8,128)(2,1)S(1)}, u32[]{:S(2)}, u32[]{:S(2)}) collective-permute-start(bf16[2,128,1024]{2,1,0:T(8,128)(2,1)S(1)} %get-tuple-element.91), channel_id=1, source_target_pairs={{0,2},{1,3},{2,0},{3,1},{4,6},{5,7},{6,4},{7,5},{8,10},{9,11},{10,... | collective-permute-start | bytes 1572872 | tf_op jit(solution)/shard_map/ppermute | solution.py:508
  83.8 11.9 %collective-permute-start.12 = (bf16[128,1024]{1,0:T(8,128)(2,1)S(1)}, bf16[128,1024]{1,0:T(8,128)(2,1)S(1)}, u32[]{:S(2)}, u32[]{:S(2)}) collective-permute-start(bf16[128,1024]{1,0:T(8,128)(2,1)S(1)} %get-tuple-element.109), channel_id=1, source_target_pairs={{0,2},{1,3},{2,0},{3,1},{4,6},{5,7},{6,4},{7,5},{8,10},{9,11},{10,... | collective-permute-start | bytes 786440 | tf_op jit(solution)/shard_map/ppermute | solution.py:508
  84.3 11.4 %collective-permute-start.13 = (bf16[128,1024]{1,0:T(8,128)(2,1)S(1)}, bf16[128,1024]{1,0:T(8,128)(2,1)S(1)}, u32[]{:S(2)}, u32[]{:S(2)}) collective-permute-start(bf16[128,1024]{1,0:T(8,128)(2,1)S(1)} %get-tuple-element.110), channel_id=1, source_target_pairs={{0,4},{1,5},{2,6},{3,7},{4,0},{5,1},{6,2},{7,3},{8,12},{9,13},{10,... | collective-permute-start | bytes 786440 | tf_op jit(solution)/shard_map/ppermute | solution.py:508
  95.7 36.8 %collective-permute-start.24 = (bf16[2,256,2048]{2,1,0:T(8,128)(2,1)S(1)}, bf16[2,256,2048]{2,1,0:T(8,128)(2,1)S(1)}, u32[]{:S(2)}, u32[]{:S(2)}) collective-permute-start(bf16[2,256,2048]{2,1,0:T(8,128)(2,1)S(1)} %get-tuple-element.140), channel_id=1, source_target_pairs={{0,1},{1,0},{2,3},{3,2},{4,5},{5,4},{6,7},{7,6},{8,9},{9,8},{10,11... | collective-permute-start | bytes 6291464 | tf_op jit(solution)/shard_map/ppermute | solution.py:508
  95.8 21.3 %collective-permute-start.14 = (bf16[2,128,1024]{2,1,0:T(8,128)(2,1)S(1)}, bf16[2,128,1024]{2,1,0:T(8,128)(2,1)S(1)}, u32[]{:S(2)}, u32[]{:S(2)}) collective-permute-start(bf16[2,128,1024]{2,1,0:T(8,128)(2,1)S(1)} %pad_add_fusion.3), channel_id=1, source_target_pairs={{0,2},{1,3},{2,0},{3,1},{4,6},{5,7},{6,4},{7,5},{8,10},{9,11},{10,... | collective-permute-start | bytes 1572872 | tf_op jit(solution)/shard_map/ppermute | solution.py:508
  97.4 19.7 %collective-permute-start.15 = (bf16[2,128,1024]{2,1,0:T(8,128)(2,1)S(1)}, bf16[2,128,1024]{2,1,0:T(8,128)(2,1)S(1)}, u32[]{:S(2)}, u32[]{:S(2)}) collective-permute-start(bf16[2,128,1024]{2,1,0:T(8,128)(2,1)S(1)} %pad_add_fusion.2), channel_id=1, source_target_pairs={{0,4},{1,5},{2,6},{3,7},{4,0},{5,1},{6,2},{7,3},{8,12},{9,13},{10,... | collective-permute-start | bytes 1572872 | tf_op jit(solution)/shard_map/ppermute | solution.py:508
  101.5 4.4 %collective-permute-start.19 = (f32[1,128]{1,0:T(1,128)S(1)}, f32[1,128]{1,0:T(1,128)S(1)}, u32[]{:S(2)}, u32[]{:S(2)}) collective-permute-start(f32[1,128]{1,0:T(1,128)S(1)} %add.63), channel_id=1, source_target_pairs={{0,16},{8,24},{16,0},{24,8},{1,17},{9,25},{17,1},{25,9},{2,18},{10... | collective-permute-start | bytes 1544 | tf_op jit(solution)/shard_map/ppermute | solution.py:508
  106.0 9.8 %collective-permute-start.16 = (bf16[128,1024]{1,0:T(8,128)(2,1)S(1)}, bf16[128,1024]{1,0:T(8,128)(2,1)S(1)}, u32[]{:S(2)}, u32[]{:S(2)}) collective-permute-start(bf16[128,1024]{1,0:T(8,128)(2,1)S(1)} %get-tuple-element.130), channel_id=1, source_target_pairs={{0,2},{1,3},{2,0},{3,1},{4,6},{5,7},{6,4},{7,5},{8,10},{9,11},{10,... | collective-permute-start | bytes 786440 | tf_op jit(solution)/shard_map/ppermute | solution.py:508
  107.1 10.0 %collective-permute-start.17 = (bf16[128,1024]{1,0:T(8,128)(2,1)S(1)}, bf16[128,1024]{1,0:T(8,128)(2,1)S(1)}, u32[]{:S(2)}, u32[]{:S(2)}) collective-permute-start(bf16[128,1024]{1,0:T(8,128)(2,1)S(1)} %get-tuple-element.131), channel_id=1, source_target_pairs={{0,4},{1,5},{2,6},{3,7},{4,0},{5,1},{6,2},{7,3},{8,12},{9,13},{10,... | collective-permute-start | bytes 786440 | tf_op jit(solution)/shard_map/ppermute | solution.py:508
  117.2 15.2 %collective-permute-start.22 = (bf16[2,128,1024]{2,1,0:T(8,128)(2,1)S(1)}, bf16[2,128,1024]{2,1,0:T(8,128)(2,1)S(1)}, u32[]{:S(2)}, u32[]{:S(2)}) collective-permute-start(bf16[2,128,1024]{2,1,0:T(8,128)(2,1)S(1)} %pad_add_fusion), channel_id=1, source_target_pairs={{0,4},{1,5},{2,6},{3,7},{4,0},{5,1},{6,2},{7,3},{8,12},{9,13},{10,... | collective-permute-start | bytes 1572872 | tf_op jit(solution)/shard_map/ppermute | solution.py:508
  117.8 14.6 %collective-permute-start.21 = (bf16[2,128,1024]{2,1,0:T(8,128)(2,1)S(1)}, bf16[2,128,1024]{2,1,0:T(8,128)(2,1)S(1)}, u32[]{:S(2)}, u32[]{:S(2)}) collective-permute-start(bf16[2,128,1024]{2,1,0:T(8,128)(2,1)S(1)} %pad_add_fusion.1), channel_id=1, source_target_pairs={{0,2},{1,3},{2,0},{3,1},{4,6},{5,7},{6,4},{7,5},{8,10},{9,11},{10,... | collective-permute-start | bytes 1572872 | tf_op jit(solution)/shard_map/ppermute | solution.py:508
  118.5 13.9 %collective-permute-start.23 = (bf16[128,1024]{1,0:T(8,128)(2,1)S(1)}, bf16[128,1024]{1,0:T(8,128)(2,1)S(1)}, u32[]{:S(2)}, u32[]{:S(2)}) collective-permute-start(bf16[128,1024]{1,0:T(8,128)(2,1)S(1)} %get-tuple-element.160), channel_id=1, source_target_pairs={{0,1},{1,0},{2,3},{3,2},{4,5},{5,4},{6,7},{7,6},{8,9},{9,8},{10,11... | collective-permute-start | bytes 786440 | tf_op jit(solution)/shard_map/ppermute | solution.py:508
  118.6 12.5 %collective-permute-start.26 = (f32[1,128]{1,0:T(1,128)S(1)}, f32[1,128]{1,0:T(1,128)S(1)}, u32[]{:S(2)}, u32[]{:S(2)}) collective-permute-start(f32[1,128]{1,0:T(1,128)S(1)} %add.65), channel_id=1, source_target_pairs={{0,2},{1,3},{2,0},{3,1},{4,6},{5,7},{6,4},{7,5},{8,10},{9,11},{10,... | collective-permute-start | bytes 1544 | tf_op jit(solution)/shard_map/ppermute | solution.py:508
  132.6 4.1 %collective-permute-start.25 = (bf16[128,1024]{1,0:T(8,128)(2,1)S(1)}, bf16[128,1024]{1,0:T(8,128)(2,1)S(1)}, u32[]{:S(2)}, u32[]{:S(2)}) collective-permute-start(bf16[128,1024]{1,0:T(8,128)(2,1)S(1)} %get-tuple-element.158), channel_id=1, source_target_pairs={{0,1},{1,0},{2,3},{3,2},{4,5},{5,4},{6,7},{7,6},{8,9},{9,8},{10,11... | collective-permute-start | bytes 786440 | tf_op jit(solution)/shard_map/ppermute | solution.py:508
  (14 other events, 211.6 us)

commit v3 on v2

--- a/solution.py
+++ b/solution.py
@@ -154,24 +154,16 @@
     )(me, queries, cotangent)
 
 
-def layout(packs):
-    if packs == 8:
-        return [(0, 2), (2, 2), (4, 2), (6, 1), (7, 1)]
-    return [(first, 2) for first in range(0, packs, 2)]
-
-
 def attention_kernel(
     me_ref, table_ref, scale_ref, *refs, packs, first, bases, half, at
 ):
-    places = layout(packs)
-    sources = len(places)
     pieces = refs[:packs]
     k_ref, v_ref, sibling_ref = refs[packs : packs + 3]
     outs = refs[packs + 3 + (0 if first else 3) :]
     k_out, v_out, sibling_out = outs[:3]
-    query_outs = outs[3 : 3 + sources]
-    loss_out = outs[3 + sources]
-    kv, qc, dq, dkv, loss, scaling, in_sem, qc_sem, out_sem, dkv_sem = outs[sources + 4 :]
+    query_outs = outs[3 : 3 + packs]
+    loss_out = outs[3 + packs]
+    kv, qc, dq, dkv, loss, scaling, in_sem, qc_sem, out_sem, dkv_sem = outs[packs + 4 :]
     width = qc.shape[-1]
     rows = qc.shape[2]
     keys = kv.shape[2]
@@ -389,10 +381,8 @@
             vector = vector + jnp.where(lane == table_ref[item, 5], amount, 0.0)
 
     query_copies = [
-        pltpu.make_async_copy(
-            dq.at[pl.ds(base, 2)] if count == 2 else dq.at[base], target, out_sem.at[i]
-        )
-        for i, (target, (base, count)) in enumerate(zip(query_outs, places))
+        pltpu.make_async_copy(dq.at[distance], target, out_sem.at[distance])
+        for distance, target in enumerate(query_outs)
     ]
     for copy in query_copies:
         copy.start()
@@ -407,7 +397,6 @@
 def attention_chunk(
     me, table, scales, pieces, keys, values, sibling, full, packs, bases, at, width
 ):
-    sources = len(layout(packs))
     rows = pieces[0].shape[1]
     key_rows, features = keys.shape
     half = features // 2
@@ -429,13 +418,10 @@
             jax.ShapeDtypeStruct(keys.shape, low),
             jax.ShapeDtypeStruct((2, key_rows, half), low),
         ]
-        + [
-            jax.ShapeDtypeStruct((count, rows, width)[2 - count :], low)
-            for _, count in layout(packs)
-        ]
+        + [jax.ShapeDtypeStruct((rows, width), low)] * packs
         + [jax.ShapeDtypeStruct((1, 128), jnp.float32)],
         in_specs=[SMEM] * 3 + [ANY] * packs + [HBM] * 2 + [ANY] + [HBM] * (0 if first else 3),
-        out_specs=[HBM] * 3 + [ANY] * sources + [VMEM],
+        out_specs=[HBM] * 3 + [ANY] * packs + [VMEM],
         scratch_shapes=[
             pltpu.VMEM((2, 2, key_rows, width), low),
             pltpu.VMEM((4, 2, rows, width), low),
@@ -445,7 +431,7 @@
             pltpu.VMEM((2, rows, PAIR), jnp.float32),
             pltpu.SemaphoreType.DMA((2, 2)),
             pltpu.SemaphoreType.DMA((4,)),
-            pltpu.SemaphoreType.DMA((sources,)),
+            pltpu.SemaphoreType.DMA((packs,)),
             pltpu.SemaphoreType.DMA((2, 2)),
         ],
         input_output_aliases={} if first else {before + i: i for i in range(3)},
@@ -459,49 +445,56 @@
     )(me, table, scales, *pieces, keys, values, sibling, *(() if first else full))
 
 
-def finish_kernel(me_ref, *refs, spots, half, with_keys):
-    count = 2 * len(spots)
-    outs = refs[-1 - (3 if with_keys else 1) : -1]
-    sem = refs[-1]
+def finish_kernel(me_ref, *refs, terms, at, half, with_keys):
+    near, far = refs[:terms], refs[terms : 2 * terms]
+    outs = refs[-2 - (3 if with_keys else 1) : -2]
+    merged, sem = refs[-2:]
+    width = merged.shape[-1]
     core = lax.rem(me_ref[0], 2)
-    moves = []
-    for i, (at, width) in enumerate(spots):
-        for side, base in enumerate((core, 1 - core)):
-            columns = pl.ds(pl.multiple_of(base * half + at, PAIR), width)
-            moves.append((refs[2 * i + side], outs[0], columns))
+    copies = []
     if with_keys:
         other = pl.ds(pl.multiple_of((1 - core) * half, PAIR), half)
-        moves += [(refs[count].at[tensor], outs[1 + tensor], other) for tensor in range(2)]
-    copies = [
-        pltpu.make_async_copy(source, out.at[:, columns], sem.at[i])
-        for i, (source, out, columns) in enumerate(moves)
-    ]
-    for copy in copies:
-        copy.start()
+        for tensor in range(2):
+            copies.append(
+                pltpu.make_async_copy(
+                    refs[2 * terms].at[tensor], outs[1 + tensor].at[:, other], sem.at[tensor]
+                )
+            )
+            copies[-1].start()
+    for side, (base, parts) in enumerate(((core, near), (1 - core, far))):
+        columns = pl.ds(pl.multiple_of(base * half + at, PAIR), width)
+        merged[side] = functools.reduce(jnp.add, [part[...] for part in parts])
+        copies.append(
+            pltpu.make_async_copy(merged.at[side], outs[0].at[:, columns], sem.at[2 + side])
+        )
+        copies[-1].start()
     for copy in copies:
         copy.wait()
 
 
-def finish(me, parts, spots, like, back=None, given=()):
+def finish(me, near, far, at, like, back=None, given=()):
     with_keys = back is not None
-    read = len(parts) + (1 if with_keys else 0)
+    read = 2 * len(near) + (1 if with_keys else 0)
     shapes = [jax.ShapeDtypeStruct(like.shape, like.dtype)]
     if with_keys:
         shapes += [jax.ShapeDtypeStruct(array.shape, array.dtype) for array in given]
     skipped = len(shapes) - len(given)
     return pl.pallas_call(
         functools.partial(
-            finish_kernel, spots=spots, half=like.shape[1] // 2, with_keys=with_keys
+            finish_kernel, terms=len(near), at=at, half=like.shape[1] // 2, with_keys=with_keys
         ),
         out_shape=shapes,
         in_specs=[SMEM] + [VMEM] * read + [HBM] * len(given),
         out_specs=[HBM] * len(shapes),
-        scratch_shapes=[pltpu.SemaphoreType.DMA((len(parts) + 2,))],
+        scratch_shapes=[
+            pltpu.VMEM((2, *near[0].shape), like.dtype),
+            pltpu.SemaphoreType.DMA((4,)),
+        ],
         input_output_aliases={1 + read + i: skipped + i for i in range(len(given))},
         compiler_params=ROOM,
         cost_estimate=SMALL,
         name="finish",
-    )(me, *parts, *((back,) if with_keys else ()), *given)
+    )(me, *near, *far, *((back,) if with_keys else ()), *given)
 
 
 def swap(array, axis_name, size, bits):
@@ -570,7 +563,7 @@
         kv_other, table, group_counts = tabulated(me)
         kv_sibling = swapped(kv_other, 1)
         counts, scales = scales_of(group_counts)
-        full, losses, query_parts = None, [], []
+        full, losses, ends = None, [], []
         for at, width in spots:
             *result, loss = attention_chunk(
                 me, table, scales, pieces, enc_keys, enc_values, kv_sibling, full,
@@ -578,10 +571,8 @@
             )
             full, parts = result[:3], result[3:]
             losses.append(loss)
-            summed = parts[0]
-            for chip in range(1, len(parts)):
-                summed = summed + swapped(parts[chip], 2 * chip)
-            query_parts += [summed[0], swapped(summed[1], 1)]
+            arrived = parts[:1] + [swapped(parts[i], i) for i in range(1, packs)]
+            ends.append((arrived[0::2], arrived[1::2]))
         back = swapped(full[2], 1)
         loss = doubled_sum(functools.reduce(jnp.add, losses), "pack", packs)
         loss = doubled_sum(loss, "dp", groups)
@@ -615,45 +606,42 @@
             return result[:3], result[3:], loss
 
         def forwarded(parts):
-            return [swapped(parts[3], 2), swapped(parts[4], 4)]
+            return [swapped(parts[6], 2), swapped(parts[7], 4)]
+
+        def sent(parts):
+            return [swapped(parts[2], 2), swapped(parts[5], 5), swapped(parts[1], 1)]
 
         def merged(parts, relay):
-            via_x, via_y = relay
-            to_y = parts[2] + jnp.stack([via_x, jnp.zeros_like(via_x)])
-            to_x = parts[1] + jnp.stack([jnp.zeros_like(via_y), via_y])
-            return [swapped(to_x, 2), swapped(to_y, 4)]
-
-        def total(parts, arrived):
-            return parts[0] + arrived[0] + arrived[1]
+            return [swapped(parts[4] + relay[0], 4), swapped(parts[3] + relay[1], 3)]
+
+        def sums(parts, direct, last):
+            return [parts[0], direct[0], last[0]], [direct[2], direct[1], last[1]]
 
         full, parts_a, loss_a = attend(None, 0, diagonal, 0)
         later, full, parts_a = together((later, full, parts_a))
 
-        relay_a = forwarded(parts_a)
+        relay_a, direct_a = forwarded(parts_a), sent(parts_a)
         full, parts_b, loss_b = attend(full, 1, later, first)
-        relay_a, full, parts_b = together((relay_a, full, parts_b))
-
-        arrived_a = merged(parts_a, relay_a)
-        relay_b = forwarded(parts_b)
-        loss = doubled_sum(doubled_sum(loss_a + loss_b, "dp", groups), "pack", packs, 1, 2)
-        arrived_a, relay_b, loss = together((arrived_a, relay_b, loss))
-
-        arrived_b = merged(parts_b, relay_b)
-        total_a = total(parts_a, arrived_a)
-        query_parts = [total_a[0], swapped(total_a[1], 1)]
+        relay_a, direct_a, full, parts_b, loss_b = together(
+            (relay_a, direct_a, full, parts_b, loss_b)
+        )
+
+        last_a, relay_b = merged(parts_a, relay_a), forwarded(parts_b)
+        loss = doubled_sum(loss_a + loss_b, "dp", groups)
+        loss = doubled_sum(loss, "pack", packs, 1, 4)
+        last_a, relay_b, loss, full = together((last_a, relay_b, loss, full))
+
+        last_b, direct_b = merged(parts_b, relay_b), sent(parts_b)
         back = swapped(full[2], 1)
-        arrived_b, query_parts, back = together((arrived_b, query_parts, back))
-
-        total_b = total(parts_b, arrived_b)
-        query_parts += [total_b[0], swapped(total_b[1], 1)]
-        loss = doubled_sum(loss, "pack", packs, 2)
+        loss = doubled_sum(loss, "pack", packs, 4)
+        last_b, direct_b, back, loss = together((last_b, direct_b, back, loss))
+        ends = [sums(parts_a, direct_a, last_a), sums(parts_b, direct_b, last_b)]
 
     queries_gradient, keys_gradient, values_gradient = finish(
-        me, query_parts[:-2], spots[:-1], dec_queries, back, full[:2]
+        me, *ends[0], starts[0], dec_queries, back, full[:2]
     )
-    (queries_gradient,) = finish(
-        me, query_parts[-2:], spots[-1:], dec_queries, None, (queries_gradient,)
-    )
+    for (at, _), end in zip(spots[1:], ends[1:]):
+        (queries_gradient,) = finish(me, *end, at, dec_queries, None, (queries_gradient,))
     group_loss = (loss / counts)[0, :GROUPS]
     return (queries_gradient, keys_gradient, values_gradient, group_loss)
 

time: 138 us -> 135 us (0.978)
  waiting for transfers between devices: 78.8 us -> 74.1 us
  starting transfers between devices: 27.1 us -> 29.3 us
    ppermute x28 -> x32, waiting for transfers between devices: 78.8 us -> 74.1 us  [swap(): return lax.ppermute(array, axis_name, [(i, i ^ bits) for i in range(size)])]
    ppermute x28 -> x32, starting transfers between devices: 27.1 us -> 29.3 us  [swap(): return lax.ppermute(array, axis_name, [(i, i ^ bits) for i in range(size)])]
  transfers between devices with their start and end apart: 28 -> 32, of which waited for: 16 -> 17; matrix products, arithmetic and copies ran while one was open for 2% -> 1% of each run, Pallas kernels for 17% -> 16%
where the time goes in v3:
time: 135 us
  waiting for transfers between devices  74.1 us (55%)
  starting transfers between devices  29.3 us (22%)
  Pallas kernels  24.3 us (18%)
  local copies, waits for them, and re-layouts  4.88 us (4%)
  other arithmetic  1.55 us (1%)
    ppermute x32, waiting for transfers between devices, swap(): return lax.ppermute(array, axis_name, [(i, i ^ bits) for i in range(size)])  74.1 us
    ppermute x32, starting transfers between devices, swap(): return lax.ppermute(array, axis_name, [(i, i ^ bits) for i in range(size)])  29.3 us
    pallas_call x2, Pallas kernels, attention_chunk(): pl.pallas_call(functools.partial(attention_kernel, packs=packs, first=fir...  19.5 us
    unnamed x20, local copies, waits for them, and re-layouts  4.21 us
  transfers between devices with their start and end apart: 32, of which 17 were waited for; matrix products, arithmetic and copies ran while one was open for 1% of the time, Pallas kernels for 16%

profile of v3, /device:TPU:0, one launch (start us, length us, event | category | flops | bytes accessed | tf_op | source)
XLA Modules:
  0.0 135.2 jit_solution(3577397425444396886)
XLA Ops:
  3.7 3.0 %collective-permute-start = (bf16[2,128,2048]{2,1,0:T(8,128)(2,1)S(1)}, bf16[2,128,2048]{2,1,0:T(8,128)(2,1)S(1)}, u32[]{:S(2)}, u32[]{:S(2)}) collective-permute-start(bf16[2,128,2048]{2,1,0:T(8,128)(2,1)S(1)} %get-tuple-element.99.refs_0_), channel_id=1, source_target_pairs={{0,2},{1,3},{2,0},{3,1},{4,6},{5,7},{6,4},{7,5},{8,10},{9,11},{10,... | collective-permute-start | bytes 3145736 | tf_op jit(solution)/shard_map/ppermute | solution.py:501
  6.7 1.6 %collective-permute-start.3 = (bf16[2,128,2048]{2,1,0:T(8,128)(2,1)S(1)}, bf16[2,128,2048]{2,1,0:T(8,128)(2,1)S(1)}, u32[]{:S(2)}, u32[]{:S(2)}) collective-permute-start(bf16[2,128,2048]{2,1,0:T(8,128)(2,1)S(1)} %get-tuple-element.101), channel_id=1, source_target_pairs={{0,5},{1,4},{2,7},{3,6},{4,1},{5,0},{6,3},{7,2},{8,13},{9,12},{10,... | collective-permute-start | bytes 3145736 | tf_op jit(solution)/shard_map/ppermute | solution.py:501
  8.8 21.8 %collective-permute-done.refs_2_ = bf16[2,128,2048]{2,1,0:T(8,128)(2,1)S(1)} collective-permute-done((bf16[2,128,2048]{2,1,0:T(8,128)(2,1)S(1)}, bf16[2,128,2048]{2,1,0:T(8,128)(2,1)S(1)}, u32[]{:S(2)}, u32[]{:S(2)}) %collective-permute-start) | collective-permute-done | bytes 1048608 | tf_op jit(solution)/shard_map/ppermute | solution.py:501
  30.7 1.6 %copy-done.1 = bf16[256,4096]{1,0:T(8,128)(2,1)S(1)} copy-done((bf16[256,4096]{1,0:T(8,128)(2,1)S(1)}, bf16[256,4096]{1,0:T(8,128)(2,1)}, u32[]{:S(2)}) %copy-start.1) | copy-done | bytes 2097176
  32.3 2.0 %tabulate.1 = (bf16[2,256,2048]{2,1,0:T(8,128)(2,1)S(1)}, s32[4,8]{1,0:T(4,128)S(1)}, f32[1,128]{1,0:T(1,128)S(1)}) custom-call(s32[1]{0:T(128)} %bitcast.me_ref, s32[1,16]{1,0:T(1,128)S(1)} %copy-done.4, s32[1,16]{1,0:T(1,128)S(1)} %copy-done.5, s32[1,16]{1,0:T(1,128)S(1)} %copy-done.6, s32[1,16]{1,0:T(1,128)S(1)} %copy-done.7, s32[1,16]{1,0:T(1,128)S(1)} %bitcast.6, ...), custom_call_target="tpu_custom_call" | custom-call | bytes 2097152 | tf_op jit(solution)/shard_map/tabulate/pallas_call | solution.py:100
  34.4 17.1 %collective-permute-done.2.refs_3_ = bf16[2,128,2048]{2,1,0:T(8,128)(2,1)S(1)} collective-permute-done((bf16[2,128,2048]{2,1,0:T(8,128)(2,1)S(1)}, bf16[2,128,2048]{2,1,0:T(8,128)(2,1)S(1)}, u32[]{:S(2)}, u32[]{:S(2)}) %collective-permute-start.2) | collective-permute-done | bytes 1048608 | tf_op jit(solution)/shard_map/ppermute | solution.py:501
  51.5 3.0 %collective-permute-done.1.refs_4_ = bf16[2,128,2048]{2,1,0:T(8,128)(2,1)S(1)} collective-permute-done((bf16[2,128,2048]{2,1,0:T(8,128)(2,1)S(1)}, bf16[2,128,2048]{2,1,0:T(8,128)(2,1)S(1)}, u32[]{:S(2)}, u32[]{:S(2)}) %collective-permute-start.1) | collective-permute-done | bytes 1048608 | tf_op jit(solution)/shard_map/ppermute | solution.py:501
  54.6 1.5 %collective-permute-start.5 = (bf16[2,128,1024]{2,1,0:T(8,128)(2,1)S(1)}, bf16[2,128,1024]{2,1,0:T(8,128)(2,1)S(1)}, u32[]{:S(2)}, u32[]{:S(2)}) collective-permute-start(bf16[2,128,1024]{2,1,0:T(8,128)(2,1)S(1)} %get-tuple-element.106), channel_id=1, source_target_pairs={{0,4},{1,5},{2,6},{3,7},{4,0},{5,1},{6,2},{7,3},{8,12},{9,13},{10,... | collective-permute-start | bytes 1572872 | tf_op jit(solution)/shard_map/ppermute | solution.py:501
  56.8 1.6 %collective-permute-start.8 = (f32[1,128]{1,0:T(1,128)S(1)}, f32[1,128]{1,0:T(1,128)S(1)}, u32[]{:S(2)}, u32[]{:S(2)}) collective-permute-start(f32[1,128]{1,0:T(1,128)S(1)} %get-tuple-element.110), channel_id=1, source_target_pairs={{0,8},{8,0},{16,24},{24,16},{1,9},{9,1},{17,25},{25,17},{2,10},{10... | collective-permute-start | bytes 1544 | tf_op jit(solution)/shard_map/ppermute | solution.py:501
  58.4 2.0 %collective-permute-done.8 = f32[1,128]{1,0:T(1,128)S(1)} collective-permute-done((f32[1,128]{1,0:T(1,128)S(1)}, f32[1,128]{1,0:T(1,128)S(1)}, u32[]{:S(2)}, u32[]{:S(2)}) %collective-permute-start.8) | collective-permute-done | bytes 544 | tf_op jit(solution)/shard_map/ppermute | solution.py:501
  60.3 2.6 %collective-permute-start.9 = (f32[1,128]{1,0:T(1,128)S(1)}, f32[1,128]{1,0:T(1,128)S(1)}, u32[]{:S(2)}, u32[]{:S(2)}) collective-permute-start(f32[1,128]{1,0:T(1,128)S(1)} %add.38), channel_id=1, source_target_pairs={{0,16},{8,24},{16,0},{24,8},{1,17},{9,25},{17,1},{25,9},{2,18},{10... | collective-permute-start | bytes 1544 | tf_op jit(solution)/shard_map/ppermute | solution.py:501
  65.4 3.5 %collective-permute-done.5.refs_6_ = bf16[2,128,1024]{2,1,0:T(8,128)(2,1)S(1)} collective-permute-done((bf16[2,128,1024]{2,1,0:T(8,128)(2,1)S(1)}, bf16[2,128,1024]{2,1,0:T(8,128)(2,1)S(1)}, u32[]{:S(2)}, u32[]{:S(2)}) %collective-permute-start.5) | collective-permute-done | bytes 524320 | tf_op jit(solution)/shard_map/ppermute | solution.py:501
  71.2 9.6 %attention_chunk.2 = (bf16[256,4096]{1,0:T(8,128)(2,1)}, bf16[256,4096]{1,0:T(8,128)(2,1)}, bf16[2,256,2048]{2,1,0:T(8,128)(2,1)S(1)}, bf16[128,1024]{1,0:T(8,12...) custom-call(s32[1]{0:T(128)} %bitcast.me_ref, ...), custom_call_target="tpu_custom_call" | custom-call | flops 33554432 | bytes 8388608 | tf_op jit(solution)/shard_map/attention_chunk/pallas_call | solution.py:407
  80.9 2.7 %collective-permute-done.10.refs_6_ = bf16[2,128,1024]{2,1,0:T(8,128)(2,1)S(1)} collective-permute-done((bf16[2,128,1024]{2,1,0:T(8,128)(2,1)S(1)}, bf16[2,128,1024]{2,1,0:T(8,128)(2,1)S(1)}, u32[]{:S(2)}, u32[]{:S(2)}) %collective-permute-start.10) | collective-permute-done | bytes 524320 | tf_op jit(solution)/shard_map/ppermute | solution.py:501
  84.3 1.6 %collective-permute-start.13 = (bf16[128,1024]{1,0:T(8,128)(2,1)S(1)}, bf16[128,1024]{1,0:T(8,128)(2,1)S(1)}, u32[]{:S(2)}, u32[]{:S(2)}) collective-permute-start(bf16[128,1024]{1,0:T(8,128)(2,1)S(1)} %get-tuple-element.134), channel_id=1, source_target_pairs={{0,4},{1,5},{2,6},{3,7},{4,0},{5,1},{6,2},{7,3},{8,12},{9,13},{10,... | collective-permute-start | bytes 786440 | tf_op jit(solution)/shard_map/ppermute | solution.py:501
  88.0 9.8 %attention_chunk.3 = (bf16[256,4096]{1,0:T(8,128)(2,1)}, bf16[256,4096]{1,0:T(8,128)(2,1)}, bf16[2,256,2048]{2,1,0:T(8,128)(2,1)S(1)}, bf16[128,1024]{1,0:T(8,12...) custom-call(s32[1]{0:T(128)} %bitcast.me_ref, ...), custom_call_target="tpu_custom_call", output_to_operand_aliasing={{0}: (14, {}), {1}: (15, {}), {2}: (16, {})} | custom-call | flops 33554432 | bytes 8388608 | tf_op jit(solution)/shard_map/attention_chunk/pallas_call | solution.py:407
  97.9 1.6 %collective-permute-start.17 = (bf16[128,1024]{1,0:T(8,128)(2,1)S(1)}, bf16[128,1024]{1,0:T(8,128)(2,1)S(1)}, u32[]{:S(2)}, u32[]{:S(2)}) collective-permute-start(bf16[128,1024]{1,0:T(8,128)(2,1)S(1)} %add.40), channel_id=1, source_target_pairs={{0,4},{1,5},{2,6},{3,7},{4,0},{5,1},{6,2},{7,3},{8,12},{9,13},{10,... | collective-permute-start | bytes 786440 | tf_op jit(solution)/shard_map/ppermute | solution.py:501
  101.5 1.6 %collective-permute-start.21 = (f32[1,128]{1,0:T(1,128)S(1)}, f32[1,128]{1,0:T(1,128)S(1)}, u32[]{:S(2)}, u32[]{:S(2)}) collective-permute-start(f32[1,128]{1,0:T(1,128)S(1)} %add.42), channel_id=1, source_target_pairs={{0,8},{8,0},{16,24},{24,16},{1,9},{9,1},{17,25},{25,17},{2,10},{10... | collective-permute-start | bytes 1544 | tf_op jit(solution)/shard_map/ppermute | solution.py:501
  103.1 2.0 %collective-permute-done.21 = f32[1,128]{1,0:T(1,128)S(1)} collective-permute-done((f32[1,128]{1,0:T(1,128)S(1)}, f32[1,128]{1,0:T(1,128)S(1)}, u32[]{:S(2)}, u32[]{:S(2)}) %collective-permute-start.21) | collective-permute-done | bytes 544 | tf_op jit(solution)/shard_map/ppermute | solution.py:501
  105.0 2.6 %collective-permute-start.22 = (f32[1,128]{1,0:T(1,128)S(1)}, f32[1,128]{1,0:T(1,128)S(1)}, u32[]{:S(2)}, u32[]{:S(2)}) collective-permute-start(f32[1,128]{1,0:T(1,128)S(1)} %add.43), channel_id=1, source_target_pairs={{0,16},{8,24},{16,0},{24,8},{1,17},{9,25},{17,1},{25,9},{2,18},{10... | collective-permute-start | bytes 1544 | tf_op jit(solution)/shard_map/ppermute | solution.py:501
  107.6 1.8 %collective-permute-done.22 = f32[1,128]{1,0:T(1,128)S(1)} collective-permute-done((f32[1,128]{1,0:T(1,128)S(1)}, f32[1,128]{1,0:T(1,128)S(1)}, u32[]{:S(2)}, u32[]{:S(2)}) %collective-permute-start.22) | collective-permute-done | bytes 544 | tf_op jit(solution)/shard_map/ppermute | solution.py:501
  111.4 2.8 %collective-permute-done.24 = f32[1,128]{1,0:T(1,128)S(1)} collective-permute-done((f32[1,128]{1,0:T(1,128)S(1)}, f32[1,128]{1,0:T(1,128)S(1)}, u32[]{:S(2)}, u32[]{:S(2)}) %collective-permute-start.24) | collective-permute-done | bytes 544 | tf_op jit(solution)/shard_map/ppermute | solution.py:501
  117.1 5.9 %collective-permute-done.27.refs_1_ = bf16[128,1024]{1,0:T(8,128)(2,1)S(1)} collective-permute-done((bf16[128,1024]{1,0:T(8,128)(2,1)S(1)}, bf16[128,1024]{1,0:T(8,128)(2,1)S(1)}, u32[]{:S(2)}, u32[]{:S(2)}) %collective-permute-start.27) | collective-permute-done | bytes 262176 | tf_op jit(solution)/shard_map/ppermute | solution.py:501
  125.2 6.2 %collective-permute-done.26.refs_5_ = bf16[128,1024]{1,0:T(8,128)(2,1)S(1)} collective-permute-done((bf16[128,1024]{1,0:T(8,128)(2,1)S(1)}, bf16[128,1024]{1,0:T(8,128)(2,1)S(1)}, u32[]{:S(2)}, u32[]{:S(2)}) %collective-permute-start.26) | collective-permute-done | bytes 262176 | tf_op jit(solution)/shard_map/ppermute | solution.py:501
  (84 shorter events, 24.6 us)
Async XLA Ops:
  3.7 27.0 %collective-permute-start = (bf16[2,128,2048]{2,1,0:T(8,128)(2,1)S(1)}, bf16[2,128,2048]{2,1,0:T(8,128)(2,1)S(1)}, u32[]{:S(2)}, u32[]{:S(2)}) collective-permute-start(bf16[2,128,2048]{2,1,0:T(8,128)(2,1)S(1)} %get-tuple-element.99.refs_0_), channel_id=1, source_target_pairs={{0,2},{1,3},{2,0},{3,1},{4,6},{5,7},{6,4},{7,5},{8,10},{9,11},{10,... | collective-permute-start | bytes 3145736 | tf_op jit(solution)/shard_map/ppermute | solution.py:501
  6.7 27.8 %collective-permute-start.4 = (bf16[2,128,2048]{2,1,0:T(8,128)(2,1)S(1)}, bf16[2,128,2048]{2,1,0:T(8,128)(2,1)S(1)}, u32[]{:S(2)}, u32[]{:S(2)}) collective-permute-start(bf16[2,128,2048]{2,1,0:T(8,128)(2,1)S(1)} %get-tuple-element.101), channel_id=1, source_target_pairs={{0,1},{1,0},{2,3},{3,2},{4,5},{5,4},{6,7},{7,6},{8,9},{9,8},{10,11... | collective-permute-start | bytes 3145736 | tf_op jit(solution)/shard_map/ppermute | solution.py:501
  6.7 27.8 %collective-permute-start.3 = (bf16[2,128,2048]{2,1,0:T(8,128)(2,1)S(1)}, bf16[2,128,2048]{2,1,0:T(8,128)(2,1)S(1)}, u32[]{:S(2)}, u32[]{:S(2)}) collective-permute-start(bf16[2,128,2048]{2,1,0:T(8,128)(2,1)S(1)} %get-tuple-element.101), channel_id=1, source_target_pairs={{0,5},{1,4},{2,7},{3,6},{4,1},{5,0},{6,3},{7,2},{8,13},{9,12},{10,... | collective-permute-start | bytes 3145736 | tf_op jit(solution)/shard_map/ppermute | solution.py:501
  8.3 43.3 %collective-permute-start.2 = (bf16[2,128,2048]{2,1,0:T(8,128)(2,1)S(1)}, bf16[2,128,2048]{2,1,0:T(8,128)(2,1)S(1)}, u32[]{:S(2)}, u32[]{:S(2)}) collective-permute-start(bf16[2,128,2048]{2,1,0:T(8,128)(2,1)S(1)} %get-tuple-element.101), channel_id=1, source_target_pairs={{0,3},{1,2},{2,1},{3,0},{4,7},{5,6},{6,5},{7,4},{8,11},{9,10},{10,... | collective-permute-start | bytes 3145736 | tf_op jit(solution)/shard_map/ppermute | solution.py:501
  8.4 46.2 %collective-permute-start.1 = (bf16[2,128,2048]{2,1,0:T(8,128)(2,1)S(1)}, bf16[2,128,2048]{2,1,0:T(8,128)(2,1)S(1)}, u32[]{:S(2)}, u32[]{:S(2)}) collective-permute-start(bf16[2,128,2048]{2,1,0:T(8,128)(2,1)S(1)} %get-tuple-element.99.refs_0_), channel_id=1, source_target_pairs={{0,4},{1,5},{2,6},{3,7},{4,0},{5,1},{6,2},{7,3},{8,12},{9,13},{10,... | collective-permute-start | bytes 3145736 | tf_op jit(solution)/shard_map/ppermute | solution.py:501
  54.6 15.7 %collective-permute-start.7 = (bf16[2,256,2048]{2,1,0:T(8,128)(2,1)S(1)}, bf16[2,256,2048]{2,1,0:T(8,128)(2,1)S(1)}, u32[]{:S(2)}, u32[]{:S(2)}) collective-permute-start(bf16[2,256,2048]{2,1,0:T(8,128)(2,1)S(1)} %get-tuple-element.109), channel_id=1, source_target_pairs={{0,1},{1,0},{2,3},{3,2},{4,5},{5,4},{6,7},{7,6},{8,9},{9,8},{10,11... | collective-permute-start | bytes 6291464 | tf_op jit(solution)/shard_map/ppermute | solution.py:501
  54.6 14.3 %collective-permute-start.5 = (bf16[2,128,1024]{2,1,0:T(8,128)(2,1)S(1)}, bf16[2,128,1024]{2,1,0:T(8,128)(2,1)S(1)}, u32[]{:S(2)}, u32[]{:S(2)}) collective-permute-start(bf16[2,128,1024]{2,1,0:T(8,128)(2,1)S(1)} %get-tuple-element.106), channel_id=1, source_target_pairs={{0,4},{1,5},{2,6},{3,7},{4,0},{5,1},{6,2},{7,3},{8,12},{9,13},{10,... | collective-permute-start | bytes 1572872 | tf_op jit(solution)/shard_map/ppermute | solution.py:501
  56.2 14.1 %collective-permute-start.6 = (bf16[2,128,1024]{2,1,0:T(8,128)(2,1)S(1)}, bf16[2,128,1024]{2,1,0:T(8,128)(2,1)S(1)}, u32[]{:S(2)}, u32[]{:S(2)}) collective-permute-start(bf16[2,128,1024]{2,1,0:T(8,128)(2,1)S(1)} %get-tuple-element.197), channel_id=1, source_target_pairs={{0,2},{1,3},{2,0},{3,1},{4,6},{5,7},{6,4},{7,5},{8,10},{9,11},{10,... | collective-permute-start | bytes 1572872 | tf_op jit(solution)/shard_map/ppermute | solution.py:501
  70.3 13.2 %collective-permute-start.10 = (bf16[2,128,1024]{2,1,0:T(8,128)(2,1)S(1)}, bf16[2,128,1024]{2,1,0:T(8,128)(2,1)S(1)}, u32[]{:S(2)}, u32[]{:S(2)}) collective-permute-start(bf16[2,128,1024]{2,1,0:T(8,128)(2,1)S(1)} %get-tuple-element.111), channel_id=1, source_target_pairs={{0,4},{1,5},{2,6},{3,7},{4,0},{5,1},{6,2},{7,3},{8,12},{9,13},{10,... | collective-permute-start | bytes 1572872 | tf_op jit(solution)/shard_map/ppermute | solution.py:501
  70.8 13.0 %collective-permute-start.11 = (bf16[2,128,1024]{2,1,0:T(8,128)(2,1)S(1)}, bf16[2,128,1024]{2,1,0:T(8,128)(2,1)S(1)}, u32[]{:S(2)}, u32[]{:S(2)}) collective-permute-start(bf16[2,128,1024]{2,1,0:T(8,128)(2,1)S(1)} %get-tuple-element.112), channel_id=1, source_target_pairs={{0,2},{1,3},{2,0},{3,1},{4,6},{5,7},{6,4},{7,5},{8,10},{9,11},{10,... | collective-permute-start | bytes 1572872 | tf_op jit(solution)/shard_map/ppermute | solution.py:501
  83.8 14.0 %collective-permute-start.12 = (bf16[128,1024]{1,0:T(8,128)(2,1)S(1)}, bf16[128,1024]{1,0:T(8,128)(2,1)S(1)}, u32[]{:S(2)}, u32[]{:S(2)}) collective-permute-start(bf16[128,1024]{1,0:T(8,128)(2,1)S(1)} %get-tuple-element.133), channel_id=1, source_target_pairs={{0,2},{1,3},{2,0},{3,1},{4,6},{5,7},{6,4},{7,5},{8,10},{9,11},{10,... | collective-permute-start | bytes 786440 | tf_op jit(solution)/shard_map/ppermute | solution.py:501
  84.3 13.5 %collective-permute-start.13 = (bf16[128,1024]{1,0:T(8,128)(2,1)S(1)}, bf16[128,1024]{1,0:T(8,128)(2,1)S(1)}, u32[]{:S(2)}, u32[]{:S(2)}) collective-permute-start(bf16[128,1024]{1,0:T(8,128)(2,1)S(1)} %get-tuple-element.134), channel_id=1, source_target_pairs={{0,4},{1,5},{2,6},{3,7},{4,0},{5,1},{6,2},{7,3},{8,12},{9,13},{10,... | collective-permute-start | bytes 786440 | tf_op jit(solution)/shard_map/ppermute | solution.py:501
  85.8 12.0 %collective-permute-start.14 = (bf16[128,1024]{1,0:T(8,128)(2,1)S(1)}, bf16[128,1024]{1,0:T(8,128)(2,1)S(1)}, u32[]{:S(2)}, u32[]{:S(2)}) collective-permute-start(bf16[128,1024]{1,0:T(8,128)(2,1)S(1)} %get-tuple-element.135), channel_id=1, source_target_pairs={{0,2},{1,3},{2,0},{3,1},{4,6},{5,7},{6,4},{7,5},{8,10},{9,11},{10,... | collective-permute-start | bytes 786440 | tf_op jit(solution)/shard_map/ppermute | solution.py:501
  87.3 10.5 %collective-permute-start.15 = (bf16[128,1024]{1,0:T(8,128)(2,1)S(1)}, bf16[128,1024]{1,0:T(8,128)(2,1)S(1)}, u32[]{:S(2)}, u32[]{:S(2)}) collective-permute-start(bf16[128,1024]{1,0:T(8,128)(2,1)S(1)} %get-tuple-element.136), channel_id=1, source_target_pairs={{0,5},{1,4},{2,7},{3,6},{4,1},{5,0},{6,3},{7,2},{8,13},{9,12},{10,... | collective-permute-start | bytes 786440 | tf_op jit(solution)/shard_map/ppermute | solution.py:501
  87.3 10.5 %collective-permute-start.16 = (bf16[128,1024]{1,0:T(8,128)(2,1)S(1)}, bf16[128,1024]{1,0:T(8,128)(2,1)S(1)}, u32[]{:S(2)}, u32[]{:S(2)}) collective-permute-start(bf16[128,1024]{1,0:T(8,128)(2,1)S(1)} %get-tuple-element.137), channel_id=1, source_target_pairs={{0,1},{1,0},{2,3},{3,2},{4,5},{5,4},{6,7},{7,6},{8,9},{9,8},{10,11... | collective-permute-start | bytes 786440 | tf_op jit(solution)/shard_map/ppermute | solution.py:501
  97.9 16.2 %collective-permute-start.17 = (bf16[128,1024]{1,0:T(8,128)(2,1)S(1)}, bf16[128,1024]{1,0:T(8,128)(2,1)S(1)}, u32[]{:S(2)}, u32[]{:S(2)}) collective-permute-start(bf16[128,1024]{1,0:T(8,128)(2,1)S(1)} %add.40), channel_id=1, source_target_pairs={{0,4},{1,5},{2,6},{3,7},{4,0},{5,1},{6,2},{7,3},{8,12},{9,13},{10,... | collective-permute-start | bytes 786440 | tf_op jit(solution)/shard_map/ppermute | solution.py:501
  99.6 14.6 %collective-permute-start.18 = (bf16[128,1024]{1,0:T(8,128)(2,1)S(1)}, bf16[128,1024]{1,0:T(8,128)(2,1)S(1)}, u32[]{:S(2)}, u32[]{:S(2)}) collective-permute-start(bf16[128,1024]{1,0:T(8,128)(2,1)S(1)} %add.41), channel_id=1, source_target_pairs={{0,3},{1,2},{2,1},{3,0},{4,7},{5,6},{6,5},{7,4},{8,11},{9,10},{10,... | collective-permute-start | bytes 786440 | tf_op jit(solution)/shard_map/ppermute | solution.py:501
  99.7 14.5 %collective-permute-start.19 = (bf16[128,1024]{1,0:T(8,128)(2,1)S(1)}, bf16[128,1024]{1,0:T(8,128)(2,1)S(1)}, u32[]{:S(2)}, u32[]{:S(2)}) collective-permute-start(bf16[128,1024]{1,0:T(8,128)(2,1)S(1)} %get-tuple-element.161), channel_id=1, source_target_pairs={{0,2},{1,3},{2,0},{3,1},{4,6},{5,7},{6,4},{7,5},{8,10},{9,11},{10,... | collective-permute-start | bytes 786440 | tf_op jit(solution)/shard_map/ppermute | solution.py:501
  101.0 13.2 %collective-permute-start.20 = (bf16[128,1024]{1,0:T(8,128)(2,1)S(1)}, bf16[128,1024]{1,0:T(8,128)(2,1)S(1)}, u32[]{:S(2)}, u32[]{:S(2)}) collective-permute-start(bf16[128,1024]{1,0:T(8,128)(2,1)S(1)} %get-tuple-element.162), channel_id=1, source_target_pairs={{0,4},{1,5},{2,6},{3,7},{4,0},{5,1},{6,2},{7,3},{8,12},{9,13},{10,... | collective-permute-start | bytes 786440 | tf_op jit(solution)/shard_map/ppermute | solution.py:501
  114.2 17.9 %collective-permute-start.30 = (bf16[2,256,2048]{2,1,0:T(8,128)(2,1)S(1)}, bf16[2,256,2048]{2,1,0:T(8,128)(2,1)S(1)}, u32[]{:S(2)}, u32[]{:S(2)}) collective-permute-start(bf16[2,256,2048]{2,1,0:T(8,128)(2,1)S(1)} %get-tuple-element.174), channel_id=1, source_target_pairs={{0,1},{1,0},{2,3},{3,2},{4,5},{5,4},{6,7},{7,6},{8,9},{9,8},{10,11... | collective-permute-start | bytes 6291464 | tf_op jit(solution)/shard_map/ppermute | solution.py:501
  114.3 8.7 %collective-permute-start.27 = (bf16[128,1024]{1,0:T(8,128)(2,1)S(1)}, bf16[128,1024]{1,0:T(8,128)(2,1)S(1)}, u32[]{:S(2)}, u32[]{:S(2)}) collective-permute-start(bf16[128,1024]{1,0:T(8,128)(2,1)S(1)} %get-tuple-element.171), channel_id=1, source_target_pairs={{0,2},{1,3},{2,0},{3,1},{4,6},{5,7},{6,4},{7,5},{8,10},{9,11},{10,... | collective-permute-start | bytes 786440 | tf_op jit(solution)/shard_map/ppermute | solution.py:501
  115.1 10.1 %collective-permute-start.28 = (bf16[128,1024]{1,0:T(8,128)(2,1)S(1)}, bf16[128,1024]{1,0:T(8,128)(2,1)S(1)}, u32[]{:S(2)}, u32[]{:S(2)}) collective-permute-start(bf16[128,1024]{1,0:T(8,128)(2,1)S(1)} %get-tuple-element.172), channel_id=1, source_target_pairs={{0,5},{1,4},{2,7},{3,6},{4,1},{5,0},{6,3},{7,2},{8,13},{9,12},{10,... | collective-permute-start | bytes 786440 | tf_op jit(solution)/shard_map/ppermute | solution.py:501
  123.0 8.4 %collective-permute-start.26 = (bf16[128,1024]{1,0:T(8,128)(2,1)S(1)}, bf16[128,1024]{1,0:T(8,128)(2,1)S(1)}, u32[]{:S(2)}, u32[]{:S(2)}) collective-permute-start(bf16[128,1024]{1,0:T(8,128)(2,1)S(1)} %add.48), channel_id=1, source_target_pairs={{0,3},{1,2},{2,1},{3,0},{4,7},{5,6},{6,5},{7,4},{8,11},{9,10},{10,... | collective-permute-start | bytes 786440 | tf_op jit(solution)/shard_map/ppermute | solution.py:501
  123.7 8.4 %collective-permute-start.25 = (bf16[128,1024]{1,0:T(8,128)(2,1)S(1)}, bf16[128,1024]{1,0:T(8,128)(2,1)S(1)}, u32[]{:S(2)}, u32[]{:S(2)}) collective-permute-start(bf16[128,1024]{1,0:T(8,128)(2,1)S(1)} %add.47), channel_id=1, source_target_pairs={{0,4},{1,5},{2,6},{3,7},{4,0},{5,1},{6,2},{7,3},{8,12},{9,13},{10,... | collective-permute-start | bytes 786440 | tf_op jit(solution)/shard_map/ppermute | solution.py:501
  (18 other events, 236.1 us)

commit v4 on v3

--- a/solution.py
+++ b/solution.py
@@ -161,9 +161,9 @@
     k_ref, v_ref, sibling_ref = refs[packs : packs + 3]
     outs = refs[packs + 3 + (0 if first else 3) :]
     k_out, v_out, sibling_out = outs[:3]
-    query_outs = outs[3 : 3 + packs]
-    loss_out = outs[3 + packs]
-    kv, qc, dq, dkv, loss, scaling, in_sem, qc_sem, out_sem, dkv_sem = outs[packs + 4 :]
+    query_outs = outs[3 : 2 + packs]
+    loss_out = outs[2 + packs]
+    kv, qc, dq, dkv, loss, scaling, in_sem, qc_sem, out_sem, dkv_sem = outs[packs + 3 :]
     width = qc.shape[-1]
     rows = qc.shape[2]
     keys = kv.shape[2]
@@ -189,7 +189,9 @@
         ],
         [
             pltpu.make_async_copy(
-                dkv.at[1, tensor], sibling_out.at[tensor, :, half_columns], dkv_sem.at[1, tensor]
+                dkv.at[1, tensor],
+                sibling_out.at[pl.ds(tensor * keys, keys), half_columns],
+                dkv_sem.at[1, tensor],
             )
             for tensor in range(2)
         ],
@@ -380,9 +382,10 @@
             amount = jnp.sum(part, axis=1, keepdims=True)
             vector = vector + jnp.where(lane == table_ref[item, 5], amount, 0.0)
 
+    targets = [query_outs[0], sibling_out.at[pl.ds(2 * keys, rows), half_columns], *query_outs[1:]]
     query_copies = [
         pltpu.make_async_copy(dq.at[distance], target, out_sem.at[distance])
-        for distance, target in enumerate(query_outs)
+        for distance, target in enumerate(targets)
     ]
     for copy in query_copies:
         copy.start()
@@ -416,12 +419,12 @@
         out_shape=[
             jax.ShapeDtypeStruct(keys.shape, low),
             jax.ShapeDtypeStruct(keys.shape, low),
-            jax.ShapeDtypeStruct((2, key_rows, half), low),
+            jax.ShapeDtypeStruct((2 * key_rows + rows, half), low),
         ]
-        + [jax.ShapeDtypeStruct((rows, width), low)] * packs
+        + [jax.ShapeDtypeStruct((rows, width), low)] * (packs - 1)
         + [jax.ShapeDtypeStruct((1, 128), jnp.float32)],
         in_specs=[SMEM] * 3 + [ANY] * packs + [HBM] * 2 + [ANY] + [HBM] * (0 if first else 3),
-        out_specs=[HBM] * 3 + [ANY] * packs + [VMEM],
+        out_specs=[HBM] * 3 + [ANY] * (packs - 1) + [VMEM],
         scratch_shapes=[
             pltpu.VMEM((2, 2, key_rows, width), low),
             pltpu.VMEM((4, 2, rows, width), low),
@@ -445,56 +448,54 @@
     )(me, table, scales, *pieces, keys, values, sibling, *(() if first else full))
 
 
-def finish_kernel(me_ref, *refs, terms, at, half, with_keys):
-    near, far = refs[:terms], refs[terms : 2 * terms]
-    outs = refs[-2 - (3 if with_keys else 1) : -2]
-    merged, sem = refs[-2:]
-    width = merged.shape[-1]
+def finish_kernel(me_ref, *refs, counts, starts, half):
+    back = refs[sum(counts)]
+    outs = refs[sum(counts) + 3 : sum(counts) + 6]
+    *merged, sem = refs[sum(counts) + 6 :]
+    rows, keys = merged[0].shape[1], outs[1].shape[0]
     core = lax.rem(me_ref[0], 2)
     copies = []
-    if with_keys:
-        other = pl.ds(pl.multiple_of((1 - core) * half, PAIR), half)
-        for tensor in range(2):
-            copies.append(
-                pltpu.make_async_copy(
-                    refs[2 * terms].at[tensor], outs[1 + tensor].at[:, other], sem.at[tensor]
-                )
-            )
-            copies[-1].start()
-    for side, (base, parts) in enumerate(((core, near), (1 - core, far))):
-        columns = pl.ds(pl.multiple_of(base * half + at, PAIR), width)
-        merged[side] = functools.reduce(jnp.add, [part[...] for part in parts])
-        copies.append(
-            pltpu.make_async_copy(merged.at[side], outs[0].at[:, columns], sem.at[2 + side])
-        )
+
+    def write(source, out, columns):
+        copies.append(pltpu.make_async_copy(source, out.at[:, columns], sem.at[len(copies)]))
         copies[-1].start()
+
+    other = pl.ds(pl.multiple_of((1 - core) * half, PAIR), half)
+    for tensor in range(2):
+        write(back.at[pl.ds(tensor * keys, keys)], outs[1 + tensor], other)
+    given = list(refs[: sum(counts)])
+    for chunk, (at, held) in enumerate(zip(starts, merged)):
+        width = held.shape[-1]
+        for side, base in enumerate((core, 1 - core)):
+            terms = [given.pop(0)[...] for _ in range(counts[2 * chunk + side])]
+            if side == 1:
+                terms.append(back[2 * keys : 2 * keys + rows, at : at + width])
+            held[side] = functools.reduce(jnp.add, terms)
+            columns = pl.ds(pl.multiple_of(base * half + at, PAIR), width)
+            write(held.at[side], outs[0], columns)
     for copy in copies:
         copy.wait()
 
 
-def finish(me, near, far, at, like, back=None, given=()):
-    with_keys = back is not None
-    read = 2 * len(near) + (1 if with_keys else 0)
-    shapes = [jax.ShapeDtypeStruct(like.shape, like.dtype)]
-    if with_keys:
-        shapes += [jax.ShapeDtypeStruct(array.shape, array.dtype) for array in given]
-    skipped = len(shapes) - len(given)
+def finish(me, ends, starts, packs, back, like, keys, values):
+    parts = [part for near, far in ends for part in near + far]
+    counts = [len(side) for end in ends for side in end]
     return pl.pallas_call(
         functools.partial(
-            finish_kernel, terms=len(near), at=at, half=like.shape[1] // 2, with_keys=with_keys
+            finish_kernel, counts=counts, starts=starts, half=like.shape[1] // 2
         ),
-        out_shape=shapes,
-        in_specs=[SMEM] + [VMEM] * read + [HBM] * len(given),
-        out_specs=[HBM] * len(shapes),
-        scratch_shapes=[
-            pltpu.VMEM((2, *near[0].shape), like.dtype),
-            pltpu.SemaphoreType.DMA((4,)),
-        ],
-        input_output_aliases={1 + read + i: skipped + i for i in range(len(given))},
-        compiler_params=ROOM,
+        out_shape=[
+            jax.ShapeDtypeStruct(array.shape, array.dtype) for array in (like, keys, values)
+        ],
+        in_specs=[SMEM] + [VMEM] * (len(parts) + 1) + [HBM] * 2,
+        out_specs=[HBM] * 3,
+        scratch_shapes=[pltpu.VMEM((2, *near[0].shape), like.dtype) for near, _ in ends]
+        + [pltpu.SemaphoreType.DMA((2 + 2 * len(ends),))],
+        input_output_aliases={len(parts) + 2: 1, len(parts) + 3: 2},
+        compiler_params=pltpu.CompilerParams(vmem_limit_bytes=(8 + packs) * 1024 * 1024),
         cost_estimate=SMALL,
         name="finish",
-    )(me, *near, *far, *((back,) if with_keys else ()), *given)
+    )(me, *parts, back, keys, values)
 
 
 def swap(array, axis_name, size, bits):
@@ -571,28 +572,26 @@
             )
             full, parts = result[:3], result[3:]
             losses.append(loss)
-            arrived = parts[:1] + [swapped(parts[i], i) for i in range(1, packs)]
-            ends.append((arrived[0::2], arrived[1::2]))
+            arrived = [swapped(part, i) for i, part in enumerate(parts[1:], 2)]
+            ends.append((parts[:1] + arrived[0::2], arrived[1::2]))
         back = swapped(full[2], 1)
         loss = doubled_sum(functools.reduce(jnp.add, losses), "pack", packs)
         loss = doubled_sum(loss, "dp", groups)
     else:
         first = widths[0]
-        x_own, y_own = swapped(own, 2), swapped(own, 4)
-        x_other, y_other = swapped(other, 3), swapped(other, 5)
+        x_own, y_other = swapped(own, 2), swapped(other, 5)
+        x_other, y_own = swapped(other, 3), swapped(own, 4)
         sibling = swapped(other, 1)
-        me_later, x_own = together((me, x_own))
-        kv_other, table, group_counts = tabulated(me_later)
+        x_own, y_other = together((x_own, y_other))
         near = [x_own[:, :, :first], x_own[:, :, first:]]
-        x_own, y_own, x_other, y_other, sibling, kv_other, group_counts, table, near = together(
-            (x_own, y_own, x_other, y_other, sibling, kv_other, group_counts, table, near)
-        )
         far = [y_other[:, :, :first], y_other[:, :, first:]]
         diagonal = [swapped(near[0], 4), swapped(far[0], 2)]
+        me_later, x_other = together((me, x_other))
+        kv_other, table, group_counts = tabulated(me_later)
         kv_sibling = swapped(kv_other, 1)
         counts, scales = scales_of(group_counts)
-        diagonal, near, far, kv_sibling, scales = together(
-            (diagonal, near, far, kv_sibling, scales)
+        y_own, x_other, sibling, kv_sibling, scales, diagonal, near, far = together(
+            (y_own, x_other, sibling, kv_sibling, scales, diagonal, near, far)
         )
         later = [swapped(near[1], 4), swapped(far[1], 2)]
 
@@ -606,16 +605,16 @@
             return result[:3], result[3:], loss
 
         def forwarded(parts):
-            return [swapped(parts[6], 2), swapped(parts[7], 4)]
+            return [swapped(parts[5], 2), swapped(parts[6], 4)]
 
         def sent(parts):
-            return [swapped(parts[2], 2), swapped(parts[5], 5), swapped(parts[1], 1)]
+            return [swapped(parts[1], 2), swapped(parts[4], 5)]
 
         def merged(parts, relay):
-            return [swapped(parts[4] + relay[0], 4), swapped(parts[3] + relay[1], 3)]
+            return [swapped(parts[3] + relay[0], 4), swapped(parts[2] + relay[1], 3)]
 
         def sums(parts, direct, last):
-            return [parts[0], direct[0], last[0]], [direct[2], direct[1], last[1]]
+            return [parts[0], direct[0], last[0]], [direct[1], last[1]]
 
         full, parts_a, loss_a = attend(None, 0, diagonal, 0)
         later, full, parts_a = together((later, full, parts_a))
@@ -628,20 +627,19 @@
 
         last_a, relay_b = merged(parts_a, relay_a), forwarded(parts_b)
         loss = doubled_sum(loss_a + loss_b, "dp", groups)
-        loss = doubled_sum(loss, "pack", packs, 1, 4)
+        loss = doubled_sum(loss, "pack", packs, 1, 2)
         last_a, relay_b, loss, full = together((last_a, relay_b, loss, full))
 
         last_b, direct_b = merged(parts_b, relay_b), sent(parts_b)
         back = swapped(full[2], 1)
+        loss = doubled_sum(loss, "pack", packs, 2, 4)
+        last_b, direct_b, back, loss = together((last_b, direct_b, back, loss))
         loss = doubled_sum(loss, "pack", packs, 4)
-        last_b, direct_b, back, loss = together((last_b, direct_b, back, loss))
         ends = [sums(parts_a, direct_a, last_a), sums(parts_b, direct_b, last_b)]
 
     queries_gradient, keys_gradient, values_gradient = finish(
-        me, *ends[0], starts[0], dec_queries, back, full[:2]
+        me, ends, starts, packs, back, dec_queries, *full[:2]
     )
-    for (at, _), end in zip(spots[1:], ends[1:]):
-        (queries_gradient,) = finish(me, *end, at, dec_queries, None, (queries_gradient,))
     group_loss = (loss / counts)[0, :GROUPS]
     return (queries_gradient, keys_gradient, values_gradient, group_loss)
 

time: 135 us -> 135 us (level)
  starting transfers between devices: 29.3 us -> 38.6 us
  waiting for transfers between devices: 74.1 us -> 65.5 us
    ppermute x32 -> x30, starting transfers between devices: 29.3 us -> 38.6 us  [swap(): return lax.ppermute(array, axis_name, [(i, i ^ bits) for i in range(size)])]
    ppermute x32 -> x30, waiting for transfers between devices: 74.1 us -> 65.5 us  [swap(): return lax.ppermute(array, axis_name, [(i, i ^ bits) for i in range(size)])]
  transfers between devices with their start and end apart: 32 -> 30, of which waited for: 17 -> 13; matrix products, arithmetic and copies ran while one was open for 1% -> 1% of each run, Pallas kernels for 16% -> 17%
where the time goes in v4:
time: 135 us
  waiting for transfers between devices  65.5 us (49%)
  starting transfers between devices  38.6 us (29%)
  Pallas kernels  23.7 us (18%)
  local copies, waits for them, and re-layouts  4.87 us (4%)
  other arithmetic  1.55 us (1%)
    ppermute x30, waiting for transfers between devices, swap(): return lax.ppermute(array, axis_name, [(i, i ^ bits) for i in range(size)])  65.5 us
    ppermute x30, starting transfers between devices, swap(): return lax.ppermute(array, axis_name, [(i, i ^ bits) for i in range(size)])  38.6 us
    pallas_call x2, Pallas kernels, attention_chunk(): pl.pallas_call(functools.partial(attention_kernel, packs=packs, first=fir...  19.5 us
    unnamed x20, local copies, waits for them, and re-layouts  4.2 us
  transfers between devices with their start and end apart: 30, of which 13 were waited for; matrix products, arithmetic and copies ran while one was open for 1% of the time, Pallas kernels for 17%

profile of v4, /device:TPU:0, one launch (start us, length us, event | category | flops | bytes accessed | tf_op | source)
XLA Modules:
  0.0 135.0 jit_solution(15552221922202327472)
XLA Ops:
  3.7 2.4 %collective-permute-start.1 = (bf16[2,128,2048]{2,1,0:T(8,128)(2,1)S(1)}, bf16[2,128,2048]{2,1,0:T(8,128)(2,1)S(1)}, u32[]{:S(2)}, u32[]{:S(2)}) collective-permute-start(bf16[2,128,2048]{2,1,0:T(8,128)(2,1)S(1)} %get-tuple-element.89), channel_id=1, source_target_pairs={{0,3},{1,2},{2,1},{3,0},{4,7},{5,6},{6,5},{7,4},{8,11},{9,10},{10,... | collective-permute-start | bytes 3145736 | tf_op jit(solution)/shard_map/ppermute | solution.py:502
  6.1 1.8 %collective-permute-start.7 = (bf16[2,128,2048]{2,1,0:T(8,128)(2,1)S(1)}, bf16[2,128,2048]{2,1,0:T(8,128)(2,1)S(1)}, u32[]{:S(2)}, u32[]{:S(2)}) collective-permute-start(bf16[2,128,2048]{2,1,0:T(8,128)(2,1)S(1)} %get-tuple-element.89), channel_id=1, source_target_pairs={{0,5},{1,4},{2,7},{3,6},{4,1},{5,0},{6,3},{7,2},{8,13},{9,12},{10,... | collective-permute-start | bytes 3145736 | tf_op jit(solution)/shard_map/ppermute | solution.py:502
  8.4 21.2 %collective-permute-done.1.refs_3_ = bf16[2,128,2048]{2,1,0:T(8,128)(2,1)S(1)} collective-permute-done((bf16[2,128,2048]{2,1,0:T(8,128)(2,1)S(1)}, bf16[2,128,2048]{2,1,0:T(8,128)(2,1)S(1)}, u32[]{:S(2)}, u32[]{:S(2)}) %collective-permute-start.1) | collective-permute-done | bytes 1048608 | tf_op jit(solution)/shard_map/ppermute | solution.py:502
  31.3 2.1 %tabulate.1 = (bf16[2,256,2048]{2,1,0:T(8,128)(2,1)S(1)}, s32[4,8]{1,0:T(4,128)S(1)}, f32[1,128]{1,0:T(1,128)S(1)}) custom-call(s32[1]{0:T(128)} %bitcast.me_ref, s32[1,16]{1,0:T(1,128)S(1)} %copy-done.4, s32[1,16]{1,0:T(1,128)S(1)} %copy-done.5, s32[1,16]{1,0:T(1,128)S(1)} %copy-done.6, s32[1,16]{1,0:T(1,128)S(1)} %copy-done.7, s32[1,16]{1,0:T(1,128)S(1)} %bitcast.6, ...), custom_call_target="tpu_custom_call" | custom-call | bytes 2097152 | tf_op jit(solution)/shard_map/tabulate/pallas_call | solution.py:100
  34.7 1.7 %collective-permute-start = (bf16[2,128,2048]{2,1,0:T(8,128)(2,1)S(1)}, bf16[2,128,2048]{2,1,0:T(8,128)(2,1)S(1)}, u32[]{:S(2)}, u32[]{:S(2)}) collective-permute-start(bf16[2,128,2048]{2,1,0:T(8,128)(2,1)S(1)} %get-tuple-element.88.refs_0_), channel_id=1, source_target_pairs={{0,4},{1,5},{2,6},{3,7},{4,0},{5,1},{6,2},{7,3},{8,12},{9,13},{10,... | collective-permute-start | bytes 3145736 | tf_op jit(solution)/shard_map/ppermute | solution.py:502
  36.4 15.9 %collective-permute-done.6.refs_2_ = bf16[2,128,2048]{2,1,0:T(8,128)(2,1)S(1)} collective-permute-done((bf16[2,128,2048]{2,1,0:T(8,128)(2,1)S(1)}, bf16[2,128,2048]{2,1,0:T(8,128)(2,1)S(1)}, u32[]{:S(2)}, u32[]{:S(2)}) %collective-permute-start.6) | collective-permute-done | bytes 1048608 | tf_op jit(solution)/shard_map/ppermute | solution.py:502
  52.3 2.4 %collective-permute-start.4 = (f32[1,128]{1,0:T(1,128)S(1)}, f32[1,128]{1,0:T(1,128)S(1)}, u32[]{:S(2)}, u32[]{:S(2)}) collective-permute-start(f32[1,128]{1,0:T(1,128)S(1)} %get-tuple-element.93), channel_id=1, source_target_pairs={{0,8},{8,0},{16,24},{24,16},{1,9},{9,1},{17,25},{25,17},{2,10},{10... | collective-permute-start | bytes 1544 | tf_op jit(solution)/shard_map/ppermute | solution.py:502
  56.4 2.9 %collective-permute-start.5 = (f32[1,128]{1,0:T(1,128)S(1)}, f32[1,128]{1,0:T(1,128)S(1)}, u32[]{:S(2)}, u32[]{:S(2)}) collective-permute-start(f32[1,128]{1,0:T(1,128)S(1)} %add.38), channel_id=1, source_target_pairs={{0,16},{8,24},{16,0},{24,8},{1,17},{9,25},{17,1},{25,9},{2,18},{10... | collective-permute-start | bytes 1544 | tf_op jit(solution)/shard_map/ppermute | solution.py:502
  60.8 1.8 %collective-permute-start.9 = (bf16[2,128,1024]{2,1,0:T(8,128)(2,1)S(1)}, bf16[2,128,1024]{2,1,0:T(8,128)(2,1)S(1)}, u32[]{:S(2)}, u32[]{:S(2)}) collective-permute-start(bf16[2,128,1024]{2,1,0:T(8,128)(2,1)S(1)} %get-tuple-element.175), channel_id=1, source_target_pairs={{0,2},{1,3},{2,0},{3,1},{4,6},{5,7},{6,4},{7,5},{8,10},{9,11},{10,... | collective-permute-start | bytes 1572872 | tf_op jit(solution)/shard_map/ppermute | solution.py:502
  63.9 7.6 %collective-permute-done.8.refs_6_ = bf16[2,128,1024]{2,1,0:T(8,128)(2,1)S(1)} collective-permute-done((bf16[2,128,1024]{2,1,0:T(8,128)(2,1)S(1)}, bf16[2,128,1024]{2,1,0:T(8,128)(2,1)S(1)}, u32[]{:S(2)}, u32[]{:S(2)}) %collective-permute-start.8) | collective-permute-done | bytes 524320 | tf_op jit(solution)/shard_map/ppermute | solution.py:502
  76.0 9.6 %attention_chunk.2 = (bf16[256,4096]{1,0:T(8,128)(2,1)}, bf16[256,4096]{1,0:T(8,128)(2,1)}, bf16[640,2048]{1,0:T(8,128)(2,1)S(1)}, bf16[128,1024]{1,0:T(8,128)(2...) custom-call(s32[1]{0:T(128)} %bitcast.me_ref, ...), custom_call_target="tpu_custom_call" | custom-call | flops 33554432 | bytes 8388608 | tf_op jit(solution)/shard_map/attention_chunk/pallas_call | solution.py:410
  86.2 1.9 %collective-permute-start.12 = (bf16[128,1024]{1,0:T(8,128)(2,1)S(1)}, bf16[128,1024]{1,0:T(8,128)(2,1)S(1)}, u32[]{:S(2)}, u32[]{:S(2)}) collective-permute-start(bf16[128,1024]{1,0:T(8,128)(2,1)S(1)} %get-tuple-element.117), channel_id=1, source_target_pairs={{0,2},{1,3},{2,0},{3,1},{4,6},{5,7},{6,4},{7,5},{8,10},{9,11},{10,... | collective-permute-start | bytes 786440 | tf_op jit(solution)/shard_map/ppermute | solution.py:502
  89.1 9.8 %attention_chunk.3 = (bf16[256,4096]{1,0:T(8,128)(2,1)}, bf16[256,4096]{1,0:T(8,128)(2,1)}, bf16[640,2048]{1,0:T(8,128)(2,1)S(1)}, bf16[128,1024]{1,0:T(8,128)(2...) custom-call(s32[1]{0:T(128)} %bitcast.me_ref, ...), custom_call_target="tpu_custom_call", output_to_operand_aliasing={{0}: (14, {}), {1}: (15, {}), {2}: (16, {})} | custom-call | flops 33554432 | bytes 8388608 | tf_op jit(solution)/shard_map/attention_chunk/pallas_call | solution.py:410
  100.3 1.8 %collective-permute-start.17 = (bf16[128,1024]{1,0:T(8,128)(2,1)S(1)}, bf16[128,1024]{1,0:T(8,128)(2,1)S(1)}, u32[]{:S(2)}, u32[]{:S(2)}) collective-permute-start(bf16[128,1024]{1,0:T(8,128)(2,1)S(1)} %add.41), channel_id=1, source_target_pairs={{0,3},{1,2},{2,1},{3,0},{4,7},{5,6},{6,5},{7,4},{8,11},{9,10},{10,... | collective-permute-start | bytes 786440 | tf_op jit(solution)/shard_map/ppermute | solution.py:502
  105.5 2.0 %collective-permute-done.20 = f32[1,128]{1,0:T(1,128)S(1)} collective-permute-done((f32[1,128]{1,0:T(1,128)S(1)}, f32[1,128]{1,0:T(1,128)S(1)}, u32[]{:S(2)}, u32[]{:S(2)}) %collective-permute-start.20) | collective-permute-done | bytes 544 | tf_op jit(solution)/shard_map/ppermute | solution.py:502
  107.5 2.8 %collective-permute-start.21 = (f32[1,128]{1,0:T(1,128)S(1)}, f32[1,128]{1,0:T(1,128)S(1)}, u32[]{:S(2)}, u32[]{:S(2)}) collective-permute-start(f32[1,128]{1,0:T(1,128)S(1)} %add.43), channel_id=1, source_target_pairs={{0,16},{8,24},{16,0},{24,8},{1,17},{9,25},{17,1},{25,9},{2,18},{10... | collective-permute-start | bytes 1544 | tf_op jit(solution)/shard_map/ppermute | solution.py:502
  110.3 1.7 %collective-permute-done.21 = f32[1,128]{1,0:T(1,128)S(1)} collective-permute-done((f32[1,128]{1,0:T(1,128)S(1)}, f32[1,128]{1,0:T(1,128)S(1)}, u32[]{:S(2)}, u32[]{:S(2)}) %collective-permute-start.21) | collective-permute-done | bytes 544 | tf_op jit(solution)/shard_map/ppermute | solution.py:502
  113.1 1.6 %collective-permute-done.18 = bf16[128,1024]{1,0:T(8,128)(2,1)S(1)} collective-permute-done((bf16[128,1024]{1,0:T(8,128)(2,1)S(1)}, bf16[128,1024]{1,0:T(8,128)(2,1)S(1)}, u32[]{:S(2)}, u32[]{:S(2)}) %collective-permute-start.18) | collective-permute-done | bytes 262176 | tf_op jit(solution)/shard_map/ppermute | solution.py:502
  114.7 1.9 %collective-permute-start.28 = (f32[1,128]{1,0:T(1,128)S(1)}, f32[1,128]{1,0:T(1,128)S(1)}, u32[]{:S(2)}, u32[]{:S(2)}) collective-permute-start(f32[1,128]{1,0:T(1,128)S(1)} %add.45), channel_id=1, source_target_pairs={{0,2},{1,3},{2,0},{3,1},{4,6},{5,7},{6,4},{7,5},{8,10},{9,11},{10,... | collective-permute-start | bytes 1544 | tf_op jit(solution)/shard_map/ppermute | solution.py:502
  118.7 1.7 %collective-permute-start.24 = (bf16[128,1024]{1,0:T(8,128)(2,1)S(1)}, bf16[128,1024]{1,0:T(8,128)(2,1)S(1)}, u32[]{:S(2)}, u32[]{:S(2)}) collective-permute-start(bf16[128,1024]{1,0:T(8,128)(2,1)S(1)} %add.47), channel_id=1, source_target_pairs={{0,3},{1,2},{2,1},{3,0},{4,7},{5,6},{6,5},{7,4},{8,11},{9,10},{10,... | collective-permute-start | bytes 786440 | tf_op jit(solution)/shard_map/ppermute | solution.py:502
  120.4 5.4 %collective-permute-done.25.refs_6_ = bf16[128,1024]{1,0:T(8,128)(2,1)S(1)} collective-permute-done((bf16[128,1024]{1,0:T(8,128)(2,1)S(1)}, bf16[128,1024]{1,0:T(8,128)(2,1)S(1)}, u32[]{:S(2)}, u32[]{:S(2)}) %collective-permute-start.25) | collective-permute-done | bytes 262176 | tf_op jit(solution)/shard_map/ppermute | solution.py:502
  125.7 5.2 %collective-permute-done.23.refs_7_ = bf16[128,1024]{1,0:T(8,128)(2,1)S(1)} collective-permute-done((bf16[128,1024]{1,0:T(8,128)(2,1)S(1)}, bf16[128,1024]{1,0:T(8,128)(2,1)S(1)}, u32[]{:S(2)}, u32[]{:S(2)}) %collective-permute-start.23) | collective-permute-done | bytes 262176 | tf_op jit(solution)/shard_map/ppermute | solution.py:502
  131.0 1.6 %collective-permute-start.29 = (f32[1,128]{1,0:T(1,128)S(1)}, f32[1,128]{1,0:T(1,128)S(1)}, u32[]{:S(2)}, u32[]{:S(2)}) collective-permute-start(f32[1,128]{1,0:T(1,128)S(1)} %add.48), channel_id=1, source_target_pairs={{0,4},{1,5},{2,6},{3,7},{4,0},{5,1},{6,2},{7,3},{8,12},{9,13},{10,... | collective-permute-start | bytes 1544 | tf_op jit(solution)/shard_map/ppermute | solution.py:502
  132.6 1.7 %finish.1 = (bf16[128,4096]{1,0:T(8,128)(2,1)}, bf16[256,4096]{1,0:T(8,128)(2,1)}, bf16[256,4096]{1,0:T(8,128)(2,1)}) custom-call(s32[1]{0:T(128)} %bitcast.me_ref, bf16[128,1024]{1,0:T(8,128)(2,1)S(1)} %get-tuple-element.116.refs_0_, bf16[128,1024]{1,0:T(8,128)(2,1)S(1)} %collective-permute-done.14.refs_1_, ...), custom_call_target="tpu_custom_call", output_to_operand_aliasing={{1}: (12, {}), {2}: (13, {})} | custom-call | bytes 2097152 | tf_op jit(solution)/shard_map/finish/pallas_call | solution.py:483
  (78 shorter events, 25.6 us)
Async XLA Ops:
  3.7 26.0 %collective-permute-start.1 = (bf16[2,128,2048]{2,1,0:T(8,128)(2,1)S(1)}, bf16[2,128,2048]{2,1,0:T(8,128)(2,1)S(1)}, u32[]{:S(2)}, u32[]{:S(2)}) collective-permute-start(bf16[2,128,2048]{2,1,0:T(8,128)(2,1)S(1)} %get-tuple-element.89), channel_id=1, source_target_pairs={{0,3},{1,2},{2,1},{3,0},{4,7},{5,6},{6,5},{7,4},{8,11},{9,10},{10,... | collective-permute-start | bytes 3145736 | tf_op jit(solution)/shard_map/ppermute | solution.py:502
  6.1 30.3 %collective-permute-start.7 = (bf16[2,128,2048]{2,1,0:T(8,128)(2,1)S(1)}, bf16[2,128,2048]{2,1,0:T(8,128)(2,1)S(1)}, u32[]{:S(2)}, u32[]{:S(2)}) collective-permute-start(bf16[2,128,2048]{2,1,0:T(8,128)(2,1)S(1)} %get-tuple-element.89), channel_id=1, source_target_pairs={{0,5},{1,4},{2,7},{3,6},{4,1},{5,0},{6,3},{7,2},{8,13},{9,12},{10,... | collective-permute-start | bytes 3145736 | tf_op jit(solution)/shard_map/ppermute | solution.py:502
  7.9 44.4 %collective-permute-start.6 = (bf16[2,128,2048]{2,1,0:T(8,128)(2,1)S(1)}, bf16[2,128,2048]{2,1,0:T(8,128)(2,1)S(1)}, u32[]{:S(2)}, u32[]{:S(2)}) collective-permute-start(bf16[2,128,2048]{2,1,0:T(8,128)(2,1)S(1)} %get-tuple-element.88.refs_0_), channel_id=1, source_target_pairs={{0,2},{1,3},{2,0},{3,1},{4,6},{5,7},{6,4},{7,5},{8,10},{9,11},{10,... | collective-permute-start | bytes 3145736 | tf_op jit(solution)/shard_map/ppermute | solution.py:502
  33.4 39.6 %collective-permute-start.3 = (bf16[2,256,2048]{2,1,0:T(8,128)(2,1)S(1)}, bf16[2,256,2048]{2,1,0:T(8,128)(2,1)S(1)}, u32[]{:S(2)}, u32[]{:S(2)}) collective-permute-start(bf16[2,256,2048]{2,1,0:T(8,128)(2,1)S(1)} %get-tuple-element.92), channel_id=1, source_target_pairs={{0,1},{1,0},{2,3},{3,2},{4,5},{5,4},{6,7},{7,6},{8,9},{9,8},{10,11... | collective-permute-start | bytes 6291464 | tf_op jit(solution)/shard_map/ppermute | solution.py:502
  34.6 29.2 %collective-permute-start.2 = (bf16[2,128,2048]{2,1,0:T(8,128)(2,1)S(1)}, bf16[2,128,2048]{2,1,0:T(8,128)(2,1)S(1)}, u32[]{:S(2)}, u32[]{:S(2)}) collective-permute-start(bf16[2,128,2048]{2,1,0:T(8,128)(2,1)S(1)} %get-tuple-element.89), channel_id=1, source_target_pairs={{0,1},{1,0},{2,3},{3,2},{4,5},{5,4},{6,7},{7,6},{8,9},{9,8},{10,11... | collective-permute-start | bytes 3145736 | tf_op jit(solution)/shard_map/ppermute | solution.py:502
  34.7 29.2 %collective-permute-start = (bf16[2,128,2048]{2,1,0:T(8,128)(2,1)S(1)}, bf16[2,128,2048]{2,1,0:T(8,128)(2,1)S(1)}, u32[]{:S(2)}, u32[]{:S(2)}) collective-permute-start(bf16[2,128,2048]{2,1,0:T(8,128)(2,1)S(1)} %get-tuple-element.88.refs_0_), channel_id=1, source_target_pairs={{0,4},{1,5},{2,6},{3,7},{4,0},{5,1},{6,2},{7,3},{8,12},{9,13},{10,... | collective-permute-start | bytes 3145736 | tf_op jit(solution)/shard_map/ppermute | solution.py:502
  54.8 16.7 %collective-permute-start.8 = (bf16[2,128,1024]{2,1,0:T(8,128)(2,1)S(1)}, bf16[2,128,1024]{2,1,0:T(8,128)(2,1)S(1)}, u32[]{:S(2)}, u32[]{:S(2)}) collective-permute-start(bf16[2,128,1024]{2,1,0:T(8,128)(2,1)S(1)} %get-tuple-element.177), channel_id=1, source_target_pairs={{0,4},{1,5},{2,6},{3,7},{4,0},{5,1},{6,2},{7,3},{8,12},{9,13},{10,... | collective-permute-start | bytes 1572872 | tf_op jit(solution)/shard_map/ppermute | solution.py:502
  56.4 4.4 %collective-permute-start.5 = (f32[1,128]{1,0:T(1,128)S(1)}, f32[1,128]{1,0:T(1,128)S(1)}, u32[]{:S(2)}, u32[]{:S(2)}) collective-permute-start(f32[1,128]{1,0:T(1,128)S(1)} %add.38), channel_id=1, source_target_pairs={{0,16},{8,24},{16,0},{24,8},{1,17},{9,25},{17,1},{25,9},{2,18},{10... | collective-permute-start | bytes 1544 | tf_op jit(solution)/shard_map/ppermute | solution.py:502
  60.8 12.2 %collective-permute-start.9 = (bf16[2,128,1024]{2,1,0:T(8,128)(2,1)S(1)}, bf16[2,128,1024]{2,1,0:T(8,128)(2,1)S(1)}, u32[]{:S(2)}, u32[]{:S(2)}) collective-permute-start(bf16[2,128,1024]{2,1,0:T(8,128)(2,1)S(1)} %get-tuple-element.175), channel_id=1, source_target_pairs={{0,2},{1,3},{2,0},{3,1},{4,6},{5,7},{6,4},{7,5},{8,10},{9,11},{10,... | collective-permute-start | bytes 1572872 | tf_op jit(solution)/shard_map/ppermute | solution.py:502
  73.0 12.7 %collective-permute-start.10 = (bf16[2,128,1024]{2,1,0:T(8,128)(2,1)S(1)}, bf16[2,128,1024]{2,1,0:T(8,128)(2,1)S(1)}, u32[]{:S(2)}, u32[]{:S(2)}) collective-permute-start(bf16[2,128,1024]{2,1,0:T(8,128)(2,1)S(1)} %get-tuple-element.96), channel_id=1, source_target_pairs={{0,4},{1,5},{2,6},{3,7},{4,0},{5,1},{6,2},{7,3},{8,12},{9,13},{10,... | collective-permute-start | bytes 1572872 | tf_op jit(solution)/shard_map/ppermute | solution.py:502
  74.5 11.7 %collective-permute-start.11 = (bf16[2,128,1024]{2,1,0:T(8,128)(2,1)S(1)}, bf16[2,128,1024]{2,1,0:T(8,128)(2,1)S(1)}, u32[]{:S(2)}, u32[]{:S(2)}) collective-permute-start(bf16[2,128,1024]{2,1,0:T(8,128)(2,1)S(1)} %get-tuple-element.97), channel_id=1, source_target_pairs={{0,2},{1,3},{2,0},{3,1},{4,6},{5,7},{6,4},{7,5},{8,10},{9,11},{10,... | collective-permute-start | bytes 1572872 | tf_op jit(solution)/shard_map/ppermute | solution.py:502
  86.2 12.8 %collective-permute-start.12 = (bf16[128,1024]{1,0:T(8,128)(2,1)S(1)}, bf16[128,1024]{1,0:T(8,128)(2,1)S(1)}, u32[]{:S(2)}, u32[]{:S(2)}) collective-permute-start(bf16[128,1024]{1,0:T(8,128)(2,1)S(1)} %get-tuple-element.117), channel_id=1, source_target_pairs={{0,2},{1,3},{2,0},{3,1},{4,6},{5,7},{6,4},{7,5},{8,10},{9,11},{10,... | collective-permute-start | bytes 786440 | tf_op jit(solution)/shard_map/ppermute | solution.py:502
  88.1 10.9 %collective-permute-start.13 = (bf16[128,1024]{1,0:T(8,128)(2,1)S(1)}, bf16[128,1024]{1,0:T(8,128)(2,1)S(1)}, u32[]{:S(2)}, u32[]{:S(2)}) collective-permute-start(bf16[128,1024]{1,0:T(8,128)(2,1)S(1)} %get-tuple-element.118), channel_id=1, source_target_pairs={{0,4},{1,5},{2,6},{3,7},{4,0},{5,1},{6,2},{7,3},{8,12},{9,13},{10,... | collective-permute-start | bytes 786440 | tf_op jit(solution)/shard_map/ppermute | solution.py:502
  88.5 10.5 %collective-permute-start.14 = (bf16[128,1024]{1,0:T(8,128)(2,1)S(1)}, bf16[128,1024]{1,0:T(8,128)(2,1)S(1)}, u32[]{:S(2)}, u32[]{:S(2)}) collective-permute-start(bf16[128,1024]{1,0:T(8,128)(2,1)S(1)} %get-tuple-element.119), channel_id=1, source_target_pairs={{0,2},{1,3},{2,0},{3,1},{4,6},{5,7},{6,4},{7,5},{8,10},{9,11},{10,... | collective-permute-start | bytes 786440 | tf_op jit(solution)/shard_map/ppermute | solution.py:502
  89.1 9.9 %collective-permute-start.15 = (bf16[128,1024]{1,0:T(8,128)(2,1)S(1)}, bf16[128,1024]{1,0:T(8,128)(2,1)S(1)}, u32[]{:S(2)}, u32[]{:S(2)}) collective-permute-start(bf16[128,1024]{1,0:T(8,128)(2,1)S(1)} %get-tuple-element.120), channel_id=1, source_target_pairs={{0,5},{1,4},{2,7},{3,6},{4,1},{5,0},{6,3},{7,2},{8,13},{9,12},{10,... | collective-permute-start | bytes 786440 | tf_op jit(solution)/shard_map/ppermute | solution.py:502
  99.1 13.9 %collective-permute-start.16 = (bf16[128,1024]{1,0:T(8,128)(2,1)S(1)}, bf16[128,1024]{1,0:T(8,128)(2,1)S(1)}, u32[]{:S(2)}, u32[]{:S(2)}) collective-permute-start(bf16[128,1024]{1,0:T(8,128)(2,1)S(1)} %add.40), channel_id=1, source_target_pairs={{0,4},{1,5},{2,6},{3,7},{4,0},{5,1},{6,2},{7,3},{8,12},{9,13},{10,... | collective-permute-start | bytes 786440 | tf_op jit(solution)/shard_map/ppermute | solution.py:502
  100.3 12.7 %collective-permute-start.17 = (bf16[128,1024]{1,0:T(8,128)(2,1)S(1)}, bf16[128,1024]{1,0:T(8,128)(2,1)S(1)}, u32[]{:S(2)}, u32[]{:S(2)}) collective-permute-start(bf16[128,1024]{1,0:T(8,128)(2,1)S(1)} %add.41), channel_id=1, source_target_pairs={{0,3},{1,2},{2,1},{3,0},{4,7},{5,6},{6,5},{7,4},{8,11},{9,10},{10,... | collective-permute-start | bytes 786440 | tf_op jit(solution)/shard_map/ppermute | solution.py:502
  102.2 12.5 %collective-permute-start.18 = (bf16[128,1024]{1,0:T(8,128)(2,1)S(1)}, bf16[128,1024]{1,0:T(8,128)(2,1)S(1)}, u32[]{:S(2)}, u32[]{:S(2)}) collective-permute-start(bf16[128,1024]{1,0:T(8,128)(2,1)S(1)} %get-tuple-element.142), channel_id=1, source_target_pairs={{0,2},{1,3},{2,0},{3,1},{4,6},{5,7},{6,4},{7,5},{8,10},{9,11},{10,... | collective-permute-start | bytes 786440 | tf_op jit(solution)/shard_map/ppermute | solution.py:502
  102.8 11.9 %collective-permute-start.19 = (bf16[128,1024]{1,0:T(8,128)(2,1)S(1)}, bf16[128,1024]{1,0:T(8,128)(2,1)S(1)}, u32[]{:S(2)}, u32[]{:S(2)}) collective-permute-start(bf16[128,1024]{1,0:T(8,128)(2,1)S(1)} %get-tuple-element.143), channel_id=1, source_target_pairs={{0,4},{1,5},{2,6},{3,7},{4,0},{5,1},{6,2},{7,3},{8,12},{9,13},{10,... | collective-permute-start | bytes 786440 | tf_op jit(solution)/shard_map/ppermute | solution.py:502
  114.7 16.3 %collective-permute-start.27 = (bf16[640,2048]{1,0:T(8,128)(2,1)S(1)}, bf16[640,2048]{1,0:T(8,128)(2,1)S(1)}, u32[]{:S(2)}, u32[]{:S(2)}) collective-permute-start(bf16[640,2048]{1,0:T(8,128)(2,1)S(1)} %get-tuple-element.159), channel_id=1, source_target_pairs={{0,1},{1,0},{2,3},{3,2},{4,5},{5,4},{6,7},{7,6},{8,9},{9,8},{10,11... | collective-permute-start | bytes 7864328 | tf_op jit(solution)/shard_map/ppermute | solution.py:502
  116.6 9.1 %collective-permute-start.25 = (bf16[128,1024]{1,0:T(8,128)(2,1)S(1)}, bf16[128,1024]{1,0:T(8,128)(2,1)S(1)}, u32[]{:S(2)}, u32[]{:S(2)}) collective-permute-start(bf16[128,1024]{1,0:T(8,128)(2,1)S(1)} %get-tuple-element.157), channel_id=1, source_target_pairs={{0,2},{1,3},{2,0},{3,1},{4,6},{5,7},{6,4},{7,5},{8,10},{9,11},{10,... | collective-permute-start | bytes 786440 | tf_op jit(solution)/shard_map/ppermute | solution.py:502
  116.7 9.0 %collective-permute-start.26 = (bf16[128,1024]{1,0:T(8,128)(2,1)S(1)}, bf16[128,1024]{1,0:T(8,128)(2,1)S(1)}, u32[]{:S(2)}, u32[]{:S(2)}) collective-permute-start(bf16[128,1024]{1,0:T(8,128)(2,1)S(1)} %get-tuple-element.158), channel_id=1, source_target_pairs={{0,5},{1,4},{2,7},{3,6},{4,1},{5,0},{6,3},{7,2},{8,13},{9,12},{10,... | collective-permute-start | bytes 786440 | tf_op jit(solution)/shard_map/ppermute | solution.py:502
  118.0 13.0 %collective-permute-start.23 = (bf16[128,1024]{1,0:T(8,128)(2,1)S(1)}, bf16[128,1024]{1,0:T(8,128)(2,1)S(1)}, u32[]{:S(2)}, u32[]{:S(2)}) collective-permute-start(bf16[128,1024]{1,0:T(8,128)(2,1)S(1)} %add.46), channel_id=1, source_target_pairs={{0,4},{1,5},{2,6},{3,7},{4,0},{5,1},{6,2},{7,3},{8,12},{9,13},{10,... | collective-permute-start | bytes 786440 | tf_op jit(solution)/shard_map/ppermute | solution.py:502
  118.7 12.3 %collective-permute-start.24 = (bf16[128,1024]{1,0:T(8,128)(2,1)S(1)}, bf16[128,1024]{1,0:T(8,128)(2,1)S(1)}, u32[]{:S(2)}, u32[]{:S(2)}) collective-permute-start(bf16[128,1024]{1,0:T(8,128)(2,1)S(1)} %add.47), channel_id=1, source_target_pairs={{0,3},{1,2},{2,1},{3,0},{4,7},{5,6},{6,5},{7,4},{8,11},{9,10},{10,... | collective-permute-start | bytes 786440 | tf_op jit(solution)/shard_map/ppermute | solution.py:502
  (16 other events, 196.3 us)

commit v5 on v4

--- a/solution.py
+++ b/solution.py
@@ -579,19 +579,21 @@
         loss = doubled_sum(loss, "dp", groups)
     else:
         first = widths[0]
-        x_own, y_other = swapped(own, 2), swapped(other, 5)
-        x_other, y_own = swapped(other, 3), swapped(own, 4)
+        x_own, y_own = swapped(own, 2), swapped(own, 4)
+        x_other, y_other = swapped(other, 3), swapped(other, 5)
         sibling = swapped(other, 1)
-        x_own, y_other = together((x_own, y_other))
+        me_later, x_own = together((me, x_own))
+        kv_other, table, group_counts = tabulated(me_later)
         near = [x_own[:, :, :first], x_own[:, :, first:]]
+        x_own, y_own, x_other, y_other, sibling, kv_other, group_counts, table, near = together(
+            (x_own, y_own, x_other, y_other, sibling, kv_other, group_counts, table, near)
+        )
         far = [y_other[:, :, :first], y_other[:, :, first:]]
         diagonal = [swapped(near[0], 4), swapped(far[0], 2)]
-        me_later, x_other = together((me, x_other))
-        kv_other, table, group_counts = tabulated(me_later)
         kv_sibling = swapped(kv_other, 1)
         counts, scales = scales_of(group_counts)
-        y_own, x_other, sibling, kv_sibling, scales, diagonal, near, far = together(
-            (y_own, x_other, sibling, kv_sibling, scales, diagonal, near, far)
+        diagonal, near, far, kv_sibling, scales = together(
+            (diagonal, near, far, kv_sibling, scales)
         )
         later = [swapped(near[1], 4), swapped(far[1], 2)]
 

time: 135 us -> 133 us (0.985)
  starting transfers between devices: 38.6 us -> 30.6 us
  waiting for transfers between devices: 65.5 us -> 71 us
    ppermute x30, starting transfers between devices: 38.6 us -> 30.6 us  [swap(): return lax.ppermute(array, axis_name, [(i, i ^ bits) for i in range(size)])]
    ppermute x30, waiting for transfers between devices: 65.5 us -> 71 us  [swap(): return lax.ppermute(array, axis_name, [(i, i ^ bits) for i in range(size)])]
  transfers between devices with their start and end apart: 30 -> 30, of which waited for: 13 -> 17; matrix products, arithmetic and copies ran while one was open for 1% -> 1% of each run, Pallas kernels for 17% -> 18%
where the time goes in v5:
time: 133 us
  waiting for transfers between devices  71 us (53%)
  starting transfers between devices  30.6 us (23%)
  Pallas kernels  23.7 us (18%)
  local copies, waits for them, and re-layouts  4.88 us (4%)
  other arithmetic  1.55 us (1%)
    ppermute x30, waiting for transfers between devices, swap(): return lax.ppermute(array, axis_name, [(i, i ^ bits) for i in range(size)])  71 us
    ppermute x30, starting transfers between devices, swap(): return lax.ppermute(array, axis_name, [(i, i ^ bits) for i in range(size)])  30.6 us
    pallas_call x2, Pallas kernels, attention_chunk(): pl.pallas_call(functools.partial(attention_kernel, packs=packs, first=fir...  19.5 us
    unnamed x20, local copies, waits for them, and re-layouts  4.21 us
  transfers between devices with their start and end apart: 30, of which 17 were waited for; matrix products, arithmetic and copies ran while one was open for 1% of the time, Pallas kernels for 18%

profile of v5, /device:TPU:0, one launch (start us, length us, event | category | flops | bytes accessed | tf_op | source)
XLA Modules:
  0.0 132.6 jit_solution(8990303692584007576)
XLA Ops:
  3.7 3.0 %collective-permute-start = (bf16[2,128,2048]{2,1,0:T(8,128)(2,1)S(1)}, bf16[2,128,2048]{2,1,0:T(8,128)(2,1)S(1)}, u32[]{:S(2)}, u32[]{:S(2)}) collective-permute-start(bf16[2,128,2048]{2,1,0:T(8,128)(2,1)S(1)} %get-tuple-element.93.refs_0_), channel_id=1, source_target_pairs={{0,2},{1,3},{2,0},{3,1},{4,6},{5,7},{6,4},{7,5},{8,10},{9,11},{10,... | collective-permute-start | bytes 3145736 | tf_op jit(solution)/shard_map/ppermute | solution.py:502
  6.7 1.6 %collective-permute-start.3 = (bf16[2,128,2048]{2,1,0:T(8,128)(2,1)S(1)}, bf16[2,128,2048]{2,1,0:T(8,128)(2,1)S(1)}, u32[]{:S(2)}, u32[]{:S(2)}) collective-permute-start(bf16[2,128,2048]{2,1,0:T(8,128)(2,1)S(1)} %get-tuple-element.95), channel_id=1, source_target_pairs={{0,5},{1,4},{2,7},{3,6},{4,1},{5,0},{6,3},{7,2},{8,13},{9,12},{10,... | collective-permute-start | bytes 3145736 | tf_op jit(solution)/shard_map/ppermute | solution.py:502
  8.8 21.8 %collective-permute-done.refs_2_ = bf16[2,128,2048]{2,1,0:T(8,128)(2,1)S(1)} collective-permute-done((bf16[2,128,2048]{2,1,0:T(8,128)(2,1)S(1)}, bf16[2,128,2048]{2,1,0:T(8,128)(2,1)S(1)}, u32[]{:S(2)}, u32[]{:S(2)}) %collective-permute-start) | collective-permute-done | bytes 1048608 | tf_op jit(solution)/shard_map/ppermute | solution.py:502
  30.7 1.6 %copy-done.1 = bf16[256,4096]{1,0:T(8,128)(2,1)S(1)} copy-done((bf16[256,4096]{1,0:T(8,128)(2,1)S(1)}, bf16[256,4096]{1,0:T(8,128)(2,1)}, u32[]{:S(2)}) %copy-start.1) | copy-done | bytes 2097176
  32.3 2.1 %tabulate.1 = (bf16[2,256,2048]{2,1,0:T(8,128)(2,1)S(1)}, s32[4,8]{1,0:T(4,128)S(1)}, f32[1,128]{1,0:T(1,128)S(1)}) custom-call(s32[1]{0:T(128)} %bitcast.me_ref, s32[1,16]{1,0:T(1,128)S(1)} %copy-done.4, s32[1,16]{1,0:T(1,128)S(1)} %copy-done.5, s32[1,16]{1,0:T(1,128)S(1)} %copy-done.6, s32[1,16]{1,0:T(1,128)S(1)} %copy-done.7, s32[1,16]{1,0:T(1,128)S(1)} %bitcast.6, ...), custom_call_target="tpu_custom_call" | custom-call | bytes 2097152 | tf_op jit(solution)/shard_map/tabulate/pallas_call | solution.py:100
  34.5 17.1 %collective-permute-done.2.refs_3_ = bf16[2,128,2048]{2,1,0:T(8,128)(2,1)S(1)} collective-permute-done((bf16[2,128,2048]{2,1,0:T(8,128)(2,1)S(1)}, bf16[2,128,2048]{2,1,0:T(8,128)(2,1)S(1)}, u32[]{:S(2)}, u32[]{:S(2)}) %collective-permute-start.2) | collective-permute-done | bytes 1048608 | tf_op jit(solution)/shard_map/ppermute | solution.py:502
  51.5 3.0 %collective-permute-done.1.refs_4_ = bf16[2,128,2048]{2,1,0:T(8,128)(2,1)S(1)} collective-permute-done((bf16[2,128,2048]{2,1,0:T(8,128)(2,1)S(1)}, bf16[2,128,2048]{2,1,0:T(8,128)(2,1)S(1)}, u32[]{:S(2)}, u32[]{:S(2)}) %collective-permute-start.1) | collective-permute-done | bytes 1048608 | tf_op jit(solution)/shard_map/ppermute | solution.py:502
  56.8 1.6 %collective-permute-start.8 = (f32[1,128]{1,0:T(1,128)S(1)}, f32[1,128]{1,0:T(1,128)S(1)}, u32[]{:S(2)}, u32[]{:S(2)}) collective-permute-start(f32[1,128]{1,0:T(1,128)S(1)} %get-tuple-element.104), channel_id=1, source_target_pairs={{0,8},{8,0},{16,24},{24,16},{1,9},{9,1},{17,25},{25,17},{2,10},{10... | collective-permute-start | bytes 1544 | tf_op jit(solution)/shard_map/ppermute | solution.py:502
  58.4 2.0 %collective-permute-done.8 = f32[1,128]{1,0:T(1,128)S(1)} collective-permute-done((f32[1,128]{1,0:T(1,128)S(1)}, f32[1,128]{1,0:T(1,128)S(1)}, u32[]{:S(2)}, u32[]{:S(2)}) %collective-permute-start.8) | collective-permute-done | bytes 544 | tf_op jit(solution)/shard_map/ppermute | solution.py:502
  60.4 2.6 %collective-permute-start.9 = (f32[1,128]{1,0:T(1,128)S(1)}, f32[1,128]{1,0:T(1,128)S(1)}, u32[]{:S(2)}, u32[]{:S(2)}) collective-permute-start(f32[1,128]{1,0:T(1,128)S(1)} %add.38), channel_id=1, source_target_pairs={{0,16},{8,24},{16,0},{24,8},{1,17},{9,25},{17,1},{25,9},{2,18},{10... | collective-permute-start | bytes 1544 | tf_op jit(solution)/shard_map/ppermute | solution.py:502
  65.5 3.5 %collective-permute-done.5.refs_6_ = bf16[2,128,1024]{2,1,0:T(8,128)(2,1)S(1)} collective-permute-done((bf16[2,128,1024]{2,1,0:T(8,128)(2,1)S(1)}, bf16[2,128,1024]{2,1,0:T(8,128)(2,1)S(1)}, u32[]{:S(2)}, u32[]{:S(2)}) %collective-permute-start.5) | collective-permute-done | bytes 524320 | tf_op jit(solution)/shard_map/ppermute | solution.py:502
  71.3 9.7 %attention_chunk.2 = (bf16[256,4096]{1,0:T(8,128)(2,1)}, bf16[256,4096]{1,0:T(8,128)(2,1)}, bf16[640,2048]{1,0:T(8,128)(2,1)S(1)}, bf16[128,1024]{1,0:T(8,128)(2...) custom-call(s32[1]{0:T(128)} %bitcast.me_ref, ...), custom_call_target="tpu_custom_call" | custom-call | flops 33554432 | bytes 8388608 | tf_op jit(solution)/shard_map/attention_chunk/pallas_call | solution.py:410
  80.9 2.6 %collective-permute-done.10.refs_6_ = bf16[2,128,1024]{2,1,0:T(8,128)(2,1)S(1)} collective-permute-done((bf16[2,128,1024]{2,1,0:T(8,128)(2,1)S(1)}, bf16[2,128,1024]{2,1,0:T(8,128)(2,1)S(1)}, u32[]{:S(2)}, u32[]{:S(2)}) %collective-permute-start.10) | collective-permute-done | bytes 524320 | tf_op jit(solution)/shard_map/ppermute | solution.py:502
  84.3 1.6 %collective-permute-start.13 = (bf16[128,1024]{1,0:T(8,128)(2,1)S(1)}, bf16[128,1024]{1,0:T(8,128)(2,1)S(1)}, u32[]{:S(2)}, u32[]{:S(2)}) collective-permute-start(bf16[128,1024]{1,0:T(8,128)(2,1)S(1)} %get-tuple-element.128), channel_id=1, source_target_pairs={{0,4},{1,5},{2,6},{3,7},{4,0},{5,1},{6,2},{7,3},{8,12},{9,13},{10,... | collective-permute-start | bytes 786440 | tf_op jit(solution)/shard_map/ppermute | solution.py:502
  87.3 9.8 %attention_chunk.3 = (bf16[256,4096]{1,0:T(8,128)(2,1)}, bf16[256,4096]{1,0:T(8,128)(2,1)}, bf16[640,2048]{1,0:T(8,128)(2,1)S(1)}, bf16[128,1024]{1,0:T(8,128)(2...) custom-call(s32[1]{0:T(128)} %bitcast.me_ref, ...), custom_call_target="tpu_custom_call", output_to_operand_aliasing={{0}: (14, {}), {1}: (15, {}), {2}: (16, {})} | custom-call | flops 33554432 | bytes 8388608 | tf_op jit(solution)/shard_map/attention_chunk/pallas_call | solution.py:410
  97.9 1.6 %collective-permute-start.17 = (bf16[128,1024]{1,0:T(8,128)(2,1)S(1)}, bf16[128,1024]{1,0:T(8,128)(2,1)S(1)}, u32[]{:S(2)}, u32[]{:S(2)}) collective-permute-start(bf16[128,1024]{1,0:T(8,128)(2,1)S(1)} %add.41), channel_id=1, source_target_pairs={{0,3},{1,2},{2,1},{3,0},{4,7},{5,6},{6,5},{7,4},{8,11},{9,10},{10,... | collective-permute-start | bytes 786440 | tf_op jit(solution)/shard_map/ppermute | solution.py:502
  101.5 1.6 %collective-permute-start.20 = (f32[1,128]{1,0:T(1,128)S(1)}, f32[1,128]{1,0:T(1,128)S(1)}, u32[]{:S(2)}, u32[]{:S(2)}) collective-permute-start(f32[1,128]{1,0:T(1,128)S(1)} %add.42), channel_id=1, source_target_pairs={{0,8},{8,0},{16,24},{24,16},{1,9},{9,1},{17,25},{25,17},{2,10},{10... | collective-permute-start | bytes 1544 | tf_op jit(solution)/shard_map/ppermute | solution.py:502
  103.1 2.0 %collective-permute-done.20 = f32[1,128]{1,0:T(1,128)S(1)} collective-permute-done((f32[1,128]{1,0:T(1,128)S(1)}, f32[1,128]{1,0:T(1,128)S(1)}, u32[]{:S(2)}, u32[]{:S(2)}) %collective-permute-start.20) | collective-permute-done | bytes 544 | tf_op jit(solution)/shard_map/ppermute | solution.py:502
  105.1 2.6 %collective-permute-start.21 = (f32[1,128]{1,0:T(1,128)S(1)}, f32[1,128]{1,0:T(1,128)S(1)}, u32[]{:S(2)}, u32[]{:S(2)}) collective-permute-start(f32[1,128]{1,0:T(1,128)S(1)} %add.43), channel_id=1, source_target_pairs={{0,16},{8,24},{16,0},{24,8},{1,17},{9,25},{17,1},{25,9},{2,18},{10... | collective-permute-start | bytes 1544 | tf_op jit(solution)/shard_map/ppermute | solution.py:502
  107.7 1.8 %collective-permute-done.21 = f32[1,128]{1,0:T(1,128)S(1)} collective-permute-done((f32[1,128]{1,0:T(1,128)S(1)}, f32[1,128]{1,0:T(1,128)S(1)}, u32[]{:S(2)}, u32[]{:S(2)}) %collective-permute-start.21) | collective-permute-done | bytes 544 | tf_op jit(solution)/shard_map/ppermute | solution.py:502
  110.6 1.6 %collective-permute-done.18 = bf16[128,1024]{1,0:T(8,128)(2,1)S(1)} collective-permute-done((bf16[128,1024]{1,0:T(8,128)(2,1)S(1)}, bf16[128,1024]{1,0:T(8,128)(2,1)S(1)}, u32[]{:S(2)}, u32[]{:S(2)}) %collective-permute-start.18) | collective-permute-done | bytes 262176 | tf_op jit(solution)/shard_map/ppermute | solution.py:502
  117.3 5.4 %collective-permute-done.25.refs_6_ = bf16[128,1024]{1,0:T(8,128)(2,1)S(1)} collective-permute-done((bf16[128,1024]{1,0:T(8,128)(2,1)S(1)}, bf16[128,1024]{1,0:T(8,128)(2,1)S(1)}, u32[]{:S(2)}, u32[]{:S(2)}) %collective-permute-start.25) | collective-permute-done | bytes 262176 | tf_op jit(solution)/shard_map/ppermute | solution.py:502
  122.7 5.7 %collective-permute-done.23.refs_7_ = bf16[128,1024]{1,0:T(8,128)(2,1)S(1)} collective-permute-done((bf16[128,1024]{1,0:T(8,128)(2,1)S(1)}, bf16[128,1024]{1,0:T(8,128)(2,1)S(1)}, u32[]{:S(2)}, u32[]{:S(2)}) %collective-permute-start.23) | collective-permute-done | bytes 262176 | tf_op jit(solution)/shard_map/ppermute | solution.py:502
  130.0 1.7 %finish.1 = (bf16[128,4096]{1,0:T(8,128)(2,1)}, bf16[256,4096]{1,0:T(8,128)(2,1)}, bf16[256,4096]{1,0:T(8,128)(2,1)}) custom-call(s32[1]{0:T(128)} %bitcast.me_ref, bf16[128,1024]{1,0:T(8,128)(2,1)S(1)} %get-tuple-element.126.refs_0_, bf16[128,1024]{1,0:T(8,128)(2,1)S(1)} %collective-permute-done.14.refs_1_, ...), custom_call_target="tpu_custom_call", output_to_operand_aliasing={{1}: (12, {}), {2}: (13, {})} | custom-call | bytes 2097152 | tf_op jit(solution)/shard_map/finish/pallas_call | solution.py:483
  (78 shorter events, 24.2 us)
Async XLA Ops:
  3.7 27.0 %collective-permute-start = (bf16[2,128,2048]{2,1,0:T(8,128)(2,1)S(1)}, bf16[2,128,2048]{2,1,0:T(8,128)(2,1)S(1)}, u32[]{:S(2)}, u32[]{:S(2)}) collective-permute-start(bf16[2,128,2048]{2,1,0:T(8,128)(2,1)S(1)} %get-tuple-element.93.refs_0_), channel_id=1, source_target_pairs={{0,2},{1,3},{2,0},{3,1},{4,6},{5,7},{6,4},{7,5},{8,10},{9,11},{10,... | collective-permute-start | bytes 3145736 | tf_op jit(solution)/shard_map/ppermute | solution.py:502
  6.7 27.8 %collective-permute-start.4 = (bf16[2,128,2048]{2,1,0:T(8,128)(2,1)S(1)}, bf16[2,128,2048]{2,1,0:T(8,128)(2,1)S(1)}, u32[]{:S(2)}, u32[]{:S(2)}) collective-permute-start(bf16[2,128,2048]{2,1,0:T(8,128)(2,1)S(1)} %get-tuple-element.95), channel_id=1, source_target_pairs={{0,1},{1,0},{2,3},{3,2},{4,5},{5,4},{6,7},{7,6},{8,9},{9,8},{10,11... | collective-permute-start | bytes 3145736 | tf_op jit(solution)/shard_map/ppermute | solution.py:502
  6.7 27.8 %collective-permute-start.3 = (bf16[2,128,2048]{2,1,0:T(8,128)(2,1)S(1)}, bf16[2,128,2048]{2,1,0:T(8,128)(2,1)S(1)}, u32[]{:S(2)}, u32[]{:S(2)}) collective-permute-start(bf16[2,128,2048]{2,1,0:T(8,128)(2,1)S(1)} %get-tuple-element.95), channel_id=1, source_target_pairs={{0,5},{1,4},{2,7},{3,6},{4,1},{5,0},{6,3},{7,2},{8,13},{9,12},{10,... | collective-permute-start | bytes 3145736 | tf_op jit(solution)/shard_map/ppermute | solution.py:502
  8.3 43.3 %collective-permute-start.2 = (bf16[2,128,2048]{2,1,0:T(8,128)(2,1)S(1)}, bf16[2,128,2048]{2,1,0:T(8,128)(2,1)S(1)}, u32[]{:S(2)}, u32[]{:S(2)}) collective-permute-start(bf16[2,128,2048]{2,1,0:T(8,128)(2,1)S(1)} %get-tuple-element.95), channel_id=1, source_target_pairs={{0,3},{1,2},{2,1},{3,0},{4,7},{5,6},{6,5},{7,4},{8,11},{9,10},{10,... | collective-permute-start | bytes 3145736 | tf_op jit(solution)/shard_map/ppermute | solution.py:502
  8.4 46.2 %collective-permute-start.1 = (bf16[2,128,2048]{2,1,0:T(8,128)(2,1)S(1)}, bf16[2,128,2048]{2,1,0:T(8,128)(2,1)S(1)}, u32[]{:S(2)}, u32[]{:S(2)}) collective-permute-start(bf16[2,128,2048]{2,1,0:T(8,128)(2,1)S(1)} %get-tuple-element.93.refs_0_), channel_id=1, source_target_pairs={{0,4},{1,5},{2,6},{3,7},{4,0},{5,1},{6,2},{7,3},{8,12},{9,13},{10,... | collective-permute-start | bytes 3145736 | tf_op jit(solution)/shard_map/ppermute | solution.py:502
  54.6 15.7 %collective-permute-start.7 = (bf16[2,256,2048]{2,1,0:T(8,128)(2,1)S(1)}, bf16[2,256,2048]{2,1,0:T(8,128)(2,1)S(1)}, u32[]{:S(2)}, u32[]{:S(2)}) collective-permute-start(bf16[2,256,2048]{2,1,0:T(8,128)(2,1)S(1)} %get-tuple-element.103), channel_id=1, source_target_pairs={{0,1},{1,0},{2,3},{3,2},{4,5},{5,4},{6,7},{7,6},{8,9},{9,8},{10,11... | collective-permute-start | bytes 6291464 | tf_op jit(solution)/shard_map/ppermute | solution.py:502
  54.6 14.3 %collective-permute-start.5 = (bf16[2,128,1024]{2,1,0:T(8,128)(2,1)S(1)}, bf16[2,128,1024]{2,1,0:T(8,128)(2,1)S(1)}, u32[]{:S(2)}, u32[]{:S(2)}) collective-permute-start(bf16[2,128,1024]{2,1,0:T(8,128)(2,1)S(1)} %get-tuple-element.100), channel_id=1, source_target_pairs={{0,4},{1,5},{2,6},{3,7},{4,0},{5,1},{6,2},{7,3},{8,12},{9,13},{10,... | collective-permute-start | bytes 1572872 | tf_op jit(solution)/shard_map/ppermute | solution.py:502
  56.2 14.1 %collective-permute-start.6 = (bf16[2,128,1024]{2,1,0:T(8,128)(2,1)S(1)}, bf16[2,128,1024]{2,1,0:T(8,128)(2,1)S(1)}, u32[]{:S(2)}, u32[]{:S(2)}) collective-permute-start(bf16[2,128,1024]{2,1,0:T(8,128)(2,1)S(1)} %get-tuple-element.185), channel_id=1, source_target_pairs={{0,2},{1,3},{2,0},{3,1},{4,6},{5,7},{6,4},{7,5},{8,10},{9,11},{10,... | collective-permute-start | bytes 1572872 | tf_op jit(solution)/shard_map/ppermute | solution.py:502
  60.4 4.4 %collective-permute-start.9 = (f32[1,128]{1,0:T(1,128)S(1)}, f32[1,128]{1,0:T(1,128)S(1)}, u32[]{:S(2)}, u32[]{:S(2)}) collective-permute-start(f32[1,128]{1,0:T(1,128)S(1)} %add.38), channel_id=1, source_target_pairs={{0,16},{8,24},{16,0},{24,8},{1,17},{9,25},{17,1},{25,9},{2,18},{10... | collective-permute-start | bytes 1544 | tf_op jit(solution)/shard_map/ppermute | solution.py:502
  70.3 13.2 %collective-permute-start.10 = (bf16[2,128,1024]{2,1,0:T(8,128)(2,1)S(1)}, bf16[2,128,1024]{2,1,0:T(8,128)(2,1)S(1)}, u32[]{:S(2)}, u32[]{:S(2)}) collective-permute-start(bf16[2,128,1024]{2,1,0:T(8,128)(2,1)S(1)} %get-tuple-element.105), channel_id=1, source_target_pairs={{0,4},{1,5},{2,6},{3,7},{4,0},{5,1},{6,2},{7,3},{8,12},{9,13},{10,... | collective-permute-start | bytes 1572872 | tf_op jit(solution)/shard_map/ppermute | solution.py:502
  70.8 13.0 %collective-permute-start.11 = (bf16[2,128,1024]{2,1,0:T(8,128)(2,1)S(1)}, bf16[2,128,1024]{2,1,0:T(8,128)(2,1)S(1)}, u32[]{:S(2)}, u32[]{:S(2)}) collective-permute-start(bf16[2,128,1024]{2,1,0:T(8,128)(2,1)S(1)} %get-tuple-element.106), channel_id=1, source_target_pairs={{0,2},{1,3},{2,0},{3,1},{4,6},{5,7},{6,4},{7,5},{8,10},{9,11},{10,... | collective-permute-start | bytes 1572872 | tf_op jit(solution)/shard_map/ppermute | solution.py:502
  83.8 13.4 %collective-permute-start.12 = (bf16[128,1024]{1,0:T(8,128)(2,1)S(1)}, bf16[128,1024]{1,0:T(8,128)(2,1)S(1)}, u32[]{:S(2)}, u32[]{:S(2)}) collective-permute-start(bf16[128,1024]{1,0:T(8,128)(2,1)S(1)} %get-tuple-element.127), channel_id=1, source_target_pairs={{0,2},{1,3},{2,0},{3,1},{4,6},{5,7},{6,4},{7,5},{8,10},{9,11},{10,... | collective-permute-start | bytes 786440 | tf_op jit(solution)/shard_map/ppermute | solution.py:502
  84.3 12.9 %collective-permute-start.13 = (bf16[128,1024]{1,0:T(8,128)(2,1)S(1)}, bf16[128,1024]{1,0:T(8,128)(2,1)S(1)}, u32[]{:S(2)}, u32[]{:S(2)}) collective-permute-start(bf16[128,1024]{1,0:T(8,128)(2,1)S(1)} %get-tuple-element.128), channel_id=1, source_target_pairs={{0,4},{1,5},{2,6},{3,7},{4,0},{5,1},{6,2},{7,3},{8,12},{9,13},{10,... | collective-permute-start | bytes 786440 | tf_op jit(solution)/shard_map/ppermute | solution.py:502
  85.9 11.4 %collective-permute-start.14 = (bf16[128,1024]{1,0:T(8,128)(2,1)S(1)}, bf16[128,1024]{1,0:T(8,128)(2,1)S(1)}, u32[]{:S(2)}, u32[]{:S(2)}) collective-permute-start(bf16[128,1024]{1,0:T(8,128)(2,1)S(1)} %get-tuple-element.129), channel_id=1, source_target_pairs={{0,2},{1,3},{2,0},{3,1},{4,6},{5,7},{6,4},{7,5},{8,10},{9,11},{10,... | collective-permute-start | bytes 786440 | tf_op jit(solution)/shard_map/ppermute | solution.py:502
  87.3 9.9 %collective-permute-start.15 = (bf16[128,1024]{1,0:T(8,128)(2,1)S(1)}, bf16[128,1024]{1,0:T(8,128)(2,1)S(1)}, u32[]{:S(2)}, u32[]{:S(2)}) collective-permute-start(bf16[128,1024]{1,0:T(8,128)(2,1)S(1)} %get-tuple-element.130), channel_id=1, source_target_pairs={{0,5},{1,4},{2,7},{3,6},{4,1},{5,0},{6,3},{7,2},{8,13},{9,12},{10,... | collective-permute-start | bytes 786440 | tf_op jit(solution)/shard_map/ppermute | solution.py:502
  97.3 13.3 %collective-permute-start.16 = (bf16[128,1024]{1,0:T(8,128)(2,1)S(1)}, bf16[128,1024]{1,0:T(8,128)(2,1)S(1)}, u32[]{:S(2)}, u32[]{:S(2)}) collective-permute-start(bf16[128,1024]{1,0:T(8,128)(2,1)S(1)} %add.40), channel_id=1, source_target_pairs={{0,4},{1,5},{2,6},{3,7},{4,0},{5,1},{6,2},{7,3},{8,12},{9,13},{10,... | collective-permute-start | bytes 786440 | tf_op jit(solution)/shard_map/ppermute | solution.py:502
  97.9 12.7 %collective-permute-start.17 = (bf16[128,1024]{1,0:T(8,128)(2,1)S(1)}, bf16[128,1024]{1,0:T(8,128)(2,1)S(1)}, u32[]{:S(2)}, u32[]{:S(2)}) collective-permute-start(bf16[128,1024]{1,0:T(8,128)(2,1)S(1)} %add.41), channel_id=1, source_target_pairs={{0,3},{1,2},{2,1},{3,0},{4,7},{5,6},{6,5},{7,4},{8,11},{9,10},{10,... | collective-permute-start | bytes 786440 | tf_op jit(solution)/shard_map/ppermute | solution.py:502
  99.5 12.7 %collective-permute-start.18 = (bf16[128,1024]{1,0:T(8,128)(2,1)S(1)}, bf16[128,1024]{1,0:T(8,128)(2,1)S(1)}, u32[]{:S(2)}, u32[]{:S(2)}) collective-permute-start(bf16[128,1024]{1,0:T(8,128)(2,1)S(1)} %get-tuple-element.152), channel_id=1, source_target_pairs={{0,2},{1,3},{2,0},{3,1},{4,6},{5,7},{6,4},{7,5},{8,10},{9,11},{10,... | collective-permute-start | bytes 786440 | tf_op jit(solution)/shard_map/ppermute | solution.py:502
  101.0 11.2 %collective-permute-start.19 = (bf16[128,1024]{1,0:T(8,128)(2,1)S(1)}, bf16[128,1024]{1,0:T(8,128)(2,1)S(1)}, u32[]{:S(2)}, u32[]{:S(2)}) collective-permute-start(bf16[128,1024]{1,0:T(8,128)(2,1)S(1)} %get-tuple-element.153), channel_id=1, source_target_pairs={{0,4},{1,5},{2,6},{3,7},{4,0},{5,1},{6,2},{7,3},{8,12},{9,13},{10,... | collective-permute-start | bytes 786440 | tf_op jit(solution)/shard_map/ppermute | solution.py:502
  112.2 16.3 %collective-permute-start.27 = (bf16[640,2048]{1,0:T(8,128)(2,1)S(1)}, bf16[640,2048]{1,0:T(8,128)(2,1)S(1)}, u32[]{:S(2)}, u32[]{:S(2)}) collective-permute-start(bf16[640,2048]{1,0:T(8,128)(2,1)S(1)} %get-tuple-element.169), channel_id=1, source_target_pairs={{0,1},{1,0},{2,3},{3,2},{4,5},{5,4},{6,7},{7,6},{8,9},{9,8},{10,11... | collective-permute-start | bytes 7864328 | tf_op jit(solution)/shard_map/ppermute | solution.py:502
  113.5 9.1 %collective-permute-start.25 = (bf16[128,1024]{1,0:T(8,128)(2,1)S(1)}, bf16[128,1024]{1,0:T(8,128)(2,1)S(1)}, u32[]{:S(2)}, u32[]{:S(2)}) collective-permute-start(bf16[128,1024]{1,0:T(8,128)(2,1)S(1)} %get-tuple-element.167), channel_id=1, source_target_pairs={{0,2},{1,3},{2,0},{3,1},{4,6},{5,7},{6,4},{7,5},{8,10},{9,11},{10,... | collective-permute-start | bytes 786440 | tf_op jit(solution)/shard_map/ppermute | solution.py:502
  114.3 8.5 %collective-permute-start.26 = (bf16[128,1024]{1,0:T(8,128)(2,1)S(1)}, bf16[128,1024]{1,0:T(8,128)(2,1)S(1)}, u32[]{:S(2)}, u32[]{:S(2)}) collective-permute-start(bf16[128,1024]{1,0:T(8,128)(2,1)S(1)} %get-tuple-element.168), channel_id=1, source_target_pairs={{0,5},{1,4},{2,7},{3,6},{4,1},{5,0},{6,3},{7,2},{8,13},{9,12},{10,... | collective-permute-start | bytes 786440 | tf_op jit(solution)/shard_map/ppermute | solution.py:502
  115.4 13.1 %collective-permute-start.23 = (bf16[128,1024]{1,0:T(8,128)(2,1)S(1)}, bf16[128,1024]{1,0:T(8,128)(2,1)S(1)}, u32[]{:S(2)}, u32[]{:S(2)}) collective-permute-start(bf16[128,1024]{1,0:T(8,128)(2,1)S(1)} %add.46), channel_id=1, source_target_pairs={{0,4},{1,5},{2,6},{3,7},{4,0},{5,1},{6,2},{7,3},{8,12},{9,13},{10,... | collective-permute-start | bytes 786440 | tf_op jit(solution)/shard_map/ppermute | solution.py:502
  116.1 12.4 %collective-permute-start.24 = (bf16[128,1024]{1,0:T(8,128)(2,1)S(1)}, bf16[128,1024]{1,0:T(8,128)(2,1)S(1)}, u32[]{:S(2)}, u32[]{:S(2)}) collective-permute-start(bf16[128,1024]{1,0:T(8,128)(2,1)S(1)} %add.47), channel_id=1, source_target_pairs={{0,3},{1,2},{2,1},{3,0},{4,7},{5,6},{6,5},{7,4},{8,11},{9,10},{10,... | collective-permute-start | bytes 786440 | tf_op jit(solution)/shard_map/ppermute | solution.py:502
  (16 other events, 219.9 us)

commit v6 on v5

--- a/solution.py
+++ b/solution.py
@@ -148,7 +148,7 @@
             pltpu.VMEM((4, rows, half), queries.dtype),
             pltpu.SemaphoreType.DMA((8,)),
         ],
-        compiler_params=ROOM,
+        compiler_params=ALONE,
         cost_estimate=SMALL,
         name="split_columns",
     )(me, queries, cotangent)
@@ -629,14 +629,14 @@
 
         last_a, relay_b = merged(parts_a, relay_a), forwarded(parts_b)
         loss = doubled_sum(loss_a + loss_b, "dp", groups)
-        loss = doubled_sum(loss, "pack", packs, 1, 2)
+        loss = doubled_sum(loss, "pack", packs, 2, 4)
         last_a, relay_b, loss, full = together((last_a, relay_b, loss, full))
 
         last_b, direct_b = merged(parts_b, relay_b), sent(parts_b)
         back = swapped(full[2], 1)
-        loss = doubled_sum(loss, "pack", packs, 2, 4)
+        loss = doubled_sum(loss, "pack", packs, 4)
         last_b, direct_b, back, loss = together((last_b, direct_b, back, loss))
-        loss = doubled_sum(loss, "pack", packs, 4)
+        loss = doubled_sum(loss, "pack", packs, 1, 2)
         ends = [sums(parts_a, direct_a, last_a), sums(parts_b, direct_b, last_b)]
 
     queries_gradient, keys_gradient, values_gradient = finish(

time: 133 us -> 132 us (level)
  local copies, waits for them, and re-layouts: 4.88 us -> 2.29 us
  Pallas kernels: 23.7 us -> 25.8 us
    unnamed x20 -> x18, local copies, waits for them, and re-layouts: 4.21 us -> 1.62 us
    pallas_call x1, Pallas kernels: 0.38 us -> 2.56 us  [split(): pl.pallas_call(split_kernel, out_shape=[jax.ShapeDtypeStruct((2, rows, ha...]
  transfers between devices with their start and end apart: 30 -> 30, of which waited for: 17 -> 14; matrix products, arithmetic and copies ran while one was open for 1% -> 1% of each run, Pallas kernels for 18% -> 18%
where the time goes in v6:
time: 132 us
  waiting for transfers between devices  71 us (54%)
  starting transfers between devices  30.1 us (23%)
  Pallas kernels  25.8 us (20%)
  local copies, waits for them, and re-layouts  2.29 us (2%)
  other arithmetic  1.55 us (1%)
    ppermute x30, waiting for transfers between devices, swap(): return lax.ppermute(array, axis_name, [(i, i ^ bits) for i in range(size)])  71 us
    ppermute x30, starting transfers between devices, swap(): return lax.ppermute(array, axis_name, [(i, i ^ bits) for i in range(size)])  30.1 us
    pallas_call x2, Pallas kernels, attention_chunk(): pl.pallas_call(functools.partial(attention_kernel, packs=packs, first=fir...  19.5 us
  transfers between devices with their start and end apart: 30, of which 14 were waited for; matrix products, arithmetic and copies ran while one was open for 1% of the time, Pallas kernels for 18%

profile of v6, /device:TPU:0, one launch (start us, length us, event | category | flops | bytes accessed | tf_op | source)
XLA Modules:
  0.0 131.6 jit_solution(3073133791188515307)
XLA Ops:
  0.7 2.6 %split_columns.1 = (bf16[2,128,2048]{2,1,0:T(8,128)(2,1)}, bf16[2,128,2048]{2,1,0:T(8,128)(2,1)}) custom-call(s32[1]{0:T(128)} %bitcast.me_ref, bf16[128,4096]{1,0:T(8,128)(2,1)} %q_ref.1, bf16[128,4096]{1,0:T(8,128)(2,1)} %c_ref.1), custom_call_target="tpu_custom_call" | custom-call | bytes 2097152 | tf_op jit(solution)/shard_map/split_columns/pallas_call | solution.py:142
  3.3 3.0 %collective-permute-start = (bf16[2,128,2048]{2,1,0:T(8,128)(2,1)}, bf16[2,128,2048]{2,1,0:T(8,128)(2,1)S(1)}, u32[]{:S(2)}, u32[]{:S(2)}) collective-permute-start(bf16[2,128,2048]{2,1,0:T(8,128)(2,1)} %get-tuple-element.93.refs_0_), channel_id=1, source_target_pairs={{0,2},{1,3},{2,0},{3,1},{4,6},{5,7},{6,4},{7,5},{8,10},{9,11},{10,... | collective-permute-start | bytes 3145736 | tf_op jit(solution)/shard_map/ppermute | solution.py:502
  6.3 1.6 %collective-permute-start.3 = (bf16[2,128,2048]{2,1,0:T(8,128)(2,1)}, bf16[2,128,2048]{2,1,0:T(8,128)(2,1)S(1)}, u32[]{:S(2)}, u32[]{:S(2)}) collective-permute-start(bf16[2,128,2048]{2,1,0:T(8,128)(2,1)} %get-tuple-element.95), channel_id=1, source_target_pairs={{0,5},{1,4},{2,7},{3,6},{4,1},{5,0},{6,3},{7,2},{8,13},{9,12},{10,... | collective-permute-start | bytes 3145736 | tf_op jit(solution)/shard_map/ppermute | solution.py:502
  8.4 22.0 %collective-permute-done.refs_2_ = bf16[2,128,2048]{2,1,0:T(8,128)(2,1)S(1)} collective-permute-done((bf16[2,128,2048]{2,1,0:T(8,128)(2,1)}, bf16[2,128,2048]{2,1,0:T(8,128)(2,1)S(1)}, u32[]{:S(2)}, u32[]{:S(2)}) %collective-permute-start) | collective-permute-done | bytes 1048608 | tf_op jit(solution)/shard_map/ppermute | solution.py:502
  30.5 1.6 %copy-done.1 = bf16[256,4096]{1,0:T(8,128)(2,1)S(1)} copy-done((bf16[256,4096]{1,0:T(8,128)(2,1)S(1)}, bf16[256,4096]{1,0:T(8,128)(2,1)}, u32[]{:S(2)}) %copy-start.1) | copy-done | bytes 2097176
  32.1 2.0 %tabulate.1 = (bf16[2,256,2048]{2,1,0:T(8,128)(2,1)S(1)}, s32[4,8]{1,0:T(4,128)S(1)}, f32[1,128]{1,0:T(1,128)S(1)}) custom-call(s32[1]{0:T(128)} %bitcast.me_ref, s32[1,16]{1,0:T(1,128)S(1)} %copy-done.3, s32[1,16]{1,0:T(1,128)S(1)} %copy-done.4, s32[1,16]{1,0:T(1,128)S(1)} %copy-done.5, s32[1,16]{1,0:T(1,128)S(1)} %copy-done.6, s32[1,16]{1,0:T(1,128)S(1)} %bitcast.6, ...), custom_call_target="tpu_custom_call" | custom-call | bytes 2097152 | tf_op jit(solution)/shard_map/tabulate/pallas_call | solution.py:100
  34.3 17.2 %collective-permute-done.2.refs_3_ = bf16[2,128,2048]{2,1,0:T(8,128)(2,1)S(1)} collective-permute-done((bf16[2,128,2048]{2,1,0:T(8,128)(2,1)}, bf16[2,128,2048]{2,1,0:T(8,128)(2,1)S(1)}, u32[]{:S(2)}, u32[]{:S(2)}) %collective-permute-start.2) | collective-permute-done | bytes 1048608 | tf_op jit(solution)/shard_map/ppermute | solution.py:502
  51.5 2.9 %collective-permute-done.1.refs_4_ = bf16[2,128,2048]{2,1,0:T(8,128)(2,1)S(1)} collective-permute-done((bf16[2,128,2048]{2,1,0:T(8,128)(2,1)}, bf16[2,128,2048]{2,1,0:T(8,128)(2,1)S(1)}, u32[]{:S(2)}, u32[]{:S(2)}) %collective-permute-start.1) | collective-permute-done | bytes 1048608 | tf_op jit(solution)/shard_map/ppermute | solution.py:502
  56.6 1.6 %collective-permute-start.8 = (f32[1,128]{1,0:T(1,128)S(1)}, f32[1,128]{1,0:T(1,128)S(1)}, u32[]{:S(2)}, u32[]{:S(2)}) collective-permute-start(f32[1,128]{1,0:T(1,128)S(1)} %get-tuple-element.104), channel_id=1, source_target_pairs={{0,8},{8,0},{16,24},{24,16},{1,9},{9,1},{17,25},{25,17},{2,10},{10... | collective-permute-start | bytes 1544 | tf_op jit(solution)/shard_map/ppermute | solution.py:502
  58.2 2.0 %collective-permute-done.8 = f32[1,128]{1,0:T(1,128)S(1)} collective-permute-done((f32[1,128]{1,0:T(1,128)S(1)}, f32[1,128]{1,0:T(1,128)S(1)}, u32[]{:S(2)}, u32[]{:S(2)}) %collective-permute-start.8) | collective-permute-done | bytes 544 | tf_op jit(solution)/shard_map/ppermute | solution.py:502
  60.2 2.6 %collective-permute-start.9 = (f32[1,128]{1,0:T(1,128)S(1)}, f32[1,128]{1,0:T(1,128)S(1)}, u32[]{:S(2)}, u32[]{:S(2)}) collective-permute-start(f32[1,128]{1,0:T(1,128)S(1)} %add.38), channel_id=1, source_target_pairs={{0,16},{8,24},{16,0},{24,8},{1,17},{9,25},{17,1},{25,9},{2,18},{10... | collective-permute-start | bytes 1544 | tf_op jit(solution)/shard_map/ppermute | solution.py:502
  65.3 3.5 %collective-permute-done.5.refs_6_ = bf16[2,128,1024]{2,1,0:T(8,128)(2,1)S(1)} collective-permute-done((bf16[2,128,1024]{2,1,0:T(8,128)(2,1)S(1)}, bf16[2,128,1024]{2,1,0:T(8,128)(2,1)S(1)}, u32[]{:S(2)}, u32[]{:S(2)}) %collective-permute-start.5) | collective-permute-done | bytes 524320 | tf_op jit(solution)/shard_map/ppermute | solution.py:502
  71.1 9.7 %attention_chunk.2 = (bf16[256,4096]{1,0:T(8,128)(2,1)}, bf16[256,4096]{1,0:T(8,128)(2,1)}, bf16[640,2048]{1,0:T(8,128)(2,1)S(1)}, bf16[128,1024]{1,0:T(8,128)(2...) custom-call(s32[1]{0:T(128)} %bitcast.me_ref, ...), custom_call_target="tpu_custom_call" | custom-call | flops 33554432 | bytes 8388608 | tf_op jit(solution)/shard_map/attention_chunk/pallas_call | solution.py:410
  80.7 2.6 %collective-permute-done.10.refs_6_ = bf16[2,128,1024]{2,1,0:T(8,128)(2,1)S(1)} collective-permute-done((bf16[2,128,1024]{2,1,0:T(8,128)(2,1)S(1)}, bf16[2,128,1024]{2,1,0:T(8,128)(2,1)S(1)}, u32[]{:S(2)}, u32[]{:S(2)}) %collective-permute-start.10) | collective-permute-done | bytes 524320 | tf_op jit(solution)/shard_map/ppermute | solution.py:502
  87.2 9.8 %attention_chunk.3 = (bf16[256,4096]{1,0:T(8,128)(2,1)}, bf16[256,4096]{1,0:T(8,128)(2,1)}, bf16[640,2048]{1,0:T(8,128)(2,1)S(1)}, bf16[128,1024]{1,0:T(8,128)(2...) custom-call(s32[1]{0:T(128)} %bitcast.me_ref, ...), custom_call_target="tpu_custom_call", output_to_operand_aliasing={{0}: (14, {}), {1}: (15, {}), {2}: (16, {})} | custom-call | flops 33554432 | bytes 8388608 | tf_op jit(solution)/shard_map/attention_chunk/pallas_call | solution.py:410
  101.3 1.6 %collective-permute-start.20 = (f32[1,128]{1,0:T(1,128)S(1)}, f32[1,128]{1,0:T(1,128)S(1)}, u32[]{:S(2)}, u32[]{:S(2)}) collective-permute-start(f32[1,128]{1,0:T(1,128)S(1)} %add.42), channel_id=1, source_target_pairs={{0,8},{8,0},{16,24},{24,16},{1,9},{9,1},{17,25},{25,17},{2,10},{10... | collective-permute-start | bytes 1544 | tf_op jit(solution)/shard_map/ppermute | solution.py:502
  102.9 2.0 %collective-permute-done.20 = f32[1,128]{1,0:T(1,128)S(1)} collective-permute-done((f32[1,128]{1,0:T(1,128)S(1)}, f32[1,128]{1,0:T(1,128)S(1)}, u32[]{:S(2)}, u32[]{:S(2)}) %collective-permute-start.20) | collective-permute-done | bytes 544 | tf_op jit(solution)/shard_map/ppermute | solution.py:502
  104.9 2.6 %collective-permute-start.21 = (f32[1,128]{1,0:T(1,128)S(1)}, f32[1,128]{1,0:T(1,128)S(1)}, u32[]{:S(2)}, u32[]{:S(2)}) collective-permute-start(f32[1,128]{1,0:T(1,128)S(1)} %add.43), channel_id=1, source_target_pairs={{0,16},{8,24},{16,0},{24,8},{1,17},{9,25},{17,1},{25,9},{2,18},{10... | collective-permute-start | bytes 1544 | tf_op jit(solution)/shard_map/ppermute | solution.py:502
  107.5 1.8 %collective-permute-done.21 = f32[1,128]{1,0:T(1,128)S(1)} collective-permute-done((f32[1,128]{1,0:T(1,128)S(1)}, f32[1,128]{1,0:T(1,128)S(1)}, u32[]{:S(2)}, u32[]{:S(2)}) %collective-permute-start.21) | collective-permute-done | bytes 544 | tf_op jit(solution)/shard_map/ppermute | solution.py:502
  109.8 3.0 %collective-permute-done.22 = f32[1,128]{1,0:T(1,128)S(1)} collective-permute-done((f32[1,128]{1,0:T(1,128)S(1)}, f32[1,128]{1,0:T(1,128)S(1)}, u32[]{:S(2)}, u32[]{:S(2)}) %collective-permute-start.22) | collective-permute-done | bytes 544 | tf_op jit(solution)/shard_map/ppermute | solution.py:502
  113.0 1.6 %collective-permute-start.28 = (f32[1,128]{1,0:T(1,128)S(1)}, f32[1,128]{1,0:T(1,128)S(1)}, u32[]{:S(2)}, u32[]{:S(2)}) collective-permute-start(f32[1,128]{1,0:T(1,128)S(1)} %add.45), channel_id=1, source_target_pairs={{0,4},{1,5},{2,6},{3,7},{4,0},{5,1},{6,2},{7,3},{8,12},{9,13},{10,... | collective-permute-start | bytes 1544 | tf_op jit(solution)/shard_map/ppermute | solution.py:502
  118.3 5.4 %collective-permute-done.25.refs_6_ = bf16[128,1024]{1,0:T(8,128)(2,1)S(1)} collective-permute-done((bf16[128,1024]{1,0:T(8,128)(2,1)S(1)}, bf16[128,1024]{1,0:T(8,128)(2,1)S(1)}, u32[]{:S(2)}, u32[]{:S(2)}) %collective-permute-start.25) | collective-permute-done | bytes 262176 | tf_op jit(solution)/shard_map/ppermute | solution.py:502
  123.7 5.6 %collective-permute-done.23.refs_7_ = bf16[128,1024]{1,0:T(8,128)(2,1)S(1)} collective-permute-done((bf16[128,1024]{1,0:T(8,128)(2,1)S(1)}, bf16[128,1024]{1,0:T(8,128)(2,1)S(1)}, u32[]{:S(2)}, u32[]{:S(2)}) %collective-permute-start.23) | collective-permute-done | bytes 262176 | tf_op jit(solution)/shard_map/ppermute | solution.py:502
  129.4 1.7 %finish.1 = (bf16[128,4096]{1,0:T(8,128)(2,1)}, bf16[256,4096]{1,0:T(8,128)(2,1)}, bf16[256,4096]{1,0:T(8,128)(2,1)}) custom-call(s32[1]{0:T(128)} %bitcast.me_ref, bf16[128,1024]{1,0:T(8,128)(2,1)S(1)} %get-tuple-element.126.refs_0_, bf16[128,1024]{1,0:T(8,128)(2,1)S(1)} %collective-permute-done.14.refs_1_, ...), custom_call_target="tpu_custom_call", output_to_operand_aliasing={{1}: (12, {}), {2}: (13, {})} | custom-call | bytes 2097152 | tf_op jit(solution)/shard_map/finish/pallas_call | solution.py:483
  (76 shorter events, 20.7 us)
Async XLA Ops:
  3.3 27.2 %collective-permute-start = (bf16[2,128,2048]{2,1,0:T(8,128)(2,1)}, bf16[2,128,2048]{2,1,0:T(8,128)(2,1)S(1)}, u32[]{:S(2)}, u32[]{:S(2)}) collective-permute-start(bf16[2,128,2048]{2,1,0:T(8,128)(2,1)} %get-tuple-element.93.refs_0_), channel_id=1, source_target_pairs={{0,2},{1,3},{2,0},{3,1},{4,6},{5,7},{6,4},{7,5},{8,10},{9,11},{10,... | collective-permute-start | bytes 3145736 | tf_op jit(solution)/shard_map/ppermute | solution.py:502
  6.3 28.0 %collective-permute-start.4 = (bf16[2,128,2048]{2,1,0:T(8,128)(2,1)}, bf16[2,128,2048]{2,1,0:T(8,128)(2,1)S(1)}, u32[]{:S(2)}, u32[]{:S(2)}) collective-permute-start(bf16[2,128,2048]{2,1,0:T(8,128)(2,1)} %get-tuple-element.95), channel_id=1, source_target_pairs={{0,1},{1,0},{2,3},{3,2},{4,5},{5,4},{6,7},{7,6},{8,9},{9,8},{10,11... | collective-permute-start | bytes 3145736 | tf_op jit(solution)/shard_map/ppermute | solution.py:502
  6.3 28.0 %collective-permute-start.3 = (bf16[2,128,2048]{2,1,0:T(8,128)(2,1)}, bf16[2,128,2048]{2,1,0:T(8,128)(2,1)S(1)}, u32[]{:S(2)}, u32[]{:S(2)}) collective-permute-start(bf16[2,128,2048]{2,1,0:T(8,128)(2,1)} %get-tuple-element.95), channel_id=1, source_target_pairs={{0,5},{1,4},{2,7},{3,6},{4,1},{5,0},{6,3},{7,2},{8,13},{9,12},{10,... | collective-permute-start | bytes 3145736 | tf_op jit(solution)/shard_map/ppermute | solution.py:502
  7.9 43.6 %collective-permute-start.2 = (bf16[2,128,2048]{2,1,0:T(8,128)(2,1)}, bf16[2,128,2048]{2,1,0:T(8,128)(2,1)S(1)}, u32[]{:S(2)}, u32[]{:S(2)}) collective-permute-start(bf16[2,128,2048]{2,1,0:T(8,128)(2,1)} %get-tuple-element.95), channel_id=1, source_target_pairs={{0,3},{1,2},{2,1},{3,0},{4,7},{5,6},{6,5},{7,4},{8,11},{9,10},{10,... | collective-permute-start | bytes 3145736 | tf_op jit(solution)/shard_map/ppermute | solution.py:502
  8.1 46.4 %collective-permute-start.1 = (bf16[2,128,2048]{2,1,0:T(8,128)(2,1)}, bf16[2,128,2048]{2,1,0:T(8,128)(2,1)S(1)}, u32[]{:S(2)}, u32[]{:S(2)}) collective-permute-start(bf16[2,128,2048]{2,1,0:T(8,128)(2,1)} %get-tuple-element.93.refs_0_), channel_id=1, source_target_pairs={{0,4},{1,5},{2,6},{3,7},{4,0},{5,1},{6,2},{7,3},{8,12},{9,13},{10,... | collective-permute-start | bytes 3145736 | tf_op jit(solution)/shard_map/ppermute | solution.py:502
  54.4 15.7 %collective-permute-start.7 = (bf16[2,256,2048]{2,1,0:T(8,128)(2,1)S(1)}, bf16[2,256,2048]{2,1,0:T(8,128)(2,1)S(1)}, u32[]{:S(2)}, u32[]{:S(2)}) collective-permute-start(bf16[2,256,2048]{2,1,0:T(8,128)(2,1)S(1)} %get-tuple-element.103), channel_id=1, source_target_pairs={{0,1},{1,0},{2,3},{3,2},{4,5},{5,4},{6,7},{7,6},{8,9},{9,8},{10,11... | collective-permute-start | bytes 6291464 | tf_op jit(solution)/shard_map/ppermute | solution.py:502
  54.4 14.3 %collective-permute-start.5 = (bf16[2,128,1024]{2,1,0:T(8,128)(2,1)S(1)}, bf16[2,128,1024]{2,1,0:T(8,128)(2,1)S(1)}, u32[]{:S(2)}, u32[]{:S(2)}) collective-permute-start(bf16[2,128,1024]{2,1,0:T(8,128)(2,1)S(1)} %get-tuple-element.100), channel_id=1, source_target_pairs={{0,4},{1,5},{2,6},{3,7},{4,0},{5,1},{6,2},{7,3},{8,12},{9,13},{10,... | collective-permute-start | bytes 1572872 | tf_op jit(solution)/shard_map/ppermute | solution.py:502
  56.0 14.1 %collective-permute-start.6 = (bf16[2,128,1024]{2,1,0:T(8,128)(2,1)S(1)}, bf16[2,128,1024]{2,1,0:T(8,128)(2,1)S(1)}, u32[]{:S(2)}, u32[]{:S(2)}) collective-permute-start(bf16[2,128,1024]{2,1,0:T(8,128)(2,1)S(1)} %get-tuple-element.185), channel_id=1, source_target_pairs={{0,2},{1,3},{2,0},{3,1},{4,6},{5,7},{6,4},{7,5},{8,10},{9,11},{10,... | collective-permute-start | bytes 1572872 | tf_op jit(solution)/shard_map/ppermute | solution.py:502
  60.2 4.4 %collective-permute-start.9 = (f32[1,128]{1,0:T(1,128)S(1)}, f32[1,128]{1,0:T(1,128)S(1)}, u32[]{:S(2)}, u32[]{:S(2)}) collective-permute-start(f32[1,128]{1,0:T(1,128)S(1)} %add.38), channel_id=1, source_target_pairs={{0,16},{8,24},{16,0},{24,8},{1,17},{9,25},{17,1},{25,9},{2,18},{10... | collective-permute-start | bytes 1544 | tf_op jit(solution)/shard_map/ppermute | solution.py:502
  70.1 13.2 %collective-permute-start.10 = (bf16[2,128,1024]{2,1,0:T(8,128)(2,1)S(1)}, bf16[2,128,1024]{2,1,0:T(8,128)(2,1)S(1)}, u32[]{:S(2)}, u32[]{:S(2)}) collective-permute-start(bf16[2,128,1024]{2,1,0:T(8,128)(2,1)S(1)} %get-tuple-element.105), channel_id=1, source_target_pairs={{0,4},{1,5},{2,6},{3,7},{4,0},{5,1},{6,2},{7,3},{8,12},{9,13},{10,... | collective-permute-start | bytes 1572872 | tf_op jit(solution)/shard_map/ppermute | solution.py:502
  70.6 13.0 %collective-permute-start.11 = (bf16[2,128,1024]{2,1,0:T(8,128)(2,1)S(1)}, bf16[2,128,1024]{2,1,0:T(8,128)(2,1)S(1)}, u32[]{:S(2)}, u32[]{:S(2)}) collective-permute-start(bf16[2,128,1024]{2,1,0:T(8,128)(2,1)S(1)} %get-tuple-element.106), channel_id=1, source_target_pairs={{0,2},{1,3},{2,0},{3,1},{4,6},{5,7},{6,4},{7,5},{8,10},{9,11},{10,... | collective-permute-start | bytes 1572872 | tf_op jit(solution)/shard_map/ppermute | solution.py:502
  83.6 13.4 %collective-permute-start.12 = (bf16[128,1024]{1,0:T(8,128)(2,1)S(1)}, bf16[128,1024]{1,0:T(8,128)(2,1)S(1)}, u32[]{:S(2)}, u32[]{:S(2)}) collective-permute-start(bf16[128,1024]{1,0:T(8,128)(2,1)S(1)} %get-tuple-element.127), channel_id=1, source_target_pairs={{0,2},{1,3},{2,0},{3,1},{4,6},{5,7},{6,4},{7,5},{8,10},{9,11},{10,... | collective-permute-start | bytes 786440 | tf_op jit(solution)/shard_map/ppermute | solution.py:502
  84.1 12.9 %collective-permute-start.13 = (bf16[128,1024]{1,0:T(8,128)(2,1)S(1)}, bf16[128,1024]{1,0:T(8,128)(2,1)S(1)}, u32[]{:S(2)}, u32[]{:S(2)}) collective-permute-start(bf16[128,1024]{1,0:T(8,128)(2,1)S(1)} %get-tuple-element.128), channel_id=1, source_target_pairs={{0,4},{1,5},{2,6},{3,7},{4,0},{5,1},{6,2},{7,3},{8,12},{9,13},{10,... | collective-permute-start | bytes 786440 | tf_op jit(solution)/shard_map/ppermute | solution.py:502
  85.7 11.4 %collective-permute-start.14 = (bf16[128,1024]{1,0:T(8,128)(2,1)S(1)}, bf16[128,1024]{1,0:T(8,128)(2,1)S(1)}, u32[]{:S(2)}, u32[]{:S(2)}) collective-permute-start(bf16[128,1024]{1,0:T(8,128)(2,1)S(1)} %get-tuple-element.129), channel_id=1, source_target_pairs={{0,2},{1,3},{2,0},{3,1},{4,6},{5,7},{6,4},{7,5},{8,10},{9,11},{10,... | collective-permute-start | bytes 786440 | tf_op jit(solution)/shard_map/ppermute | solution.py:502
  87.1 9.9 %collective-permute-start.15 = (bf16[128,1024]{1,0:T(8,128)(2,1)S(1)}, bf16[128,1024]{1,0:T(8,128)(2,1)S(1)}, u32[]{:S(2)}, u32[]{:S(2)}) collective-permute-start(bf16[128,1024]{1,0:T(8,128)(2,1)S(1)} %get-tuple-element.130), channel_id=1, source_target_pairs={{0,5},{1,4},{2,7},{3,6},{4,1},{5,0},{6,3},{7,2},{8,13},{9,12},{10,... | collective-permute-start | bytes 786440 | tf_op jit(solution)/shard_map/ppermute | solution.py:502
  97.1 15.7 %collective-permute-start.16 = (bf16[128,1024]{1,0:T(8,128)(2,1)S(1)}, bf16[128,1024]{1,0:T(8,128)(2,1)S(1)}, u32[]{:S(2)}, u32[]{:S(2)}) collective-permute-start(bf16[128,1024]{1,0:T(8,128)(2,1)S(1)} %add.40), channel_id=1, source_target_pairs={{0,4},{1,5},{2,6},{3,7},{4,0},{5,1},{6,2},{7,3},{8,12},{9,13},{10,... | collective-permute-start | bytes 786440 | tf_op jit(solution)/shard_map/ppermute | solution.py:502
  97.8 15.1 %collective-permute-start.17 = (bf16[128,1024]{1,0:T(8,128)(2,1)S(1)}, bf16[128,1024]{1,0:T(8,128)(2,1)S(1)}, u32[]{:S(2)}, u32[]{:S(2)}) collective-permute-start(bf16[128,1024]{1,0:T(8,128)(2,1)S(1)} %add.41), channel_id=1, source_target_pairs={{0,3},{1,2},{2,1},{3,0},{4,7},{5,6},{6,5},{7,4},{8,11},{9,10},{10,... | collective-permute-start | bytes 786440 | tf_op jit(solution)/shard_map/ppermute | solution.py:502
  99.3 13.6 %collective-permute-start.18 = (bf16[128,1024]{1,0:T(8,128)(2,1)S(1)}, bf16[128,1024]{1,0:T(8,128)(2,1)S(1)}, u32[]{:S(2)}, u32[]{:S(2)}) collective-permute-start(bf16[128,1024]{1,0:T(8,128)(2,1)S(1)} %get-tuple-element.152), channel_id=1, source_target_pairs={{0,2},{1,3},{2,0},{3,1},{4,6},{5,7},{6,4},{7,5},{8,10},{9,11},{10,... | collective-permute-start | bytes 786440 | tf_op jit(solution)/shard_map/ppermute | solution.py:502
  100.8 12.1 %collective-permute-start.19 = (bf16[128,1024]{1,0:T(8,128)(2,1)S(1)}, bf16[128,1024]{1,0:T(8,128)(2,1)S(1)}, u32[]{:S(2)}, u32[]{:S(2)}) collective-permute-start(bf16[128,1024]{1,0:T(8,128)(2,1)S(1)} %get-tuple-element.153), channel_id=1, source_target_pairs={{0,4},{1,5},{2,6},{3,7},{4,0},{5,1},{6,2},{7,3},{8,12},{9,13},{10,... | collective-permute-start | bytes 786440 | tf_op jit(solution)/shard_map/ppermute | solution.py:502
  112.9 16.4 %collective-permute-start.27 = (bf16[640,2048]{1,0:T(8,128)(2,1)S(1)}, bf16[640,2048]{1,0:T(8,128)(2,1)S(1)}, u32[]{:S(2)}, u32[]{:S(2)}) collective-permute-start(bf16[640,2048]{1,0:T(8,128)(2,1)S(1)} %get-tuple-element.169), channel_id=1, source_target_pairs={{0,1},{1,0},{2,3},{3,2},{4,5},{5,4},{6,7},{7,6},{8,9},{9,8},{10,11... | collective-permute-start | bytes 7864328 | tf_op jit(solution)/shard_map/ppermute | solution.py:502
  114.5 9.2 %collective-permute-start.25 = (bf16[128,1024]{1,0:T(8,128)(2,1)S(1)}, bf16[128,1024]{1,0:T(8,128)(2,1)S(1)}, u32[]{:S(2)}, u32[]{:S(2)}) collective-permute-start(bf16[128,1024]{1,0:T(8,128)(2,1)S(1)} %get-tuple-element.167), channel_id=1, source_target_pairs={{0,2},{1,3},{2,0},{3,1},{4,6},{5,7},{6,4},{7,5},{8,10},{9,11},{10,... | collective-permute-start | bytes 786440 | tf_op jit(solution)/shard_map/ppermute | solution.py:502
  115.1 8.6 %collective-permute-start.26 = (bf16[128,1024]{1,0:T(8,128)(2,1)S(1)}, bf16[128,1024]{1,0:T(8,128)(2,1)S(1)}, u32[]{:S(2)}, u32[]{:S(2)}) collective-permute-start(bf16[128,1024]{1,0:T(8,128)(2,1)S(1)} %get-tuple-element.168), channel_id=1, source_target_pairs={{0,5},{1,4},{2,7},{3,6},{4,1},{5,0},{6,3},{7,2},{8,13},{9,12},{10,... | collective-permute-start | bytes 786440 | tf_op jit(solution)/shard_map/ppermute | solution.py:502
  115.2 14.1 %collective-permute-start.23 = (bf16[128,1024]{1,0:T(8,128)(2,1)S(1)}, bf16[128,1024]{1,0:T(8,128)(2,1)S(1)}, u32[]{:S(2)}, u32[]{:S(2)}) collective-permute-start(bf16[128,1024]{1,0:T(8,128)(2,1)S(1)} %add.46), channel_id=1, source_target_pairs={{0,4},{1,5},{2,6},{3,7},{4,0},{5,1},{6,2},{7,3},{8,12},{9,13},{10,... | collective-permute-start | bytes 786440 | tf_op jit(solution)/shard_map/ppermute | solution.py:502
  116.8 12.5 %collective-permute-start.24 = (bf16[128,1024]{1,0:T(8,128)(2,1)S(1)}, bf16[128,1024]{1,0:T(8,128)(2,1)S(1)}, u32[]{:S(2)}, u32[]{:S(2)}) collective-permute-start(bf16[128,1024]{1,0:T(8,128)(2,1)S(1)} %add.47), channel_id=1, source_target_pairs={{0,3},{1,2},{2,1},{3,0},{4,7},{5,6},{6,5},{7,4},{8,11},{9,10},{10,... | collective-permute-start | bytes 786440 | tf_op jit(solution)/shard_map/ppermute | solution.py:502
  (15 other events, 266.8 us)
